TPU v7x, 512 devices: a whole 4x8x8 slice. The times are simulated.
512 devices in a mesh: seq: 32 (over x, y), head: 16 (over z, core).
Axes of the slice: x: 4, y: 8, z: 8, core: 2. Of those that a mesh axis runs over, the one named last changes fastest.
Arguments:
- qkv_raw: bfloat16 [16384, 3, 4096], P('seq', None, 'head'), may hold values from -6 to 6
- conv_weight: float32 [3, 4, 4096], P(None, None, 'head'), may hold values from -3 to 3
- norm_gain: float32 [4096], P('head'), may hold values from 0.1 to 1.9
- doc_starts: int32 [4], replicated, may hold values from 0 to 15744, as said below
- cotangent: bfloat16 [16384, 4096], P('seq', 'head'), may hold values from -6 to 6
Outputs:
- attn_out: bfloat16 [16384, 4096], P(('seq', 'head'))
- grad_input: bfloat16 [16384, 3, 4096], P(('seq', 'head'))
Inputs may be any that keep to these rules, and one draw needn't show every extreme that they name: `doc_starts`: the first entry is 0 and the last is 15744; the entries rise strictly and each is a multiple of 128.
All inputs are finite; a program needn't handle non-finite values.
Results may differ from a plain program's by a relative error of at most 0.0062.
Values may be sent and summed in bfloat16 or wider, within the bound.
No kernel may reach another device: no remote copies, remote signals or barrier semaphores. Data moves between devices by JAX's collectives and lax.ppermute only.
A program may use at most 64 MiB of HBM per device.

v0:
```python
import jax
import jax.numpy as jnp
from jax import lax
from jax.sharding import PartitionSpec as P

HEAD_DIM = 128
TAPS = 4


highest = lax.Precision.HIGHEST


def from_behind(block, axis, distance):
    devices = range(lax.axis_size(axis))
    route = [(i - distance, i) for i in devices if i - distance in devices]
    return lax.ppermute(block, axis, route)


def prefix(part, axis, combine, identity, reverse):
    count = lax.axis_size(axis)
    place = lax.axis_index(axis)
    ahead = count - 1 - place if reverse else place
    gathered = jax.tree.map(lambda a: lax.all_gather(a, axis), part)
    state = jax.tree.map(lambda a, e: jnp.zeros_like(a) + jnp.asarray(e, a.dtype), part, identity)

    def one(step, state):
        source = count - 1 - step if reverse else step
        return combine(
            state, jax.tree.map(lambda a: lax.dynamic_index_in_dim(a, source, 0, False), gathered)
        )

    return lax.fori_loop(0, ahead, one, state)


def segment_ids(doc_starts, positions):
    return jnp.sum((doc_starts[None, :] <= positions[:, None]).astype(jnp.int32), axis=1) - 1


def silu_slope(inputs):
    sigma = jax.nn.sigmoid(inputs)
    return sigma * (1.0 + inputs * (1.0 - sigma))


def combine_states(earlier, later):
    return (later[0] + (1.0 - later[1]) * earlier[0], jnp.maximum(earlier[1], later[1]))


def shards(qkv_raw, conv_weight, norm_gain, doc_starts, cotangent):
    row_count = qkv_raw.shape[0]
    width_local = qkv_raw.shape[2]
    heads_local = width_local // HEAD_DIM
    rim_rows = TAPS - 1
    seq_index = lax.axis_index("seq")
    first_row = seq_index * row_count
    extended_pos = first_row - rim_rows + jnp.arange(row_count + 2 * rim_rows, dtype=jnp.int32)
    seg_all = segment_ids(doc_starts, extended_pos)
    segments = seg_all[rim_rows : rim_rows + row_count]
    prev_seg = seg_all[rim_rows - 1]
    next_seg = seg_all[rim_rows + row_count]
    start_flag = jnp.any((doc_starts >= first_row) & (doc_starts < first_row + row_count)).astype(
        jnp.float32
    )
    rim_before = from_behind(qkv_raw[row_count - rim_rows :], "seq", 1)
    extended = jnp.concatenate([rim_before, qkv_raw], axis=0).astype(jnp.float32)
    conv = conv_weight[:, 0, :] * extended[rim_rows:]
    for offset in range(1, TAPS):
        same_doc = seg_all[rim_rows - offset : rim_rows - offset + row_count] == segments
        conv = conv + jnp.where(
            same_doc[:, None, None],
            conv_weight[:, offset, :] * extended[rim_rows - offset : rim_rows - offset + row_count],
            0.0,
        )
    queries = jax.nn.silu(conv[:, 0]).astype(jnp.bfloat16)
    key_rows = jax.nn.silu(conv[:, 1]).astype(jnp.bfloat16)
    values = conv[:, 2].astype(jnp.bfloat16)
    causal = jnp.arange(row_count)[:, None] >= jnp.arange(row_count)[None, :]
    doc_mask = causal & (segments[:, None] == segments[None, :])
    apply_prev = (segments == prev_seg)[:, None]
    apply_next = (segments == next_seg)[:, None]
    keep_last = (segments == segments[-1])[:, None]
    score_list = []
    local_list = []
    summary_list = []
    for head_id in range(heads_local):
        columns = slice(head_id * HEAD_DIM, (head_id + 1) * HEAD_DIM)
        scores = jnp.where(
            doc_mask,
            jnp.dot(
                queries[:, columns], key_rows[:, columns].T, preferred_element_type=jnp.float32
            ),
            0.0,
        )
        score_list.append(scores)
        local_list.append(
            jnp.dot(scores, values[:, columns].astype(jnp.float32), precision=highest)
        )
        masked_k = jnp.where(keep_last, key_rows[:, columns], jnp.zeros_like(key_rows[:, columns]))
        summary_list.append(
            jnp.dot(masked_k.T, values[:, columns], preferred_element_type=jnp.float32)
        )
    summaries = jnp.stack(summary_list)
    incoming, unused_flag = prefix(
        (summaries, start_flag),
        "seq",
        combine_states,
        (jnp.zeros_like(summaries), jnp.zeros((), jnp.float32)),
        False,
    )
    attn_list = []
    for head_id in range(heads_local):
        columns = slice(head_id * HEAD_DIM, (head_id + 1) * HEAD_DIM)
        carried = jnp.where(
            apply_prev,
            jnp.dot(queries[:, columns].astype(jnp.float32), incoming[head_id], precision=highest),
            0.0,
        )
        attn_list.append(local_list[head_id] + carried)
    attn = jnp.stack(attn_list, axis=1)
    gain_rows = norm_gain.reshape(heads_local, HEAD_DIM)
    msq = jnp.mean(attn * attn, axis=-1, keepdims=True)
    bound = msq > 1.0
    scale = lax.rsqrt(jnp.maximum(msq, 1.0))
    attn_local = (attn * scale * gain_rows).astype(jnp.bfloat16).reshape(row_count, width_local)
    scaled_cot = cotangent.astype(jnp.float32).reshape(row_count, heads_local, HEAD_DIM) * gain_rows
    inner = jnp.mean(scaled_cot * attn, axis=-1, keepdims=True)
    grad_norm = (
        (scale * scaled_cot - jnp.where(bound, attn * scale * scale * scale * inner, 0.0))
        .astype(jnp.bfloat16)
        .reshape(row_count, width_local)
    )
    grad_score_list = []
    grad_q_list = []
    back_list = []
    for head_id in range(heads_local):
        columns = slice(head_id * HEAD_DIM, (head_id + 1) * HEAD_DIM)
        grad_scores = jnp.where(
            doc_mask,
            jnp.dot(
                grad_norm[:, columns], values[:, columns].T, preferred_element_type=jnp.float32
            ),
            0.0,
        )
        grad_score_list.append(grad_scores)
        carried_grad = jnp.where(
            apply_prev,
            jnp.dot(
                grad_norm[:, columns].astype(jnp.float32), incoming[head_id].T, precision=highest
            ),
            0.0,
        )
        grad_q_list.append(
            jnp.dot(grad_scores, key_rows[:, columns].astype(jnp.float32), precision=highest)
            + carried_grad
        )
        masked_q = jnp.where(apply_prev, queries[:, columns], jnp.zeros_like(queries[:, columns]))
        back_list.append(
            jnp.dot(masked_q.T, grad_norm[:, columns], preferred_element_type=jnp.float32)
        )
    back_sums = jnp.stack(back_list)
    future, unused_back = prefix(
        (back_sums, start_flag),
        "seq",
        combine_states,
        (jnp.zeros_like(back_sums), jnp.zeros((), jnp.float32)),
        True,
    )
    grad_k_list = []
    grad_v_list = []
    for head_id in range(heads_local):
        columns = slice(head_id * HEAD_DIM, (head_id + 1) * HEAD_DIM)
        q_float = queries[:, columns].astype(jnp.float32)
        k_float = key_rows[:, columns].astype(jnp.float32)
        v_float = values[:, columns].astype(jnp.float32)
        g_float = grad_norm[:, columns].astype(jnp.float32)
        local_k = jnp.einsum("ts,te->se", grad_score_list[head_id], q_float, precision=highest)
        grad_k_list.append(
            local_k
            + jnp.where(apply_next, jnp.dot(v_float, future[head_id].T, precision=highest), 0.0)
        )
        local_v = jnp.einsum("ts,te->se", score_list[head_id], g_float, precision=highest)
        grad_v_list.append(
            local_v
            + jnp.where(apply_next, jnp.dot(k_float, future[head_id], precision=highest), 0.0)
        )
    grad_q_all = jnp.concatenate(grad_q_list, axis=1)
    grad_k_all = jnp.concatenate(grad_k_list, axis=1)
    grad_v_all = jnp.concatenate(grad_v_list, axis=1)
    grad_conv = jnp.stack(
        [grad_q_all * silu_slope(conv[:, 0]), grad_k_all * silu_slope(conv[:, 1]), grad_v_all],
        axis=1,
    )
    rim_after = from_behind(grad_conv[:rim_rows], "seq", -1)
    extended_grad = jnp.concatenate([grad_conv, rim_after], axis=0)
    total = conv_weight[:, 0, :] * grad_conv
    for offset in range(1, TAPS):
        same_doc = segments == seg_all[rim_rows + offset : rim_rows + offset + row_count]
        total = total + jnp.where(
            same_doc[:, None, None],
            conv_weight[:, offset, :] * extended_grad[offset : offset + row_count],
            0.0,
        )
    grad_local = total.astype(jnp.bfloat16)
    out_three, grad_rows = (
        lax.all_to_all(attn_local[:, None, :], "head", split_axis=0, concat_axis=2, tiled=True),
        lax.all_to_all(grad_local, "head", split_axis=0, concat_axis=2, tiled=True),
    )
    out_rows = out_three.reshape(out_three.shape[0], out_three.shape[2])
    return (out_rows, grad_rows)


def solution(mesh):
    return jax.shard_map(
        shards,
        mesh=mesh,
        in_specs=(P("seq", None, "head"), P(None, None, "head"), P("head"), P(), P("seq", "head")),
        out_specs=(P(("seq", "head"), None), P(("seq", "head"), None, None)),
        check_vma=False,
    )
```

profile of v0, /device:TPU:1, one launch (start us, length us, event | category | flops | bytes accessed | tf_op | source)
XLA Modules:
  0.0 420.0 jit_solution(6929724972079225120)
XLA Ops:
  8.1 4.0 collective-permute-start
  13.6 0.9 fusion.113
  14.5 2.5 slice_compare_fusion.2
  17.0 1.4 copy.48
  18.9 1.9 fusion.8
  20.9 1.0 fusion.39
  24.5 1.3 dynamic-slice
  26.5 59.7 %all-reduce = f32[32]{0:T(128)} all-reduce(f32[32]{0:T(128)S(1)} %dynamic-update-slice), channel_id=1, replica_groups=mesh['seq'=32,'head'=16] {'seq'}, use_global_device_ids=true, to_apply=%add | all-reduce | flops 32 | bytes 256
  86.2 1.2 convolution_select_fusion.2
  87.5 1.2 convolution_select_fusion.3
  88.7 1.4 fusion.66
  90.2 1.4 fusion.77
  91.6 20.7 %all-gather.5.cloned.1.call-done = f32[64,128,128]{2,1,0:T(8,128)} async-done(((f32[2,128,128]{2,1,0:T(8,128)}), f32[64,128,128]{2,1,0:T(8,128)}) %all-gather.5.cloned.1.call-update) | async-done | bytes 4194320 | tf_op jit(solution)/shard_map/all_gather | solution.py:23
  112.3 1.3 fusion.24
  113.6 1.3 fusion.26
  114.9 0.9 multiply_reduce_fusion
  115.8 0.9 pad_maximum_fusion.2
  118.1 2.0 copy.56
  120.1 1.1 convolution_select_fusion
  122.0 1.0 fusion.20
  124.0 1.0 fusion.22
  125.0 1.2 fusion.54
  126.2 1.2 fusion.49
  128.4 156.4 %all-gather.7.cloned.1.call-done = f32[64,128,128]{2,1,0:T(8,128)} async-done(((f32[2,128,128]{2,1,0:T(8,128)}), f32[64,128,128]{2,1,0:T(8,128)}) %all-gather.7.cloned.1.call-update) | async-done | bytes 4194320 | tf_op jit(solution)/shard_map/all_gather | solution.py:23
  284.9 68.7 %while.27 = (s32[]{:T(128)}, f32[2,128,128]{2,1,0:T(8,128)S(1)}, s32[]{:T(128)}, f32[32,2,128,128]{3,2,1,0:T(8,128)}, f32[32]{0:T(128)S(1)}, /*index=5*/s32[]{:T(128)}, s32[]{:T(128)}, s32[]{:T(128)}, s32[]{:T(128)}, f32[1]{0:T(128)}) while((s32[]{:T(128)}, f32[2,128,128]{2,1,0:T(8,128)S(1)}, s32[]{:T(128)}, f32[32,2,128,128]{3,2,1,0:T(8,128)}, ...), condition=%wide.region_7.8_spmd, body=%wide.region_6.7_spmd.sunk | while | flops 65543 | bytes 393403 | solution.py:32
  286.1 1.0 bitcast_add_fusion.5
  288.4 1.0 bitcast_add_fusion.5
  290.6 1.0 bitcast_add_fusion.5
  292.8 1.0 bitcast_add_fusion.5
  295.0 1.0 bitcast_add_fusion.5
  297.2 1.0 bitcast_add_fusion.5
  299.4 1.0 bitcast_add_fusion.5
  301.6 1.0 bitcast_add_fusion.5
  303.9 1.0 bitcast_add_fusion.5
  306.1 1.0 bitcast_add_fusion.5
  308.3 1.0 bitcast_add_fusion.5
  310.5 1.0 bitcast_add_fusion.5
  312.7 1.0 bitcast_add_fusion.5
  314.9 1.0 bitcast_add_fusion.5
  317.2 1.0 bitcast_add_fusion.5
  319.4 1.0 bitcast_add_fusion.5
  321.6 1.0 bitcast_add_fusion.5
  323.8 1.0 bitcast_add_fusion.5
  326.0 1.0 bitcast_add_fusion.5
  328.2 1.0 bitcast_add_fusion.5
  330.4 1.0 bitcast_add_fusion.5
  332.7 1.0 bitcast_add_fusion.5
  334.9 1.0 bitcast_add_fusion.5
  337.1 1.0 bitcast_add_fusion.5
  339.3 1.0 bitcast_add_fusion.5
  341.5 1.0 bitcast_add_fusion.5
  343.7 1.0 bitcast_add_fusion.5
  345.9 1.0 bitcast_add_fusion.5
  348.2 1.0 bitcast_add_fusion.5
  350.4 1.0 bitcast_add_fusion.5
  352.6 1.0 bitcast_add_fusion.5
  355.5 1.3 collective-permute-start.1
  359.0 10.6 %all-to-all-start = ((bf16[16,2,4096]{2,1,0:T(2,128)(2,1)}), bf16[16,2,4096]{2,1,0:T(2,128)(2,1)S(1)}, u32[]{:S(2)}, u32[]{:S(2)}) async-start(bf16[16,2,4096]{2,1,0:T(2,128)(2,1)} %reshape.117), calls=%async_computation | async-start | bytes 524288 | tf_op jit(solution)/shard_map/all_to_all | solution.py:204
  370.2 1.9 fusion.2
  372.1 1.4 copy.53
  373.5 7.8 %all-to-all-done = bf16[16,2,4096]{2,1,0:T(2,128)(2,1)S(1)} async-done(((bf16[16,2,4096]{2,1,0:T(2,128)(2,1)}), bf16[16,2,4096]{2,1,0:T(2,128)(2,1)S(1)}, u32[]{:S(2)}, u32[]{:S(2)}) %all-to-all-start) | async-done | bytes 262176 | tf_op jit(solution)/shard_map/all_to_all | solution.py:204
  381.3 3.6 all-to-all-start.1
  385.9 26.2 %all-to-all-done.1 = bf16[512,3,256]{2,1,0:T(4,128)(2,1)S(1)} async-done(((bf16[512,3,256]{2,1,0:T(4,128)(2,1)}), bf16[512,3,256]{2,1,0:T(4,128)(2,1)S(1)}, u32[]{:S(2)}, u32[]{:S(2)}) %all-to-all-start.1) | async-done | bytes 786464 | tf_op jit(solution)/shard_map/all_to_all | solution.py:205
  412.2 1.0 copy.62
  (137 shorter events, 33.6 us)
Async XLA Ops:
  7.2 105.1 %all-gather.5.cloned.1.call-start = ((), (), s32[]{:S(2)}) async-start(), calls=%async_computation.2 | async-start | bytes 4325376 | tf_op jit(solution)/shard_map/all_gather | solution.py:23
  8.1 10.3 %collective-permute-start = (bf16[3,3,256]{0,2,1:T(8,128)(2,1)S(1)}, bf16[3,3,256]{0,2,1:T(8,128)(2,1)S(1)}, u32[]{:S(2)}, u32[]{:S(2)}) collective-permute-start(bf16[3,3,256]{0,2,1:T(8,128)(2,1)S(1)} %copy.47), channel_id=1, source_target_pairs={{0,16},{16,32},{32,48},{48,64},{64,80},{80,96},{96,112},{112,128},... | collective-permute-start | bytes 13832 | tf_op jit(solution)/shard_map/ppermute | solution.py:16
  20.8 2.2 copy-start.23
  20.8 3.5 copy-start.12
  21.8 65.6 %copy-start.2 = (bf16[512,256]{0,1:T(8,128)(2,1)}, bf16[512,256]{0,1:T(8,128)(2,1)S(1)}, u32[]{:S(2)}) copy-start(bf16[512,256]{0,1:T(8,128)(2,1)S(1)} %get-tuple-element.156) | copy-start | bytes 786436
  22.9 261.9 %all-gather.7.cloned.1.call-start = ((), (), s32[]{:S(2)}) async-start(), calls=%async_computation.3 | async-start | bytes 4325376 | tf_op jit(solution)/shard_map/all_gather | solution.py:23
  23.0 65.7 %copy-start.21 = (s32[512]{0:T(512)}, s32[512]{0:T(512)S(1)}, u32[]{:S(2)}) copy-start(s32[512]{0:T(512)S(1)} %slice.150) | copy-start | bytes 6148
  88.7 1.4 copy-start
  90.2 22.1 %copy-start.4 = (bf16[512,256]{0,1:T(8,128)(2,1)S(1)}, bf16[512,256]{0,1:T(8,128)(2,1)}, u32[]{:S(2)}) copy-start(bf16[512,256]{0,1:T(8,128)(2,1)} %get-tuple-element.157) | copy-start | bytes 786436
  113.6 3.2 copy-start.16
  114.9 2.1 copy-start.5
  114.9 2.1 copy-start.14
  117.4 3.9 copy-start.3
  120.1 1.9 copy-start.15
  120.1 2.8 copy-start.22
  122.9 2.0 copy-start.1
  125.0 2.4 copy-start.6
  127.4 157.5 %copy-start.24 = (f32[32]{0:T(128)S(1)}, f32[32]{0:T(128)}, u32[]{:S(2)}) copy-start(f32[32]{0:T(128)} %get-tuple-element.315) | copy-start | bytes 388
  127.9 225.6 %copy-start.11 = (f32[512,128]{0,1:T(8,128)S(1)}, f32[512,128]{0,1:T(8,128)}, u32[]{:S(2)}) copy-start(f32[512,128]{0,1:T(8,128)} %fusion.49) | copy-start | bytes 786436
  127.9 225.6 %copy-start.13 = (pred[512]{0:T(512)(128)(4,1)S(1)}, pred[512]{0:T(512)(128)(4,1)}, u32[]{:S(2)}) copy-start(pred[512]{0:T(512)(128)(4,1)} %get-tuple-element.167) | copy-start | bytes 1540
  128.4 225.5 %copy-start.10 = (f32[512,128]{0,1:T(8,128)S(1)}, f32[512,128]{0,1:T(8,128)}, u32[]{:S(2)}) copy-start(f32[512,128]{0,1:T(8,128)} %fusion.54) | copy-start | bytes 786436
  353.9 1.0 copy-start.8
  353.9 1.0 copy-start.9
  355.3 1.5 copy-start.7
  355.3 1.5 copy-start.17
  355.5 14.1 %collective-permute-start.1 = (f32[3,3,256]{0,2,1:T(8,128)S(1)}, f32[3,3,256]{0,2,1:T(8,128)S(1)}, u32[]{:S(2)}, u32[]{:S(2)}) collective-permute-start(f32[3,3,256]{0,2,1:T(8,128)S(1)} %slice.203), channel_id=1, source_target_pairs={{16,0},{32,16},{48,32},{64,48},{80,64},{96,80},{112,96},{128,112},... | collective-permute-start | bytes 27656 | tf_op jit(solution)/shard_map/ppermute | solution.py:16
  359.0 22.3 %all-to-all-start = ((bf16[16,2,4096]{2,1,0:T(2,128)(2,1)}), bf16[16,2,4096]{2,1,0:T(2,128)(2,1)S(1)}, u32[]{:S(2)}, u32[]{:S(2)}) async-start(bf16[16,2,4096]{2,1,0:T(2,128)(2,1)} %reshape.117), calls=%async_computation | async-start | bytes 524288 | tf_op jit(solution)/shard_map/all_to_all | solution.py:204
  369.6 0.6 copy-start.18
  369.6 0.6 copy-start.19
  369.6 0.6 copy-start.20
  381.3 30.8 %all-to-all-start.1 = ((bf16[512,3,256]{2,1,0:T(4,128)(2,1)}), bf16[512,3,256]{2,1,0:T(4,128)(2,1)S(1)}, u32[]{:S(2)}, u32[]{:S(2)}) async-start(bf16[512,3,256]{2,1,0:T(4,128)(2,1)} %copy.53), calls=%async_computation.1 | async-start | bytes 2097152 | tf_op jit(solution)/shard_map/all_to_all | solution.py:205
Sparse Core Ops, SparseCore 0:
  23.0 89.2 all-gather.4
  118.2 166.6 all-gather.6
where the time goes:
time: 422 us; the launch traced here: 420 us
  waiting for transfers between devices  211 us (50%)
  blocking collectives  59.7 us (14%)
  other arithmetic  43.6 us (10%)
  local copies, waits for them, and re-layouts  31.9 us (8%)
  loops' own time  20.9 us (5%)
  starting transfers between devices  19.5 us (5%)
  matrix products  18 us (4%)
  between operations  15.3 us (4%)
    all_gather x2, waiting for transfers between devices, prefix(): gathered = jax.tree.map(lambda a: lax.all_gather(a, axis), part)  177 us
    unnamed x1, blocking collectives  59.7 us
    add x31, other arithmetic, combine_states(): later[0] + (1.0 - later[1]) * earlier[0]  29.6 us
    all_to_all x1, waiting for transfers between devices, shards(): lax.all_to_all(grad_local, 'head', split_axis=0, concat_axis=2, tiled=True)  26.2 us
    another operation x2, loops' own time, prefix(): return lax.fori_loop(0, ahead, one, state)  20.9 us
    dynamic_slice x31, local copies, waits for them, and re-layouts, one(): lax.dynamic_index_in_dim(a, source, 0, False)  18.2 us
    all_to_all x1, starting transfers between devices, shards(): lax.all_to_all(attn_local[:, None, :], 'head', split_axis=0, concat_axis=...  10.6 us
  transfers between devices with their start and end apart: 6, of which 4 were waited for; matrix products, arithmetic and copies ran while one was open for 7% of the time, Pallas kernels for 0%

commit v1 on v0

v1 whole, which is shorter than its diff:
```python
import jax
import jax.numpy as jnp
from jax import lax
from jax.experimental import pallas as pl
from jax.experimental.pallas import tpu as pltpu
from jax.sharding import PartitionSpec as P

HEAD_DIM = 128
TAPS = 4
CHUNK = 128
HALO = 16
FAR = 1 << 30

f32 = jnp.float32
bf16 = jnp.bfloat16


def nt(a, b):
    return lax.dot_general(a, b, (((1,), (1,)), ((), ())), preferred_element_type=f32)


def nn(a, b):
    return lax.dot_general(a, b, (((1,), (0,)), ((), ())), preferred_element_type=f32)


def tn(a, b):
    return lax.dot_general(a, b, (((0,), (0,)), ((), ())), preferred_element_type=f32)


def doc_start(starts, first, pos):
    found = jnp.int32(-FAR)
    for d in range(starts.shape[0]):
        rel = starts[d] - first
        found = jnp.maximum(found, jnp.where(rel <= pos, rel, -FAR))
    return found


def doc_end(starts, first, pos):
    found = jnp.int32(FAR)
    for d in range(starts.shape[0]):
        rel = starts[d] - first
        found = jnp.minimum(found, jnp.where(rel > pos, rel, FAR))
    return found


def row_starts(starts, first, rows):
    found = jnp.full(rows.shape, -FAR, jnp.int32)
    for d in range(starts.shape[0]):
        rel = starts[d] - first
        found = jnp.maximum(found, jnp.where(rows >= rel, rel, -FAR))
    return found


def iota(shape, axis, base=0):
    return lax.broadcasted_iota(jnp.int32, shape, axis) + base


def conv_kernel(starts, raw, rim, halo, taps, qkv, slope, summary):
    rows = raw.shape[1]
    first = lax.axis_index("seq") * rows
    total = HALO + rows + HALO
    place = iota((total, HEAD_DIM), 0, -HALO)
    age = place - row_starts(starts, first, place)
    made = []
    for m in range(3):
        ext = jnp.concatenate([rim[m], raw[m], halo[m]], axis=0).astype(f32)
        conv = taps[m, 0:1] * ext
        for j in range(1, TAPS):
            conv = conv + jnp.where(age >= j, taps[m, j : j + 1] * pltpu.roll(ext, j, 0), 0.0)
        conv = conv[HALO:]
        if m < 2:
            sigma = 1.0 / (1.0 + jnp.exp(-conv))
            slope[m] = sigma * (1.0 + conv * (1.0 - sigma))
            conv = conv * sigma
        made.append(conv.astype(bf16))
        qkv[m] = made[m]
    last = doc_start(starts, first, rows - 1)
    keep = iota((rows, HEAD_DIM), 0) >= last
    masked_k = jnp.where(keep, made[1][:rows], jnp.zeros((), bf16))
    summary[...] = tn(masked_k, made[2][:rows])


def local_kernel(starts, qkv, local):
    total = qkv.shape[1]
    rows = total - HALO
    first = lax.axis_index("seq") * rows
    for low in range(0, total, CHUNK):
        high = min(low + CHUNK, total)
        size = high - low
        start = doc_start(starts, first, low)
        scores = nt(qkv[0, low:high], qkv[1, :high])
        t, s = iota((size, high), 0, low), iota((size, high), 1)
        scores = jnp.where((s <= t) & (s >= start), scores, 0.0).astype(bf16)
        local[low:high] = nn(scores, qkv[2, :high])


def norm_kernel(starts, qkv, local, incoming, cot, halo, gain, attn_out, grad_norm, back):
    total = local.shape[0]
    rows = total - HALO
    first = lax.axis_index("seq") * rows
    place = iota((total, HEAD_DIM), 0)
    prev = row_starts(starts, first, place) < 0
    q = qkv[0]
    attn = local[...] + jnp.where(prev, nn(q, incoming[...].astype(bf16)), 0.0)
    msq = jnp.mean(attn * attn, axis=-1, keepdims=True)
    scale = lax.rsqrt(jnp.maximum(msq, 1.0))
    gains = gain[...]
    attn_out[...] = (attn[:rows] * scale[:rows] * gains).astype(bf16)
    scaled = jnp.concatenate([cot[...], halo[0]], axis=0).astype(f32) * gains
    inner = jnp.mean(scaled * attn, axis=-1, keepdims=True)
    factor = jnp.where(msq > 1.0, scale * scale * scale * inner, 0.0)
    grad = (scale * scaled - attn * factor).astype(bf16)
    grad_norm[...] = grad
    masked_q = jnp.where(prev[:rows], q[:rows], jnp.zeros((), bf16))
    back[...] = tn(masked_q, grad[:rows])


def conv_back(grad, taps, m, age, rows):
    total = grad.shape[0]
    out = taps[m, 0:1] * grad[:rows]
    for j in range(1, TAPS):
        term = jnp.where(age >= j, taps[m, j : j + 1] * grad, 0.0)
        out = out + pltpu.roll(term, total - j, 0)[:rows]
    return out.astype(bf16)


def grad_kernel(starts, qkv, grad_norm, slope, incoming, taps, attn_out, early, local_k, local_v):
    total = grad_norm.shape[0]
    rows = total - HALO
    first = lax.axis_index("seq") * rows
    place = iota((total, HEAD_DIM), 0)
    begin = row_starts(starts, first, place)
    carried = jnp.where(begin < 0, nt(grad_norm[...], incoming[...].astype(bf16)), 0.0)
    parts = []
    for low in range(0, total, CHUNK):
        high = min(low + CHUNK, total)
        size = high - low
        start = doc_start(starts, first, low)
        scores = nt(grad_norm[low:high], qkv[2, :high])
        t, s = iota((size, high), 0, low), iota((size, high), 1)
        scores = jnp.where((s <= t) & (s >= start), scores, 0.0).astype(bf16)
        parts.append(nn(scores, qkv[1, :high]))
    grad_q = (jnp.concatenate(parts, axis=0) + carried) * slope[0]
    out = conv_back(grad_q, taps, 0, place - begin, rows)
    early[:, 0] = attn_out[...].reshape(early.shape[0], early.shape[2], HEAD_DIM)
    early[:, 1] = out.reshape(early.shape[0], early.shape[2], HEAD_DIM)
    for low in range(0, rows, CHUNK):
        high = low + CHUNK
        end = doc_end(starts, first, low)
        s, t = iota((CHUNK, rows - low), 0, low), iota((CHUNK, rows - low), 1, low)
        keep = (t >= s) & (t < end)
        scores = jnp.where(keep, nt(qkv[2, low:high], grad_norm[low:rows]), 0.0).astype(bf16)
        local_k[low:high] = nn(scores, qkv[0, low:rows])
        scores = jnp.where(keep, nt(qkv[1, low:high], qkv[0, low:rows]), 0.0).astype(bf16)
        local_v[low:high] = nn(scores, grad_norm[low:rows])
    s, t = iota((HALO, HALO), 0), iota((HALO, HALO), 1)
    scores = jnp.where(t < s, -nt(qkv[2, rows:], grad_norm[rows:]), 0.0).astype(bf16)
    local_k[rows:] = nn(scores, qkv[0, rows:])
    scores = jnp.where(t < s, -nt(qkv[1, rows:], qkv[0, rows:]), 0.0).astype(bf16)
    local_v[rows:] = nn(scores, grad_norm[rows:])


def last_kernel(starts, qkv, slope, local_k, local_v, future, taps, late):
    total = local_k.shape[0]
    rows = total - HALO
    first = lax.axis_index("seq") * rows
    place = iota((total, HEAD_DIM), 0)
    age = place - row_starts(starts, first, place)
    after = place >= doc_start(starts, first, rows)
    state = future[...].astype(bf16)
    grad_k = (local_k[...] + jnp.where(after, nt(qkv[2], state), 0.0)) * slope[0]
    grad_v = local_v[...] + jnp.where(after, nn(qkv[1], state), 0.0)
    shape = (late.shape[0], late.shape[2], HEAD_DIM)
    late[:, 0] = conv_back(grad_k, taps, 1, age, rows).reshape(shape)
    late[:, 1] = conv_back(grad_v, taps, 2, age, rows).reshape(shape)


def scan_kernel(reverse, rows, starts, sums, out):
    count = sums.shape[0]
    state = jnp.zeros(sums.shape[1:], f32)
    order = range(count - 1, -1, -1) if reverse else range(count)
    for i in order:
        out[i] = state
        open_here = jnp.bool_(True)
        for d in range(starts.shape[0]):
            here = (starts[d] >= i * rows) & (starts[d] < (i + 1) * rows)
            open_here = open_here & jnp.logical_not(here)
        state = sums[i] + jnp.where(open_here, state, 0.0)


def gather_kernel(early, late, out, grad):
    count, _, _, width = early.shape
    for i in range(count):
        columns = slice(i * width, (i + 1) * width)
        out[:, columns] = early[i, 0]
        grad[0, :, columns] = early[i, 1]
        grad[1, :, columns] = late[i, 0]
        grad[2, :, columns] = late[i, 1]


def shards(qkv_raw, conv_weight, norm_gain, doc_starts, cotangent):
    rows = qkv_raw.shape[0]
    width = qkv_raw.shape[2]
    heads = width // HEAD_DIM
    total = rows + HALO
    devices = lax.axis_size("seq")
    columns = lax.axis_size("head")
    piece = rows // columns
    raw = qkv_raw.transpose(1, 0, 2)
    gain = norm_gain.reshape(1, width)

    ahead = [(i, i + 1) for i in range(devices - 1)]
    behind = [(i + 1, i) for i in range(devices - 1)]
    rim = lax.ppermute(raw[:, rows - HALO :], "seq", ahead)
    halo = lax.ppermute(
        jnp.concatenate([raw[:, :HALO], cotangent[None, :HALO]], axis=0), "seq", behind
    )

    smem = pl.BlockSpec(memory_space=pltpu.SMEM)

    def per_head(shape, axis):
        return pl.BlockSpec(shape, lambda h: tuple(h if a == axis else 0 for a in range(len(shape))))

    def call(body, ins, outs, *args, grid=(heads,)):
        return pl.pallas_call(
            body,
            grid=grid,
            in_specs=[smem] + ins,
            out_specs=[spec for spec, _ in outs],
            out_shape=[shape for _, shape in outs],
            compiler_params=pltpu.CompilerParams(vmem_limit_bytes=48 * 1024 * 1024),
        )(doc_starts, *args)

    def whole(dims, kind):
        return jax.ShapeDtypeStruct(dims, kind)

    hd = HEAD_DIM
    spec_qkv = per_head((3, total, hd), 2)
    spec_taps = per_head((3, TAPS, hd), 2)
    spec_total = per_head((total, hd), 1)
    spec_rows = per_head((rows, hd), 1)
    spec_state = per_head((hd, hd), 0)
    shape_state = whole((heads * hd, hd), f32)

    qkv, slope, summary = call(
        conv_kernel,
        [per_head((3, rows, hd), 2), per_head((3, HALO, hd), 2), per_head((4, HALO, hd), 2), spec_taps],
        [
            (spec_qkv, whole((3, total, width), bf16)),
            (per_head((2, total, hd), 2), whole((2, total, width), f32)),
            (spec_state, shape_state),
        ],
        raw, rim, halo, conv_weight,
    )
    (local,) = call(
        local_kernel, [spec_qkv], [(spec_total, whole((total, width), f32))], qkv
    )

    def scan(sums, reverse):
        share = sums.reshape(devices, -1, hd)
        share = lax.all_to_all(share, "seq", 0, 0, tiled=True)
        flat = pl.BlockSpec(share.shape, lambda: (0, 0, 0))
        (share,) = call(
            lambda *refs: scan_kernel(reverse, rows, *refs),
            [flat], [(flat, whole(share.shape, f32))], share, grid=(),
        )
        return lax.all_to_all(share, "seq", 0, 0, tiled=True).reshape(sums.shape)

    incoming = scan(summary, False)
    attn_out, grad_norm, back = call(
        norm_kernel,
        [
            spec_qkv, spec_total, spec_state, spec_rows,
            pl.BlockSpec((1, HALO, hd), lambda h: (3, 0, h)), per_head((1, hd), 1),
        ],
        [
            (spec_rows, whole((rows, width), bf16)),
            (spec_total, whole((total, width), bf16)),
            (spec_state, shape_state),
        ],
        qkv, local, incoming, cotangent, halo, gain,
    )
    spec_sent = per_head((columns, 2, piece, hd), 3)
    shape_sent = whole((columns, 2, piece, width), bf16)
    early, local_k, local_v = call(
        grad_kernel,
        [spec_qkv, spec_total, per_head((1, total, hd), 2), spec_state, spec_taps, spec_rows],
        [
            (spec_sent, shape_sent),
            (spec_total, whole((total, width), f32)),
            (spec_total, whole((total, width), f32)),
        ],
        qkv, grad_norm, slope, incoming, conv_weight, attn_out,
    )
    early = lax.all_to_all(early, "head", 0, 0, tiled=True)
    future = scan(back, True)
    (late,) = call(
        last_kernel,
        [
            spec_qkv, pl.BlockSpec((1, total, hd), lambda h: (1, 0, h)),
            spec_total, spec_total, spec_state, spec_taps,
        ],
        [(spec_sent, shape_sent)],
        qkv, slope, local_k, local_v, future, conv_weight,
    )
    late = lax.all_to_all(late, "head", 0, 0, tiled=True)
    out, grad = pl.pallas_call(
        gather_kernel,
        out_shape=[
            whole((piece, columns * width), bf16),
            whole((3, piece, columns * width), bf16),
        ],
        compiler_params=pltpu.CompilerParams(vmem_limit_bytes=48 * 1024 * 1024),
    )(early, late)
    return out, grad.transpose(1, 0, 2)


def solution(mesh):
    return jax.shard_map(
        shards,
        mesh=mesh,
        in_specs=(P("seq", None, "head"), P(None, None, "head"), P("head"), P(), P("seq", "head")),
        out_specs=(P(("seq", "head"), None), P(("seq", "head"), None, None)),
        check_vma=False,
    )
```

time: 422 us -> 137 us (0.32)
  waiting for transfers between devices: 211 us -> 21.6 us
  other arithmetic: 43.6 us -> 0.01 us
  local copies, waits for them, and re-layouts: 31.9 us -> 10.8 us
  loops' own time: 20.9 us -> 0 us
  Pallas kernels: 0 us -> 18.1 us
  matrix products: 18 us -> 0 us
  between operations: 15.3 us -> 0.79 us
  starting transfers between devices: 19.5 us -> 31.1 us
  blocking collectives: 59.7 us -> 53.2 us
    all_gather x2 -> x0, waiting for transfers between devices: 177 us -> none  [prefix(): gathered = jax.tree.map(lambda a: lax.all_gather(a, axis), part)]
    unnamed x1 -> x0, blocking collectives: 59.7 us -> none
    all_to_all x0 -> x3, blocking collectives: none -> 53.2 us  [the longest x2 33.2 us: scan(): share = lax.all_to_all(share, 'seq', 0, 0, tiled=True)]
    add x33 -> x0, other arithmetic: 31.5 us -> none  [the longest x31 29.6 us: combine_states(): later[0] + (1.0 - later[1]) * earlier[0]]
    another operation x2 -> x0, loops' own time: 20.9 us -> none  [prefix(): return lax.fori_loop(0, ahead, one, state)]
    dynamic_slice x31 -> x0, local copies, waits for them, and re-layouts: 18.2 us -> none  [one(): lax.dynamic_index_in_dim(a, source, 0, False)]
    pallas_call x0 -> x8, Pallas kernels: none -> 18.1 us  [the longest x7 17.1 us: call(): pl.pallas_call(body, grid=grid, in_specs=[smem] + ins, out_specs=[spec fo...]
    dot_general x24 -> x0, matrix products: 18 us -> none  [the longest x2 2.87 us: shards(): jnp.dot(scores, values[:, columns].astype(jnp.float32), precision=highest)]
  transfers between devices with their start and end apart: 6 -> 5, of which waited for: 4 -> 4; matrix products, arithmetic and copies ran while one was open for 7% -> 0% of each run, Pallas kernels for 0% -> 7%
where the time goes in v1:
time: 137 us; the launch traced here: 136 us
  blocking collectives  53.2 us (39%)
  starting transfers between devices  31.1 us (23%)
  waiting for transfers between devices  21.6 us (16%)
  Pallas kernels  18.1 us (13%)
  local copies, waits for them, and re-layouts  10.8 us (8%)
    all_to_all x2, blocking collectives, scan(): share = lax.all_to_all(share, 'seq', 0, 0, tiled=True)  33.2 us
    all_to_all x1, blocking collectives, shards(): late = lax.all_to_all(late, 'head', 0, 0, tiled=True)  20 us
    all_to_all x1, starting transfers between devices, shards(): early = lax.all_to_all(early, 'head', 0, 0, tiled=True)  17.5 us
    pallas_call x7, Pallas kernels, call(): pl.pallas_call(body, grid=grid, in_specs=[smem] + ins, out_specs=[spec fo...  17.1 us
    all_to_all x1, waiting for transfers between devices, shards(): early = lax.all_to_all(early, 'head', 0, 0, tiled=True)  13.2 us
    unnamed x32, local copies, waits for them, and re-layouts  9.37 us
    all_to_all x2, starting transfers between devices, scan(): return lax.all_to_all(share, 'seq', 0, 0, tiled=True).reshape(sums.shape)  7.7 us
    all_to_all x2, waiting for transfers between devices, scan(): return lax.all_to_all(share, 'seq', 0, 0, tiled=True).reshape(sums.shape)  7.45 us
  transfers between devices with their start and end apart: 5, of which 4 were waited for; matrix products, arithmetic and copies ran while one was open for 0% of the time, Pallas kernels for 7%

profile of v1, /device:TPU:1, one launch (start us, length us, event | category | flops | bytes accessed | tf_op | source)
XLA Modules:
  0.0 135.7 jit_solution(9246363235932231055)
XLA Ops:
  0.6 0.0 copy-start.14
  0.6 0.7 slice_bitcast_fusion
  1.3 0.8 fusion
  2.1 1.3 collective-permute-start.1
  3.4 4.7 %collective-permute-start = (bf16[3,16,256]{2,1,0:T(8,128)(2,1)S(1)}, bf16[3,16,256]{2,1,0:T(8,128)(2,1)S(1)}, u32[]{:S(2)}, u32[]{:S(2)}) collective-permute-start(bf16[3,16,256]{2,1,0:T(8,128)(2,1)S(1)} %get-tuple-element.25), channel_id=1, source_target_pairs={{0,16},{16,32},{32,48},{48,64},{64,80},{80,96},{96,112},{112,128},... | collective-permute-start | bytes 73736 | tf_op jit(solution)/shard_map/ppermute | solution.py:214
  8.1 0.9 collective-permute-done.rim
  9.0 0.0 collective-permute-done.1.halo
  9.0 0.0 copy-start
  9.0 1.1 copy-done
  10.1 0.0 copy-start.11
  10.1 0.7 copy-done.11
  10.9 0.0 copy-start.13
  10.9 0.7 copy-done.13
  11.5 3.0 %shard_map.68 = (bf16[3,528,256]{2,1,0:T(8,128)(2,1)S(1)}, f32[2,528,256]{2,1,0:T(8,128)S(1)}, f32[256,128]{1,0:T(8,128)S(1)}) custom-call(s32[4]{0:T(128)S(1)} %copy-done.13, bf16[3,512,256]{2,1,0:T(8,128)(2,1)S(1)} %bitcast.12, bf16[3,16,256]{2,1,0:T(8,128)(2,1)S(1)} %collective-permute-done.rim, bf16[4,16,256]{2,1,0:T(8,128)(2,1)S(1)} %collective-permute-done.1.halo, ...), custom_call_target="tpu_custom_call" | custom-call | tf_op jit(solution)/shard_map/pallas_call | solution.py:225
  14.5 0.0 copy-start.6
  14.6 0.0 copy-start.15
  14.6 20.6 %all_to_all.30.refs_1_ = f32[32,8,128]{2,1,0:T(8,128)S(1)} all-to-all(f32[32,8,128]{2,1,0:T(8,128)S(1)} %bitcast.15), channel_id=1, replica_groups=mesh['seq'=32,'head'=16] {'seq'}, dimensions={0} | all-to-all | bytes 262144 | tf_op jit(solution)/shard_map/all_to_all | solution.py:261
  35.1 1.4 shard_map.70
  36.5 3.9 %all-to-all-start.1 = ((f32[32,8,128]{2,1,0:T(8,128)}), f32[32,8,128]{2,1,0:T(8,128)S(1)}, u32[]{:S(2)}, u32[]{:S(2)}) async-start(f32[32,8,128]{2,1,0:T(8,128)} %shard_map.70), calls=%async_computation.1 | async-start | bytes 262144 | tf_op jit(solution)/shard_map/all_to_all | solution.py:267
  40.4 0.0 copy-done.14
  40.4 2.4 %shard_map.69.local = f32[528,256]{1,0:T(8,128)S(1)} custom-call(s32[4]{0:T(128)S(1)} %copy-done.14, bf16[3,528,256]{2,1,0:T(8,128)(2,1)S(1)} %get-tuple-element.13.qkv), custom_call_target="tpu_custom_call" | custom-call | tf_op jit(solution)/shard_map/pallas_call | solution.py:225
  42.8 6.7 %all-to-all-done.1 = f32[32,8,128]{2,1,0:T(8,128)S(1)} async-done(((f32[32,8,128]{2,1,0:T(8,128)}), f32[32,8,128]{2,1,0:T(8,128)S(1)}, u32[]{:S(2)}, u32[]{:S(2)}) %all-to-all-start.1) | async-done | bytes 131104 | tf_op jit(solution)/shard_map/all_to_all | solution.py:267
  49.5 0.0 copy-done.6
  49.5 0.0 copy-done.15
  49.5 0.0 copy-start.12
  49.5 1.9 %shard_map.71 = (bf16[512,256]{1,0:T(8,128)(2,1)S(1)}, bf16[528,256]{1,0:T(8,128)(2,1)S(1)}, f32[256,128]{1,0:T(8,128)S(1)}) custom-call(s32[4]{0:T(128)S(1)} %copy-done.14, bf16[3,528,256]{2,1,0:T(8,128)(2,1)S(1)} %get-tuple-element.13.qkv, f32[528,256]{1,0:T(8,128)S(1)} %shard_map.69.local, f32[256,128]{1,0:T(8,128)S(1)} %bitcast.9, ...), custom_call_target="tpu_custom_call" | custom-call | tf_op jit(solution)/shard_map/pallas_call | solution.py:225
  51.5 0.0 copy-start.7
  51.5 0.7 copy-done.7
  52.2 0.0 copy-start.9
  52.2 0.7 copy-done.9
  52.9 12.6 %all_to_all.31.refs_1_ = f32[32,8,128]{2,1,0:T(8,128)S(1)} all-to-all(f32[32,8,128]{2,1,0:T(8,128)S(1)} %bitcast.14), channel_id=1, replica_groups=mesh['seq'=32,'head'=16] {'seq'}, dimensions={0} | all-to-all | bytes 262144 | tf_op jit(solution)/shard_map/all_to_all | solution.py:261
  65.5 1.4 %shard_map.73 = f32[32,8,128]{2,1,0:T(8,128)} custom-call(s32[4]{0:T(128)S(1)} %copy-done.14, f32[32,8,128]{2,1,0:T(8,128)S(1)} %all_to_all.31.refs_1_), custom_call_target="tpu_custom_call" | custom-call | tf_op jit(solution)/shard_map/pallas_call | solution.py:225
  66.8 3.8 %all-to-all-start.4 = ((f32[32,8,128]{2,1,0:T(8,128)}), f32[32,8,128]{2,1,0:T(8,128)S(1)}, u32[]{:S(2)}, u32[]{:S(2)}) async-start(f32[32,8,128]{2,1,0:T(8,128)} %shard_map.73), calls=%async_computation.4 | async-start | bytes 262144 | tf_op jit(solution)/shard_map/all_to_all | solution.py:267
  70.7 0.0 copy-done.12
  70.7 0.0 copy-start.8
  70.7 0.9 copy-done.8
  71.7 0.0 copy-start.10
  71.7 0.9 copy-done.10
  72.6 4.9 %shard_map.72 = (bf16[16,2,32,256]{3,2,1,0:T(8,128)(2,1)S(1)}, f32[528,256]{1,0:T(8,128)S(1)}, f32[528,256]{1,0:T(8,128)S(1)}) custom-call(s32[4]{0:T(128)S(1)} %copy-done.14, bf16[3,528,256]{2,1,0:T(8,128)(2,1)S(1)} %get-tuple-element.13.qkv, bf16[528,256]{1,0:T(8,128)(2,1)S(1)} %copy-done.8, f32[2,528,256]{2,1,0:T(8,128)S(1)} %get-tuple-element.16.slope, ...), custom_call_target="tpu_custom_call" | custom-call | tf_op jit(solution)/shard_map/pallas_call | solution.py:225
  77.5 0.0 copy-start.1
  77.5 0.8 copy-done.1
  78.3 0.0 copy-start.5
  78.3 0.8 copy-done.5
  79.1 0.7 all-to-all-done.4
  79.8 0.0 copy-start.3
  79.8 17.5 %all-to-all-start.2 = ((bf16[16,2,32,256]{3,2,1,0:T(8,128)(2,1)}), bf16[16,2,32,256]{3,2,1,0:T(8,128)(2,1)S(1)}, u32[]{:S(2)}, u32[]{:S(2)}) async-start(bf16[16,2,32,256]{3,2,1,0:T(8,128)(2,1)} %copy-done.5), calls=%async_computation.2 | async-start | bytes 1048576 | tf_op jit(solution)/shard_map/all_to_all | solution.py:295
  97.3 0.0 copy-done.3
  97.3 0.0 copy-start.2
  97.3 1.0 copy-done.2
  98.4 0.0 copy-start.4
  98.4 0.9 copy-done.4
  99.3 2.1 %shard_map.74 = bf16[16,2,32,256]{3,2,1,0:T(8,128)(2,1)S(1)} custom-call(s32[4]{0:T(128)S(1)} %copy-done.14, bf16[3,528,256]{2,1,0:T(8,128)(2,1)S(1)} %get-tuple-element.13.qkv, f32[2,528,256]{2,1,0:T(8,128)S(1)} %get-tuple-element.16.slope, f32[528,256]{1,0:T(8,128)S(1)} %get-tuple-element.19.local_k, f32[528,256]{1,0:T(8,128)S(1)} %copy-done.2, ...), custom_call_target="tpu_custom_call" | custom-call | tf_op jit(solution)/shard_map/pallas_call | solution.py:225
  101.4 13.2 %all-to-all-done.2.early = bf16[16,2,32,256]{3,2,1,0:T(8,128)(2,1)S(1)} async-done(((bf16[16,2,32,256]{3,2,1,0:T(8,128)(2,1)}), bf16[16,2,32,256]{3,2,1,0:T(8,128)(2,1)S(1)}, u32[]{:S(2)}, u32[]{:S(2)}) %all-to-all-start.2) | async-done | bytes 524320 | tf_op jit(solution)/shard_map/all_to_all | solution.py:295
  114.6 20.0 %all_to_all.32.late = bf16[16,2,32,256]{3,2,1,0:T(8,128)(2,1)S(1)} all-to-all(bf16[16,2,32,256]{3,2,1,0:T(8,128)(2,1)S(1)} %shard_map.74), channel_id=1, replica_groups=mesh['seq'=32,'head'=16] {'head'}, dimensions={0} | all-to-all | bytes 1048576 | tf_op jit(solution)/shard_map/all_to_all | solution.py:306
  134.6 1.1 shard_map.75
  (1 shorter events, 0.0 us)
Async XLA Ops:
  0.6 39.7 %copy-start.14 = (s32[4]{0:T(128)S(1)}, s32[4]{0:T(128)}, u32[]{:S(2)}) copy-start(s32[4]{0:T(128)} %starts.9) | copy-start | bytes 52
  2.1 6.9 %collective-permute-start.1 = (bf16[4,16,256]{2,1,0:T(8,128)(2,1)S(1)}, bf16[4,16,256]{2,1,0:T(8,128)(2,1)S(1)}, u32[]{:S(2)}, u32[]{:S(2)}) collective-permute-start(bf16[4,16,256]{2,1,0:T(8,128)(2,1)S(1)} %pad_maximum_fusion), channel_id=1, source_target_pairs={{16,0},{32,16},{48,32},{64,48},{80,64},{96,80},{112,96},{128,112},... | collective-permute-start | bytes 98312 | tf_op jit(solution)/shard_map/ppermute | solution.py:215
  3.4 5.6 %collective-permute-start = (bf16[3,16,256]{2,1,0:T(8,128)(2,1)S(1)}, bf16[3,16,256]{2,1,0:T(8,128)(2,1)S(1)}, u32[]{:S(2)}, u32[]{:S(2)}) collective-permute-start(bf16[3,16,256]{2,1,0:T(8,128)(2,1)S(1)} %get-tuple-element.25), channel_id=1, source_target_pairs={{0,16},{16,32},{32,48},{48,64},{64,80},{80,96},{96,112},{112,128},... | collective-permute-start | bytes 73736 | tf_op jit(solution)/shard_map/ppermute | solution.py:214
  9.0 1.1 copy-start
  10.1 0.7 copy-start.11
  10.9 0.7 copy-start.13
  14.5 35.0 %copy-start.6 = (bf16[512,256]{1,0:T(8,128)(2,1)S(1)}, bf16[512,256]{1,0:T(8,128)(2,1)}, u32[]{:S(2)}) copy-start(bf16[512,256]{1,0:T(8,128)(2,1)} %cot.1) | copy-start | bytes 786436
  14.6 35.0 %copy-start.15 = (f32[256]{0:T(256)S(1)}, f32[256]{0:T(256)}, u32[]{:S(2)}) copy-start(f32[256]{0:T(256)} %param.7) | copy-start | bytes 3076
  36.5 13.0 %all-to-all-start.1 = ((f32[32,8,128]{2,1,0:T(8,128)}), f32[32,8,128]{2,1,0:T(8,128)S(1)}, u32[]{:S(2)}, u32[]{:S(2)}) async-start(f32[32,8,128]{2,1,0:T(8,128)} %shard_map.70), calls=%async_computation.1 | async-start | bytes 262144 | tf_op jit(solution)/shard_map/all_to_all | solution.py:267
  49.5 21.2 %copy-start.12 = (f32[3,4,256]{2,1,0:T(4,128)S(1)}, f32[3,4,256]{2,1,0:T(4,128)}, u32[]{:S(2)}) copy-start(f32[3,4,256]{2,1,0:T(4,128)} %taps.5) | copy-start | bytes 36868
  51.5 0.7 copy-start.7
  52.2 0.7 copy-start.9
  66.8 13.0 %all-to-all-start.4 = ((f32[32,8,128]{2,1,0:T(8,128)}), f32[32,8,128]{2,1,0:T(8,128)S(1)}, u32[]{:S(2)}, u32[]{:S(2)}) async-start(f32[32,8,128]{2,1,0:T(8,128)} %shard_map.73), calls=%async_computation.4 | async-start | bytes 262144 | tf_op jit(solution)/shard_map/all_to_all | solution.py:267
  70.7 1.0 copy-start.8
  71.7 0.9 copy-start.10
  77.5 0.8 copy-start.1
  78.3 0.8 copy-start.5
  79.8 17.5 %copy-start.3 = (f32[32,8,128]{2,1,0:T(8,128)}, f32[32,8,128]{2,1,0:T(8,128)S(1)}, u32[]{:S(2)}) copy-start(f32[32,8,128]{2,1,0:T(8,128)S(1)} %all-to-all-done.4) | copy-start | bytes 393220
  79.8 34.8 %all-to-all-start.2 = ((bf16[16,2,32,256]{3,2,1,0:T(8,128)(2,1)}), bf16[16,2,32,256]{3,2,1,0:T(8,128)(2,1)S(1)}, u32[]{:S(2)}, u32[]{:S(2)}) async-start(bf16[16,2,32,256]{3,2,1,0:T(8,128)(2,1)} %copy-done.5), calls=%async_computation.2 | async-start | bytes 1048576 | tf_op jit(solution)/shard_map/all_to_all | solution.py:295
  97.3 1.1 copy-start.2
  98.4 0.9 copy-start.4

commit v2 on v1

v2 whole, which is shorter than its diff:
```python
import functools

import jax
import jax.numpy as jnp
from jax import lax
from jax.experimental import pallas as pl
from jax.experimental.pallas import tpu as pltpu
from jax.sharding import PartitionSpec as P

HEAD_DIM = 128
TAPS = 4
CHUNK = 128
HALO = 16
EDGE = TAPS - 1
SHARE = 8
FAR = 1 << 30

f32 = jnp.float32
bf16 = jnp.bfloat16


def nt(a, b):
    return lax.dot_general(a, b, (((1,), (1,)), ((), ())), preferred_element_type=f32)


def nn(a, b):
    return lax.dot_general(a, b, (((1,), (0,)), ((), ())), preferred_element_type=f32)


def tn(a, b):
    return lax.dot_general(a, b, (((0,), (0,)), ((), ())), preferred_element_type=f32)


def doc_start(starts, first, pos):
    found = jnp.int32(-FAR)
    for d in range(starts.shape[0]):
        rel = starts[d] - first
        found = jnp.maximum(found, jnp.where(rel <= pos, rel, -FAR))
    return found


def doc_end(starts, first, pos):
    found = jnp.int32(FAR)
    for d in range(starts.shape[0]):
        rel = starts[d] - first
        found = jnp.minimum(found, jnp.where(rel > pos, rel, FAR))
    return found


def row_starts(starts, first, rows):
    found = jnp.full(rows.shape, -FAR, jnp.int32)
    for d in range(starts.shape[0]):
        rel = starts[d] - first
        found = jnp.maximum(found, jnp.where(rows >= rel, rel, -FAR))
    return found


def iota(shape, axis, base=0):
    return lax.broadcasted_iota(jnp.int32, shape, axis) + base


def conv_rows(ext, taps, m, age):
    conv = taps[m, 0:1] * ext
    for j in range(1, TAPS):
        conv = conv + jnp.where(age >= j, taps[m, j : j + 1] * pltpu.roll(ext, j, 0), 0.0)
    return conv


def logistic(x):
    return 1.0 / (1.0 + jnp.exp(-x))


def silu_slope(conv, sigma):
    return sigma * (1.0 + conv * (1.0 - sigma))


def conv_kernel(starts, raw, rim, cot, taps, qkv, message):
    rows = raw.shape[1]
    first = lax.axis_index("seq") * rows
    place = iota((HALO + rows, HEAD_DIM), 0, -HALO)
    age = place - row_starts(starts, first, place)
    made = []
    for m in range(3):
        ext = jnp.concatenate([rim[m], raw[m]], axis=0).astype(f32)
        conv = conv_rows(ext, taps, m, age)[HALO:]
        if m < 2:
            conv = conv * logistic(conv)
        made.append(conv.astype(bf16))
        qkv[m] = made[m]
    last = doc_start(starts, first, rows - 1)
    keep = iota((rows, HEAD_DIM), 0) >= last
    masked_k = jnp.where(keep, made[1], jnp.zeros((), bf16))
    summary = tn(masked_k, made[2])
    tops = [raw[m, :HALO].astype(f32) for m in range(3)] + [cot[...].astype(f32)]
    for n in range(message.shape[0]):
        row = tops[min(n // EDGE, 3)][n % EDGE : n % EDGE + 1]
        part = summary[n * SHARE : (n + 1) * SHARE]
        message[n] = jnp.concatenate([part, jnp.broadcast_to(row, part.shape)], axis=0).astype(bf16)


def slope_kernel(starts, raw, rim, taps, slope):
    rows = raw.shape[1]
    first = lax.axis_index("seq") * rows
    place = iota((HALO + rows, HEAD_DIM), 0, -HALO)
    age = place - row_starts(starts, first, place)
    for m in range(2):
        ext = jnp.concatenate([rim[m], raw[m]], axis=0).astype(f32)
        conv = conv_rows(ext, taps, m, age)[HALO:]
        slope[m] = silu_slope(conv, logistic(conv))


def local_kernel(starts, qkv, local):
    rows = qkv.shape[1]
    first = lax.axis_index("seq") * rows
    for low in range(0, rows, CHUNK):
        high = low + CHUNK
        start = doc_start(starts, first, low)
        scores = nt(qkv[0, low:high], qkv[1, :high])
        t, s = iota((CHUNK, high), 0, low), iota((CHUNK, high), 1)
        scores = jnp.where((s <= t) & (s >= start), scores, 0.0).astype(bf16)
        local[low:high] = nn(scores, qkv[2, :high])


def state_of(message):
    parts = message[...].astype(f32)[:, :SHARE]
    return parts.reshape(HEAD_DIM, HEAD_DIM).astype(bf16)


def normed(attn, gains, cots):
    msq = jnp.mean(attn * attn, axis=-1, keepdims=True)
    scale = lax.rsqrt(jnp.maximum(msq, 1.0))
    scaled = cots * gains
    inner = jnp.mean(scaled * attn, axis=-1, keepdims=True)
    factor = jnp.where(msq > 1.0, scale * scale * scale * inner, 0.0)
    return scale, (scale * scaled - attn * factor).astype(bf16)


def norm_kernel(starts, qkv, local, incoming, cot, gain, attn_out, grad_norm, back):
    rows = local.shape[0]
    first = lax.axis_index("seq") * rows
    prev = row_starts(starts, first, iota((rows, HEAD_DIM), 0)) < 0
    q = qkv[0]
    attn = local[...] + jnp.where(prev, nn(q, state_of(incoming)), 0.0)
    gains = gain[...]
    scale, grad = normed(attn, gains, cot[...].astype(f32))
    attn_out[...] = (attn * scale * gains).astype(bf16)
    grad_norm[...] = grad
    back[...] = tn(jnp.where(prev, q, jnp.zeros((), bf16)), grad)


def conv_back(grad, taps, m, age, rows):
    total = grad.shape[0]
    out = taps[m, 0:1] * grad[:rows]
    for j in range(1, TAPS):
        term = jnp.where(age >= j, taps[m, j : j + 1] * grad, 0.0)
        out = out + pltpu.roll(term, total - j, 0)[:rows]
    return out.astype(bf16)


def query_kernel(
    starts, qkv, grad_norm, slope, incoming, raw_end, taps, gain, attn_out,
    early, edge_qkv, edge_slope, edge_grad,
):
    rows = grad_norm.shape[0]
    total = rows + HALO
    first = lax.axis_index("seq") * rows
    place = iota((total, HEAD_DIM), 0)
    begin = row_starts(starts, first, place)
    age = place - begin
    state = state_of(incoming)
    k, v, g = qkv[1], qkv[2], grad_norm[...]

    line = iota((SHARE, HEAD_DIM), 0)

    def edge(a):
        block = jnp.zeros((SHARE, HEAD_DIM), f32)
        for n in range(EDGE):
            block = jnp.where(line == n, incoming[EDGE * a + n].astype(f32)[SHARE:], block)
        return jnp.concatenate([block, jnp.zeros((HALO - SHARE, HEAD_DIM), f32)], axis=0)

    edges, slopes = [], []
    for m in range(3):
        ext = jnp.concatenate([raw_end[m].astype(f32), edge(m)], axis=0)
        conv = conv_rows(ext, taps, m, age[rows - HALO :])[HALO:]
        if m < 2:
            sigma = logistic(conv)
            slopes.append(silu_slope(conv, sigma))
            conv = conv * sigma
        edges.append(conv.astype(bf16))
        edge_qkv[m] = edges[m]
    edge_slope[...] = slopes[1]
    q_e, k_e, v_e = edges
    start = doc_start(starts, first, rows)
    reach = iota((HALO, rows), 1) >= start
    causal = iota((HALO, HALO), 1) <= iota((HALO, HALO), 0)
    carry = begin[rows:] < 0

    def edge_sums(left, right, right_e, values, values_e, carried):
        scores = jnp.where(reach, nt(left, right), 0.0).astype(bf16)
        scores_e = jnp.where(causal, nt(left, right_e), 0.0).astype(bf16)
        return nn(scores, values) + nn(scores_e, values_e) + jnp.where(carry, carried, 0.0)

    attn_e = edge_sums(q_e, k, k_e, v, v_e, nn(q_e, state))
    _, g_e = normed(attn_e, gain[...], edge(3))
    edge_grad[...] = g_e
    grad_q_e = edge_sums(g_e, v, v_e, k, k_e, nt(g_e, state)) * slopes[0]

    parts = []
    for low in range(0, rows, CHUNK):
        high = low + CHUNK
        start = doc_start(starts, first, low)
        scores = nt(g[low:high], v[:high])
        t, s = iota((CHUNK, high), 0, low), iota((CHUNK, high), 1)
        scores = jnp.where((s <= t) & (s >= start), scores, 0.0).astype(bf16)
        parts.append(nn(scores, k[:high]))
    carried = jnp.where(begin[:rows] < 0, nt(g, state), 0.0)
    grad_q = (jnp.concatenate(parts, axis=0) + carried) * slope[0]
    out = conv_back(jnp.concatenate([grad_q, grad_q_e], axis=0), taps, 0, age, rows)
    shape = (early.shape[0], early.shape[2], HEAD_DIM)
    early[:, 0] = attn_out[...].reshape(shape)
    early[:, 1] = out.reshape(shape)


def key_kernel(starts, qkv, grad_norm, edge_qkv, edge_grad, local_k, local_v):
    rows = grad_norm.shape[0]
    first = lax.axis_index("seq") * rows
    q, k, v, g = qkv[0], qkv[1], qkv[2], grad_norm[...]
    for low in range(0, rows, CHUNK):
        high = low + CHUNK
        end = doc_end(starts, first, low)
        s, t = iota((CHUNK, rows - low), 0, low), iota((CHUNK, rows - low), 1, low)
        keep = (t >= s) & (t < end)
        scores = jnp.where(keep, nt(v[low:high], g[low:]), 0.0).astype(bf16)
        local_k[low:high] = nn(scores, q[low:])
        scores = jnp.where(keep, nt(k[low:high], q[low:]), 0.0).astype(bf16)
        local_v[low:high] = nn(scores, g[low:])
    q_e, k_e, v_e, g_e = edge_qkv[0], edge_qkv[1], edge_qkv[2], edge_grad[...]
    earlier = iota((HALO, HALO), 1) < iota((HALO, HALO), 0)
    scores = jnp.where(earlier, -nt(v_e, g_e), 0.0).astype(bf16)
    local_k[rows:] = nn(scores, q_e)
    scores = jnp.where(earlier, -nt(k_e, q_e), 0.0).astype(bf16)
    local_v[rows:] = nn(scores, g_e)


def last_kernel(
    starts, qkv, edge_qkv, slope, edge_slope, local_k, local_v, future, taps, early, late
):
    total = local_k.shape[0]
    rows = total - HALO
    first = lax.axis_index("seq") * rows
    place = iota((total, HEAD_DIM), 0)
    age = place - row_starts(starts, first, place)
    after = place >= doc_start(starts, first, rows)
    state = future[...].astype(bf16)
    slopes = jnp.concatenate([slope[0], edge_slope[...]], axis=0)
    k = jnp.concatenate([qkv[1], edge_qkv[1]], axis=0)
    v = jnp.concatenate([qkv[2], edge_qkv[2]], axis=0)
    grad_k = (local_k[...] + jnp.where(after, nt(v, state), 0.0)) * slopes
    grad_v = local_v[...] + jnp.where(after, nn(k, state), 0.0)
    shape = (late.shape[0], late.shape[2], HEAD_DIM)
    late[:, 0] = early[:, 0]
    late[:, 1] = early[:, 1]
    late[:, 2] = conv_back(grad_k, taps, 1, age, rows).reshape(shape)
    late[:, 3] = conv_back(grad_v, taps, 2, age, rows).reshape(shape)


def closed(starts, rows, i):
    found = jnp.bool_(False)
    for d in range(starts.shape[0]):
        found = found | ((starts[d] >= i * rows) & (starts[d] < (i + 1) * rows))
    return found


def forward_kernel(rows, starts, sums, out):
    count = sums.shape[0]
    state = jnp.zeros((SHARE, HEAD_DIM), f32)
    for i in range(count):
        here = sums[i].astype(f32)
        edge = sums[min(i + 1, count - 1)].astype(f32)[SHARE:]
        if i == count - 1:
            edge = jnp.zeros_like(edge)
        out[i] = jnp.concatenate([state, edge], axis=0).astype(bf16)
        state = here[:SHARE] + jnp.where(closed(starts, rows, i), 0.0, state)


def backward_kernel(rows, starts, sums, out):
    state = jnp.zeros(sums.shape[1:], f32)
    for i in range(sums.shape[0] - 1, -1, -1):
        out[i] = state
        state = sums[i] + jnp.where(closed(starts, rows, i), 0.0, state)


def gather_kernel(sent, out, grad):
    count, _, _, width = sent.shape
    for i in range(count):
        columns = slice(i * width, (i + 1) * width)
        out[:, columns] = sent[i, 0]
        for m in range(3):
            grad[m, :, columns] = sent[i, m + 1]


def shards(qkv_raw, conv_weight, norm_gain, doc_starts, cotangent):
    rows = qkv_raw.shape[0]
    width = qkv_raw.shape[2]
    heads = width // HEAD_DIM
    total = rows + HALO
    devices = lax.axis_size("seq")
    columns = lax.axis_size("head")
    piece = rows // columns
    share = devices // heads
    raw = qkv_raw.transpose(1, 0, 2)
    gain = norm_gain.reshape(1, width)
    in_hbm = functools.partial(pltpu.with_memory_space_constraint, memory_space=pltpu.HBM)
    doc_starts = pltpu.with_memory_space_constraint(doc_starts, pltpu.SMEM)
    hd = HEAD_DIM

    ahead = [(i, i + 1) for i in range(devices - 1)]
    rim = lax.ppermute(raw[:, rows - HALO :], "seq", ahead)

    smem = pl.BlockSpec(memory_space=pltpu.SMEM)
    params = pltpu.CompilerParams(vmem_limit_bytes=16 * 1024 * 1024)

    def block(shape, axis, **fixed):
        at = {int(name[1:]): index for name, index in fixed.items()}
        return pl.BlockSpec(
            shape, lambda h: tuple(h if a == axis else at.get(a, 0) for a in range(len(shape)))
        )

    def call(body, ins, outs, *args, grid=(heads,)):
        return pl.pallas_call(
            body,
            grid=grid,
            in_specs=[smem] + ins,
            out_specs=[spec for spec, _ in outs],
            out_shape=[shape for _, shape in outs],
            compiler_params=params,
        )(doc_starts, *args)

    def whole(dims, kind):
        return jax.ShapeDtypeStruct(dims, kind)

    spec_qkv = block((3, rows, hd), 2)
    spec_taps = block((3, TAPS, hd), 2)
    spec_rows = block((rows, hd), 1)
    spec_total = block((total, hd), 1)
    spec_state = block((hd, hd), 0)
    spec_message = block((share, 2 * SHARE, hd), 0)
    spec_gain = block((1, hd), 1)

    qkv, message = call(
        conv_kernel,
        [spec_qkv, block((3, HALO, hd), 2), block((HALO, hd), 1), spec_taps],
        [
            (spec_qkv, whole((3, rows, width), bf16)),
            (spec_message, whole((devices, 2 * SHARE, hd), bf16)),
        ],
        in_hbm(raw), rim, in_hbm(cotangent), in_hbm(conv_weight),
    )

    def swap(parts):
        return lax.all_to_all(parts, "seq", 0, 0, tiled=True)

    def scan(body, parts):
        flat = pl.BlockSpec(parts.shape, lambda: (0, 0, 0))
        (found,) = call(
            lambda *refs: body(rows, *refs), [flat], [(flat, whole(parts.shape, parts.dtype))],
            parts, grid=(),
        )
        return found

    (local,) = call(local_kernel, [spec_qkv], [(spec_rows, whole((rows, width), f32))], qkv)
    message, local = lax.optimization_barrier((swap(message), local))
    message = scan(forward_kernel, message)
    (slope,) = call(
        slope_kernel,
        [block((2, rows, hd), 2), block((2, HALO, hd), 2), spec_taps],
        [(block((2, rows, hd), 2), pltpu.HBM((2, rows, width), f32))],
        in_hbm(raw), rim, in_hbm(conv_weight),
    )
    incoming, slope = lax.optimization_barrier((swap(message), slope))
    attn_out, grad_norm, back = call(
        norm_kernel,
        [spec_qkv, spec_rows, spec_message, spec_rows, spec_gain],
        [
            (spec_rows, whole((rows, width), bf16)),
            (spec_rows, whole((rows, width), bf16)),
            (spec_state, whole((heads * hd, hd), f32)),
        ],
        qkv, local, incoming, cotangent, gain,
    )
    early, edge_qkv, edge_slope, edge_grad = call(
        query_kernel,
        [
            spec_qkv, spec_rows, block((1, rows, hd), 2), spec_message,
            block((3, HALO, hd), 2, a1=rows // HALO - 1), spec_taps, spec_gain, spec_rows,
        ],
        [
            (block((columns, 2, piece, hd), 3), whole((columns, 2, piece, width), bf16)),
            (block((3, HALO, hd), 2), whole((3, HALO, width), bf16)),
            (block((HALO, hd), 1), whole((HALO, width), f32)),
            (block((HALO, hd), 1), whole((HALO, width), bf16)),
        ],
        qkv, grad_norm, slope, incoming, in_hbm(raw), in_hbm(conv_weight), in_hbm(gain), attn_out,
    )
    back = swap(back.reshape(devices, SHARE, hd))
    back, early, edge_qkv, edge_slope, edge_grad = lax.optimization_barrier(
        (back, early, edge_qkv, edge_slope, edge_grad)
    )
    back = scan(backward_kernel, back)
    local_k, local_v = call(
        key_kernel,
        [spec_qkv, spec_rows, block((3, HALO, hd), 2), block((HALO, hd), 1)],
        [(spec_total, whole((total, width), f32))] * 2,
        qkv, grad_norm, edge_qkv, edge_grad,
    )
    future, local_k, local_v = lax.optimization_barrier((swap(back), local_k, local_v))
    (sent,) = call(
        last_kernel,
        [
            spec_qkv, block((3, HALO, hd), 2), block((1, rows, hd), 2, a0=1),
            block((HALO, hd), 1), spec_total, spec_total, spec_state, spec_taps,
            block((columns, 2, piece, hd), 3),
        ],
        [(block((columns, 4, piece, hd), 3), whole((columns, 4, piece, width), bf16))],
        qkv, edge_qkv, slope, edge_slope, local_k, local_v, future.reshape(heads * hd, hd),
        in_hbm(conv_weight), early,
    )
    sent = lax.all_to_all(sent, "head", 0, 0, tiled=True)
    out, grad = pl.pallas_call(
        gather_kernel,
        out_shape=[
            whole((piece, columns * width), bf16),
            whole((3, piece, columns * width), bf16),
        ],
        compiler_params=params,
    )(sent)
    return out, grad.transpose(1, 0, 2)


def solution(mesh):
    return jax.shard_map(
        shards,
        mesh=mesh,
        in_specs=(P("seq", None, "head"), P(None, None, "head"), P("head"), P(), P("seq", "head")),
        out_specs=(P(("seq", "head"), None), P(("seq", "head"), None, None)),
        check_vma=False,
    )
```

time: 137 us -> 126 us (0.920)
  blocking collectives: 53.2 us -> 44.8 us
  local copies, waits for them, and re-layouts: 10.8 us -> 2.6 us
  Pallas kernels: 18.1 us -> 25.3 us
  starting transfers between devices: 31.1 us -> 28 us
  waiting for transfers between devices: 21.6 us -> 23.8 us
    all_to_all x3 -> x1, blocking collectives: 53.2 us -> 44.8 us  [shards(): sent = lax.all_to_all(sent, 'head', 0, 0, tiled=True)]
    unnamed x32 -> x12, local copies, waits for them, and re-layouts: 9.37 us -> 1.85 us
    pallas_call x7 -> x9, Pallas kernels: 17.1 us -> 24.2 us  [call(): pl.pallas_call(body, grid=grid, in_specs=[smem] + ins, out_specs=[spec fo...]
    all_to_all x3 -> x4, waiting for transfers between devices: 20.7 us -> 22.9 us  [swap(): return lax.all_to_all(parts, 'seq', 0, 0, tiled=True)]
    all_to_all x3 -> x4, starting transfers between devices: 25.2 us -> 24 us  [swap(): return lax.all_to_all(parts, 'seq', 0, 0, tiled=True)]
  transfers between devices with their start and end apart: 5 -> 5, of which waited for: 4 -> 5; matrix products, arithmetic and copies ran while one was open for 0% -> 0% of each run, Pallas kernels for 7% -> 10%
where the time goes in v2:
time: 126 us; the launch traced here: 125 us
  blocking collectives  44.8 us (36%)
  starting transfers between devices  28 us (22%)
  Pallas kernels  25.3 us (20%)
  waiting for transfers between devices  23.8 us (19%)
  local copies, waits for them, and re-layouts  2.6 us (2%)
    all_to_all x1, blocking collectives, shards(): sent = lax.all_to_all(sent, 'head', 0, 0, tiled=True)  44.8 us
    pallas_call x9, Pallas kernels, call(): pl.pallas_call(body, grid=grid, in_specs=[smem] + ins, out_specs=[spec fo...  24.2 us
    all_to_all x4, starting transfers between devices, swap(): return lax.all_to_all(parts, 'seq', 0, 0, tiled=True)  24 us
    all_to_all x4, waiting for transfers between devices, swap(): return lax.all_to_all(parts, 'seq', 0, 0, tiled=True)  22.9 us
    ppermute x1, starting transfers between devices, shards(): rim = lax.ppermute(raw[:, rows - HALO:], 'seq', ahead)  4.02 us
  transfers between devices with their start and end apart: 5, of which 5 were waited for; matrix products, arithmetic and copies ran while one was open for 0% of the time, Pallas kernels for 10%

profile of v2, /device:TPU:1, one launch (start us, length us, event | category | flops | bytes accessed | tf_op | source)
XLA Modules:
  0.0 125.3 jit_solution(8881388284596369006)
XLA Ops:
  0.6 0.0 copy-start.4
  0.6 0.7 slice.4
  1.4 4.0 %collective-permute-start = (bf16[3,16,256]{2,1,0:T(8,128)(2,1)S(1)}, bf16[3,16,256]{2,1,0:T(8,128)(2,1)S(1)}, u32[]{:S(2)}, u32[]{:S(2)}) collective-permute-start(bf16[3,16,256]{2,1,0:T(8,128)(2,1)S(1)} %slice.4), channel_id=1, source_target_pairs={{0,16},{16,32},{32,48},{48,64},{64,80},{80,96},{96,112},{112,128},... | collective-permute-start | bytes 73736 | tf_op jit(solution)/shard_map/ppermute | solution.py:318
  5.4 0.9 collective-permute-done.rim
  6.3 0.0 copy-done.4
  6.3 3.7 %shard_map.68 = (bf16[3,512,256]{2,1,0:T(8,128)(2,1)S(1)}, bf16[32,16,128]{2,1,0:T(8,128)(2,1)}) custom-call(s32[4]{0:T(128)S(1)} %copy-done.4, bf16[3,512,256]{2,1,0:T(8,128)(2,1)} %bitcast.9, bf16[3,16,256]{2,1,0:T(8,128)(2,1)S(1)} %collective-permute-done.rim, bf16[512,256]{1,0:T(8,128)(2,1)} %cot.3, f32[3,4,256]{2,1,0:T(4,128)} %taps.7), custom_call_target="tpu_custom_call" | custom-call | tf_op jit(solution)/shard_map/pallas_call | solution.py:330
  10.1 11.3 %all-to-all-start = ((bf16[32,16,128]{2,1,0:T(8,128)(2,1)}), bf16[32,16,128]{2,1,0:T(8,128)(2,1)S(1)}, u32[]{:S(2)}, u32[]{:S(2)}) async-start(bf16[32,16,128]{2,1,0:T(8,128)(2,1)} %get-tuple-element.28), calls=%async_computation | async-start | bytes 262144 | tf_op jit(solution)/shard_map/all_to_all | solution.py:361
  21.4 2.2 %shard_map.69.local = f32[512,256]{1,0:T(8,128)S(1)} custom-call(s32[4]{0:T(128)S(1)} %copy-done.4, bf16[3,512,256]{2,1,0:T(8,128)(2,1)S(1)} %get-tuple-element.27.qkv), custom_call_target="tpu_custom_call" | custom-call | tf_op jit(solution)/shard_map/pallas_call | solution.py:330
  23.6 6.9 %all-to-all-done.refs_1_ = bf16[32,16,128]{2,1,0:T(8,128)(2,1)S(1)} async-done(((bf16[32,16,128]{2,1,0:T(8,128)(2,1)}), bf16[32,16,128]{2,1,0:T(8,128)(2,1)S(1)}, u32[]{:S(2)}, u32[]{:S(2)}) %all-to-all-start) | async-done | bytes 131104 | tf_op jit(solution)/shard_map/all_to_all | solution.py:361
  30.6 1.4 %shard_map.70 = bf16[32,16,128]{2,1,0:T(8,128)(2,1)} custom-call(s32[4]{0:T(128)S(1)} %copy-done.4, bf16[32,16,128]{2,1,0:T(8,128)(2,1)S(1)} %all-to-all-done.refs_1_), custom_call_target="tpu_custom_call" | custom-call | tf_op jit(solution)/shard_map/pallas_call | solution.py:330
  31.9 3.9 %all-to-all-start.1 = ((bf16[32,16,128]{2,1,0:T(8,128)(2,1)}), bf16[32,16,128]{2,1,0:T(8,128)(2,1)S(1)}, u32[]{:S(2)}, u32[]{:S(2)}) async-start(bf16[32,16,128]{2,1,0:T(8,128)(2,1)} %shard_map.70), calls=%async_computation.1 | async-start | bytes 262144 | tf_op jit(solution)/shard_map/all_to_all | solution.py:361
  35.8 0.0 copy-start.1
  35.8 0.0 copy-start.5
  35.8 3.2 %shard_map.71.slope = f32[2,512,256]{2,1,0:T(8,128)} custom-call(s32[4]{0:T(128)S(1)} %copy-done.4, bf16[3,512,256]{2,1,0:T(8,128)(2,1)} %bitcast.10, bf16[3,16,256]{2,1,0:T(8,128)(2,1)S(1)} %collective-permute-done.rim, f32[3,4,256]{2,1,0:T(4,128)} %taps.7), custom_call_target="tpu_custom_call" | custom-call | tf_op jit(solution)/shard_map/pallas_call | solution.py:330
  39.1 0.0 copy-start
  39.1 5.9 %all-to-all-done.1.incoming = bf16[32,16,128]{2,1,0:T(8,128)(2,1)S(1)} async-done(((bf16[32,16,128]{2,1,0:T(8,128)(2,1)}), bf16[32,16,128]{2,1,0:T(8,128)(2,1)S(1)}, u32[]{:S(2)}, u32[]{:S(2)}) %all-to-all-start.1) | async-done | bytes 131104 | tf_op jit(solution)/shard_map/all_to_all | solution.py:361
  44.9 0.0 copy-done.1
  44.9 0.0 copy-done.5
  45.0 2.5 %shard_map.72 = (bf16[512,256]{1,0:T(8,128)(2,1)S(1)}, bf16[512,256]{1,0:T(8,128)(2,1)S(1)}, f32[256,128]{1,0:T(8,128)}) custom-call(s32[4]{0:T(128)S(1)} %copy-done.4, bf16[3,512,256]{2,1,0:T(8,128)(2,1)S(1)} %get-tuple-element.27.qkv, f32[512,256]{1,0:T(8,128)S(1)} %shard_map.69.local, bf16[32,16,128]{2,1,0:T(8,128)(2,1)S(1)} %all-to-all-done.1.incoming, ...), custom_call_target="tpu_custom_call" | custom-call | tf_op jit(solution)/shard_map/pallas_call | solution.py:330
  47.5 3.9 %all-to-all-start.2 = ((f32[32,8,128]{2,1,0:T(8,128)}), f32[32,8,128]{2,1,0:T(8,128)S(1)}, u32[]{:S(2)}, u32[]{:S(2)}) async-start(f32[32,8,128]{2,1,0:T(8,128)} %bitcast.2), calls=%async_computation.2 | async-start | bytes 262144 | tf_op jit(solution)/shard_map/all_to_all | solution.py:361
  51.3 0.0 copy-done
  51.3 4.1 %shard_map.73 = (bf16[16,2,32,256]{3,2,1,0:T(8,128)(2,1)S(1)}, bf16[3,16,256]{2,1,0:T(8,128)(2,1)S(1)}, f32[16,256]{1,0:T(8,128)S(1)}, bf16[16,256]{1,0:T(8,128)(2,1)S(1)}) custom-call(s32[4]{0:T(128)S(1)} %copy-done.4, bf16[3,512,256]{2,1,0:T(8,128)(2,1)S(1)} %get-tuple-element.27.qkv, bf16[512,256]{1,0:T(8,128)(2,1)S(1)} %get-tuple-element.33.grad_norm, ...), custom_call_target="tpu_custom_call" | custom-call | tf_op jit(solution)/shard_map/pallas_call | solution.py:330
  55.4 0.0 copy-start.2
  55.4 0.8 copy-done.2
  56.2 4.2 %all-to-all-done.2.refs_1_ = f32[32,8,128]{2,1,0:T(8,128)S(1)} async-done(((f32[32,8,128]{2,1,0:T(8,128)}), f32[32,8,128]{2,1,0:T(8,128)S(1)}, u32[]{:S(2)}, u32[]{:S(2)}) %all-to-all-start.2) | async-done | bytes 131104 | tf_op jit(solution)/shard_map/all_to_all | solution.py:361
  60.5 1.4 %shard_map.74 = f32[32,8,128]{2,1,0:T(8,128)} custom-call(s32[4]{0:T(128)S(1)} %copy-done.4, f32[32,8,128]{2,1,0:T(8,128)S(1)} %all-to-all-done.2.refs_1_), custom_call_target="tpu_custom_call" | custom-call | tf_op jit(solution)/shard_map/pallas_call | solution.py:330
  61.8 5.0 %all-to-all-start.3 = ((f32[32,8,128]{2,1,0:T(8,128)}), f32[32,8,128]{2,1,0:T(8,128)S(1)}, u32[]{:S(2)}, u32[]{:S(2)}) async-start(f32[32,8,128]{2,1,0:T(8,128)} %shard_map.74), calls=%async_computation.3 | async-start | bytes 262144 | tf_op jit(solution)/shard_map/all_to_all | solution.py:361
  66.8 3.3 %shard_map.75 = (f32[528,256]{1,0:T(8,128)S(1)}, f32[528,256]{1,0:T(8,128)S(1)}) custom-call(s32[4]{0:T(128)S(1)} %copy-done.4, bf16[3,512,256]{2,1,0:T(8,128)(2,1)S(1)} %get-tuple-element.27.qkv, bf16[512,256]{1,0:T(8,128)(2,1)S(1)} %get-tuple-element.33.grad_norm, bf16[3,16,256]{2,1,0:T(8,128)(2,1)S(1)} %get-tuple-element.40.edge_qkv, ...), custom_call_target="tpu_custom_call" | custom-call | tf_op jit(solution)/shard_map/pallas_call | solution.py:330
  70.2 5.8 %all-to-all-done.3 = f32[32,8,128]{2,1,0:T(8,128)S(1)} async-done(((f32[32,8,128]{2,1,0:T(8,128)}), f32[32,8,128]{2,1,0:T(8,128)S(1)}, u32[]{:S(2)}, u32[]{:S(2)}) %all-to-all-start.3) | async-done | bytes 131104 | tf_op jit(solution)/shard_map/all_to_all | solution.py:361
  76.0 0.0 copy-start.3
  76.0 1.0 copy-done.3
  77.1 2.4 %shard_map.76 = bf16[16,4,32,256]{3,2,1,0:T(8,128)(2,1)S(1)} custom-call(s32[4]{0:T(128)S(1)} %copy-done.4, bf16[3,512,256]{2,1,0:T(8,128)(2,1)S(1)} %get-tuple-element.27.qkv, bf16[3,16,256]{2,1,0:T(8,128)(2,1)S(1)} %get-tuple-element.40.edge_qkv, f32[2,512,256]{2,1,0:T(8,128)S(1)} %copy-done, f32[16,256]{1,0:T(8,128)S(1)} %get-tuple-element.41.edge_slope, ...), custom_call_target="tpu_custom_call" | custom-call | tf_op jit(solution)/shard_map/pallas_call | solution.py:330
  79.4 44.8 %all_to_all.25.sent = bf16[16,4,32,256]{3,2,1,0:T(8,128)(2,1)S(1)} all-to-all(bf16[16,4,32,256]{3,2,1,0:T(8,128)(2,1)S(1)} %shard_map.76), channel_id=1, replica_groups=mesh['seq'=32,'head'=16] {'head'}, dimensions={0} | all-to-all | bytes 2097152 | tf_op jit(solution)/shard_map/all_to_all | solution.py:428
  124.3 1.1 shard_map.77
Async XLA Ops:
  0.6 5.7 %copy-start.4 = (s32[4]{0:T(128)S(1)}, s32[4]{0:T(128)}, u32[]{:S(2)}) copy-start(s32[4]{0:T(128)} %starts.13) | copy-start | bytes 52
  1.4 5.0 %collective-permute-start = (bf16[3,16,256]{2,1,0:T(8,128)(2,1)S(1)}, bf16[3,16,256]{2,1,0:T(8,128)(2,1)S(1)}, u32[]{:S(2)}, u32[]{:S(2)}) collective-permute-start(bf16[3,16,256]{2,1,0:T(8,128)(2,1)S(1)} %slice.4), channel_id=1, source_target_pairs={{0,16},{16,32},{32,48},{48,64},{64,80},{80,96},{96,112},{112,128},... | collective-permute-start | bytes 73736 | tf_op jit(solution)/shard_map/ppermute | solution.py:318
  10.1 20.5 %all-to-all-start = ((bf16[32,16,128]{2,1,0:T(8,128)(2,1)}), bf16[32,16,128]{2,1,0:T(8,128)(2,1)S(1)}, u32[]{:S(2)}, u32[]{:S(2)}) async-start(bf16[32,16,128]{2,1,0:T(8,128)(2,1)} %get-tuple-element.28), calls=%async_computation | async-start | bytes 262144 | tf_op jit(solution)/shard_map/all_to_all | solution.py:361
  31.9 13.0 %all-to-all-start.1 = ((bf16[32,16,128]{2,1,0:T(8,128)(2,1)}), bf16[32,16,128]{2,1,0:T(8,128)(2,1)S(1)}, u32[]{:S(2)}, u32[]{:S(2)}) async-start(bf16[32,16,128]{2,1,0:T(8,128)(2,1)} %shard_map.70), calls=%async_computation.1 | async-start | bytes 262144 | tf_op jit(solution)/shard_map/all_to_all | solution.py:361
  35.8 9.1 %copy-start.1 = (bf16[512,256]{1,0:T(8,128)(2,1)S(1)}, bf16[512,256]{1,0:T(8,128)(2,1)}, u32[]{:S(2)}) copy-start(bf16[512,256]{1,0:T(8,128)(2,1)} %cot.3) | copy-start | bytes 786436
  35.8 9.1 %copy-start.5 = (f32[256]{0:T(256)S(1)}, f32[256]{0:T(256)}, u32[]{:S(2)}) copy-start(f32[256]{0:T(256)} %param.7) | copy-start | bytes 3076
  39.1 12.3 %copy-start = (f32[2,512,256]{2,1,0:T(8,128)S(1)}, f32[2,512,256]{2,1,0:T(8,128)}, u32[]{:S(2)}) copy-start(f32[2,512,256]{2,1,0:T(8,128)} %shard_map.71.slope) | copy-start | bytes 3145732
  47.5 13.0 %all-to-all-start.2 = ((f32[32,8,128]{2,1,0:T(8,128)}), f32[32,8,128]{2,1,0:T(8,128)S(1)}, u32[]{:S(2)}, u32[]{:S(2)}) async-start(f32[32,8,128]{2,1,0:T(8,128)} %bitcast.2), calls=%async_computation.2 | async-start | bytes 262144 | tf_op jit(solution)/shard_map/all_to_all | solution.py:361
  55.4 0.8 copy-start.2
  61.8 14.2 %all-to-all-start.3 = ((f32[32,8,128]{2,1,0:T(8,128)}), f32[32,8,128]{2,1,0:T(8,128)S(1)}, u32[]{:S(2)}, u32[]{:S(2)}) async-start(f32[32,8,128]{2,1,0:T(8,128)} %shard_map.74), calls=%async_computation.3 | async-start | bytes 262144 | tf_op jit(solution)/shard_map/all_to_all | solution.py:361
  76.0 1.0 copy-start.3

commit v3 on v2

v3 whole, which is shorter than its diff:
```python
import functools

import jax
import jax.numpy as jnp
from jax import lax
from jax.experimental import pallas as pl
from jax.experimental.pallas import tpu as pltpu
from jax.sharding import PartitionSpec as P

HEAD_DIM = 128
TAPS = 4
CHUNK = 128
HALO = 16
EDGE = TAPS - 1
SHARE = 8
FAR = 1 << 30

f32 = jnp.float32
bf16 = jnp.bfloat16


def nt(a, b):
    return lax.dot_general(a, b, (((1,), (1,)), ((), ())), preferred_element_type=f32)


def nn(a, b):
    return lax.dot_general(a, b, (((1,), (0,)), ((), ())), preferred_element_type=f32)


def tn(a, b):
    return lax.dot_general(a, b, (((0,), (0,)), ((), ())), preferred_element_type=f32)


def doc_start(starts, first, pos):
    found = jnp.int32(-FAR)
    for d in range(starts.shape[0]):
        rel = starts[d] - first
        found = jnp.maximum(found, jnp.where(rel <= pos, rel, -FAR))
    return found


def doc_end(starts, first, pos):
    found = jnp.int32(FAR)
    for d in range(starts.shape[0]):
        rel = starts[d] - first
        found = jnp.minimum(found, jnp.where(rel > pos, rel, FAR))
    return found


def row_starts(starts, first, rows):
    found = jnp.full(rows.shape, -FAR, jnp.int32)
    for d in range(starts.shape[0]):
        rel = starts[d] - first
        found = jnp.maximum(found, jnp.where(rows >= rel, rel, -FAR))
    return found


def iota(shape, axis, base=0):
    return lax.broadcasted_iota(jnp.int32, shape, axis) + base


def conv_rows(ext, taps, m, age):
    conv = taps[m, 0:1] * ext
    for j in range(1, TAPS):
        conv = conv + jnp.where(age >= j, taps[m, j : j + 1] * pltpu.roll(ext, j, 0), 0.0)
    return conv


def logistic(x):
    return 1.0 / (1.0 + jnp.exp(-x))


def silu_slope(conv, sigma):
    return sigma * (1.0 + conv * (1.0 - sigma))


def conv_docs(ext, taps, m, starts, first):
    rows = ext.shape[0] - HALO
    conv = taps[m, 0:1] * ext
    for j in range(1, TAPS):
        conv = conv + taps[m, j : j + 1] * pltpu.roll(ext, j, 0)
    parts = []
    for low in range(0, rows, CHUNK):
        top = ext[HALO + low - SHARE : HALO + low + SHARE]
        age = iota((2 * SHARE, HEAD_DIM), 0, low - SHARE) - doc_start(starts, first, low)
        parts.append(conv_rows(top, taps, m, age)[SHARE:])
        parts.append(conv[HALO + low + SHARE : HALO + low + CHUNK])
    return jnp.concatenate(parts, axis=0)


def head_columns(h):
    return slice(h * HEAD_DIM, (h + 1) * HEAD_DIM)


def conv_kernel(
    starts, raw_far, rim, cot_far, taps_far, gain_far,
    keys, values, message, raw_q, raw_end, taps, gain, raw, tops, sems,
):
    _, rows, width = raw.shape
    heads = range(width // HEAD_DIM)
    first = lax.axis_index("seq") * rows
    taps_load = pltpu.make_async_copy(taps_far, taps, sems.at[0])
    loads = [pltpu.make_async_copy(raw_far.at[m], raw.at[m - 1], sems.at[m]) for m in (1, 2)]
    others = [
        pltpu.make_async_copy(raw_far.at[:, pl.ds(0, HALO)], tops.at[pl.ds(0, 3)], sems.at[3]),
        pltpu.make_async_copy(cot_far.at[pl.ds(0, HALO)], tops.at[3], sems.at[4]),
        pltpu.make_async_copy(raw_far.at[:, pl.ds(rows - HALO, HALO)], raw_end, sems.at[5]),
        pltpu.make_async_copy(raw_far.at[0], raw_q, sems.at[6]),
        pltpu.make_async_copy(gain_far, gain, sems.at[7]),
    ]
    for load in [loads[0], taps_load, loads[1]] + others:
        load.start()
    taps_load.wait()
    keep = iota((rows, HEAD_DIM), 0) >= doc_start(starts, first, rows - 1)
    made = {}
    for m, out in ((1, keys), (2, values)):
        loads[m - 1].wait()
        for h in heads:
            at = head_columns(h)
            ext = jnp.concatenate([rim[m, :, at], raw[m - 1, :, at]], axis=0).astype(f32)
            conv = conv_docs(ext, taps.at[:, :, at], m, starts, first)
            if m == 1:
                conv = conv * logistic(conv)
            made[m, h] = conv.astype(bf16)
            out[:, at] = made[m, h]
    for load in others:
        load.wait()
    share = HEAD_DIM // SHARE
    for h in heads:
        at = head_columns(h)
        summary = tn(jnp.where(keep, made[1, h], jnp.zeros((), bf16)), made[2, h])
        for n in range(share):
            row = tops[min(n // EDGE, 3), :, at].astype(f32)[n % EDGE : n % EDGE + 1]
            part = summary[n * SHARE : (n + 1) * SHARE]
            both = jnp.concatenate([part, jnp.broadcast_to(row, part.shape)], axis=0)
            message[h * share + n] = both.astype(bf16)


def slope_kernel(starts, raw_far, rim, taps, slope_q, slope_k, raw, sems):
    _, rows, width = raw.shape
    first = lax.axis_index("seq") * rows
    loads = [pltpu.make_async_copy(raw_far.at[m], raw.at[m], sems.at[m]) for m in range(2)]
    for load in loads:
        load.start()
    for m, out in ((0, slope_q), (1, slope_k)):
        loads[m].wait()
        for h in range(width // HEAD_DIM):
            at = head_columns(h)
            ext = jnp.concatenate([rim[m, :, at], raw[m, :, at]], axis=0).astype(f32)
            conv = conv_docs(ext, taps.at[:, :, at], m, starts, first)
            out[:, at] = silu_slope(conv, logistic(conv))


def local_kernel(starts, raw_q, rim, taps, keys, values, queries, local):
    rows, width = local.shape
    first = lax.axis_index("seq") * rows
    for h in range(width // HEAD_DIM):
        at = head_columns(h)
        ext = jnp.concatenate([rim[0, :, at], raw_q[:, at]], axis=0).astype(f32)
        conv = conv_docs(ext, taps.at[:, :, at], 0, starts, first)
        q = (conv * logistic(conv)).astype(bf16)
        queries[:, at] = q
        for low in range(0, rows, CHUNK):
            high = low + CHUNK
            start = doc_start(starts, first, low)
            scores = nt(q[low:high], keys[:high, at])
            t, s = iota((CHUNK, high), 0, low), iota((CHUNK, high), 1)
            scores = jnp.where((s <= t) & (s >= start), scores, 0.0).astype(bf16)
            local[low:high, at] = nn(scores, values[:high, at])


def state_of(message):
    return message.astype(f32)[:, :SHARE].reshape(HEAD_DIM, HEAD_DIM).astype(bf16)


def normed(attn, gains, cots):
    msq = jnp.mean(attn * attn, axis=-1, keepdims=True)
    scale = lax.rsqrt(jnp.maximum(msq, 1.0))
    scaled = cots * gains
    inner = jnp.mean(scaled * attn, axis=-1, keepdims=True)
    factor = jnp.where(msq > 1.0, scale * scale * scale * inner, 0.0)
    return scale, (scale * scaled - attn * factor).astype(bf16)


def norm_kernel(
    starts, queries, local, incoming, cot, gain, attn_out, grad_norm, back
):
    rows, width = local.shape
    heads = range(width // HEAD_DIM)
    share = HEAD_DIM // SHARE
    first = lax.axis_index("seq") * rows
    prev = row_starts(starts, first, iota((rows, HEAD_DIM), 0)) < 0
    attns = []
    for h in heads:
        at = head_columns(h)
        carried = nn(queries[:, at], state_of(incoming[h * share : (h + 1) * share]))
        attns.append(local[:, at] + jnp.where(prev, carried, 0.0))
    for h in heads:
        at = head_columns(h)
        scale, grad = normed(attns[h], gain[:, at], cot[:, at].astype(f32))
        out = (attns[h] * scale * gain[:, at]).astype(bf16)
        attn_out[:, :, at] = out.reshape(attn_out.shape[:2] + (HEAD_DIM,))
        grad_norm[:, at] = grad
        masked_q = jnp.where(prev, queries[:, at], jnp.zeros((), bf16))
        back[h * HEAD_DIM : (h + 1) * HEAD_DIM] = tn(masked_q, grad).astype(bf16)


def conv_back(grad, taps, m, starts, first, rows):
    total = grad.shape[0]
    out = taps[m, 0:1] * grad[:rows]
    for j in range(1, TAPS):
        out = out + pltpu.roll(taps[m, j : j + 1] * grad, total - j, 0)[:rows]
    parts = []
    for high in range(CHUNK, rows + 1, CHUNK):
        near = grad[high - SHARE : high + SHARE]
        age = iota((2 * SHARE, HEAD_DIM), 0, high - SHARE)
        age = age - row_starts(starts, first, age)
        end = taps[m, 0:1] * near[:SHARE]
        for j in range(1, TAPS):
            term = jnp.where(age >= j, taps[m, j : j + 1] * near, 0.0)
            end = end + pltpu.roll(term, 2 * SHARE - j, 0)[:SHARE]
        parts.append(out[high - CHUNK : high - SHARE])
        parts.append(end)
    return jnp.concatenate(parts, axis=0).astype(bf16)


def edge_rows(incoming, a):
    line = iota((SHARE, HEAD_DIM), 0)
    block = jnp.zeros((SHARE, HEAD_DIM), f32)
    for n in range(EDGE):
        block = jnp.where(line == n, incoming[EDGE * a + n].astype(f32)[SHARE:], block)
    return jnp.concatenate([block, jnp.zeros((HALO - SHARE, HEAD_DIM), f32)], axis=0)


def query_kernel(
    starts, keys, values, grad_norm, slope, incoming, raw_end, taps, gain, attn_out,
    early, edge_qkv, edge_slope, edge_grad, out_rows, sems,
):
    rows, width = grad_norm.shape
    heads = range(width // HEAD_DIM)
    share = HEAD_DIM // SHARE
    first = lax.axis_index("seq") * rows
    stores = [pltpu.make_async_copy(attn_out, early.at[:, 0], sems.at[0])]
    stores[0].start()
    carry = row_starts(starts, first, iota((rows, HEAD_DIM), 0)) < 0
    start = doc_start(starts, first, rows)
    edge_age = iota((2 * HALO, HEAD_DIM), 0, rows - HALO)
    edge_age = edge_age - row_starts(starts, first, edge_age)
    reach = iota((HALO, rows), 1) >= start
    causal = iota((HALO, HALO), 1) <= iota((HALO, HALO), 0)
    for h in heads:
        at = head_columns(h)
        heard = incoming.at[pl.ds(h * share, share)]
        state = state_of(heard[...])
        k, v, g = keys[:, at], values[:, at], grad_norm[:, at]
        edges, slopes = [], []
        for m in range(3):
            ext = jnp.concatenate([raw_end[m, :, at].astype(f32), edge_rows(heard, m)], axis=0)
            conv = conv_rows(ext, taps.at[:, :, at], m, edge_age)[HALO:]
            if m < 2:
                sigma = logistic(conv)
                slopes.append(silu_slope(conv, sigma))
                conv = conv * sigma
            edges.append(conv.astype(bf16))
            edge_qkv[m, :, at] = edges[m]
        edge_slope[:, at] = slopes[1]
        q_e, k_e, v_e = edges

        def edge_sums(left, right, right_e, values, values_e, carried):
            scores = jnp.where(reach, nt(left, right), 0.0).astype(bf16)
            scores_e = jnp.where(causal, nt(left, right_e), 0.0).astype(bf16)
            added = jnp.where(start < 0, carried, 0.0)
            return nn(scores, values) + nn(scores_e, values_e) + added

        attn_e = edge_sums(q_e, k, k_e, v, v_e, nn(q_e, state))
        _, g_e = normed(attn_e, gain[:, at], edge_rows(heard, 3))
        edge_grad[:, at] = g_e
        grad_q_e = edge_sums(g_e, v, v_e, k, k_e, nt(g_e, state)) * slopes[0]

        parts = []
        for low in range(0, rows, CHUNK):
            high = low + CHUNK
            begin = doc_start(starts, first, low)
            scores = nt(g[low:high], v[:high])
            t, s = iota((CHUNK, high), 0, low), iota((CHUNK, high), 1)
            scores = jnp.where((s <= t) & (s >= begin), scores, 0.0).astype(bf16)
            parts.append(nn(scores, k[:high]))
        carried = jnp.where(carry, nt(g, state), 0.0)
        grad_q = (jnp.concatenate(parts, axis=0) + carried) * slope[:, at]
        both = jnp.concatenate([grad_q, grad_q_e], axis=0)
        out = conv_back(both, taps.at[:, :, at], 0, starts, first, rows)
        out_rows[:, :, at] = out.reshape(out_rows.shape[:2] + (HEAD_DIM,))
        lanes = pl.ds(h * HEAD_DIM, HEAD_DIM)
        part = out_rows.at[:, :, lanes]
        stores.append(pltpu.make_async_copy(part, early.at[:, 1, :, lanes], sems.at[h + 1]))
        stores[-1].start()
    for store in stores:
        store.wait()


def key_kernel(starts, queries, keys, values, grad_norm, edge_qkv, edge_grad, local_k, local_v):
    rows, width = grad_norm.shape
    first = lax.axis_index("seq") * rows
    for h in range(width // HEAD_DIM):
        at = head_columns(h)
        q, k, v, g = queries[:, at], keys[:, at], values[:, at], grad_norm[:, at]
        for low in range(0, rows, CHUNK):
            high = low + CHUNK
            end = doc_end(starts, first, low)
            s, t = iota((CHUNK, rows - low), 0, low), iota((CHUNK, rows - low), 1, low)
            keep = (t >= s) & (t < end)
            scores = jnp.where(keep, nt(v[low:high], g[low:]), 0.0).astype(bf16)
            local_k[low:high, at] = nn(scores, q[low:])
            scores = jnp.where(keep, nt(k[low:high], q[low:]), 0.0).astype(bf16)
            local_v[low:high, at] = nn(scores, g[low:])
        q_e, k_e, v_e = edge_qkv[0, :, at], edge_qkv[1, :, at], edge_qkv[2, :, at]
        g_e = edge_grad[:, at]
        earlier = iota((HALO, HALO), 1) < iota((HALO, HALO), 0)
        scores = jnp.where(earlier, -nt(v_e, g_e), 0.0).astype(bf16)
        local_k[rows:, at] = nn(scores, q_e)
        scores = jnp.where(earlier, -nt(k_e, q_e), 0.0).astype(bf16)
        local_v[rows:, at] = nn(scores, g_e)


def last_kernel(
    starts, keys, values, edge_qkv, slope, edge_slope, local_k, local_v, future, taps, early,
    sent, sem,
):
    total, width = local_k.shape
    rows = total - HALO
    first = lax.axis_index("seq") * rows
    copy = pltpu.make_async_copy(early, sent.at[:, pl.ds(0, 2)], sem)
    copy.start()
    after = iota((total, HEAD_DIM), 0) >= doc_start(starts, first, rows)
    shape = (sent.shape[0], sent.shape[2], HEAD_DIM)
    for h in range(width // HEAD_DIM):
        at = head_columns(h)
        state = future[h * HEAD_DIM : (h + 1) * HEAD_DIM]
        k = jnp.concatenate([keys[:, at], edge_qkv[1, :, at]], axis=0)
        v = jnp.concatenate([values[:, at], edge_qkv[2, :, at]], axis=0)
        slopes = jnp.concatenate([slope[:, at], edge_slope[:, at]], axis=0)
        grad_k = (local_k[:, at] + jnp.where(after, nt(v, state), 0.0)) * slopes
        grad_v = local_v[:, at] + jnp.where(after, nn(k, state), 0.0)
        for m, grad in ((1, grad_k), (2, grad_v)):
            out = conv_back(grad, taps.at[:, :, at], m, starts, first, rows)
            sent[:, m + 1, :, at] = out.reshape(shape)
    copy.wait()


def closed(starts, rows, i):
    found = jnp.bool_(False)
    for d in range(starts.shape[0]):
        found = found | ((starts[d] >= i * rows) & (starts[d] < (i + 1) * rows))
    return found


def forward_kernel(rows, starts, sums, out):
    count = sums.shape[0]
    state = jnp.zeros((SHARE, HEAD_DIM), f32)
    for i in range(count):
        here = sums[i].astype(f32)
        edge = sums[min(i + 1, count - 1)].astype(f32)[SHARE:]
        if i == count - 1:
            edge = jnp.zeros_like(edge)
        out[i] = jnp.concatenate([state, edge], axis=0).astype(bf16)
        state = here[:SHARE] + jnp.where(closed(starts, rows, i), 0.0, state)


def backward_kernel(rows, starts, sums, out):
    count = 2 * sums.shape[0]
    state = jnp.zeros((SHARE, HEAD_DIM), f32)
    for i in range(count - 1, 0, -2):
        pair = sums[i // 2].astype(f32)
        upper = state
        state = pair[SHARE:] + jnp.where(closed(starts, rows, i), 0.0, state)
        out[i // 2] = jnp.concatenate([state, upper], axis=0).astype(bf16)
        state = pair[:SHARE] + jnp.where(closed(starts, rows, i - 1), 0.0, state)


def gather_kernel(sent, out, grad):
    count, _, _, width = sent.shape
    for i in range(count):
        columns = slice(i * width, (i + 1) * width)
        out[:, columns] = sent[i, 0]
        for m in range(3):
            grad[m, :, columns] = sent[i, m + 1]


def shards(qkv_raw, conv_weight, norm_gain, doc_starts, cotangent):
    rows = qkv_raw.shape[0]
    width = qkv_raw.shape[2]
    heads = width // HEAD_DIM
    total = rows + HALO
    devices = lax.axis_size("seq")
    columns = lax.axis_size("head")
    piece = rows // columns
    share = devices // heads
    raw = qkv_raw.transpose(1, 0, 2)
    in_hbm = functools.partial(pltpu.with_memory_space_constraint, memory_space=pltpu.HBM)
    doc_starts = pltpu.with_memory_space_constraint(doc_starts, pltpu.SMEM)
    hd = HEAD_DIM

    ahead = [(i, i + 1) for i in range(devices - 1)]
    rim = lax.ppermute(raw[:, rows - HALO :], "seq", ahead)

    smem = pl.BlockSpec(memory_space=pltpu.SMEM)
    params = pltpu.CompilerParams(vmem_limit_bytes=16 * 1024 * 1024)

    vmem = pl.BlockSpec(memory_space=pltpu.VMEM)
    hbm = pl.BlockSpec(memory_space=pltpu.HBM)
    dma = pltpu.SemaphoreType.DMA

    def flat_call(body, ins, outs, scratch, *args, alias={}):
        return pl.pallas_call(
            body,
            in_specs=[smem] + ins,
            out_specs=[hbm if out.memory_space == pltpu.HBM else vmem for out in outs],
            out_shape=outs,
            scratch_shapes=scratch,
            input_output_aliases=alias,
            compiler_params=params,
        )(doc_starts, *[in_hbm(a) if spec is hbm else a for a, spec in zip(args, ins)])

    wide = pltpu.VMEM((rows, width), bf16)
    keys, values, message, raw_q, raw_end, taps, gain = flat_call(
        conv_kernel,
        [hbm, vmem, hbm, hbm, hbm],
        [
            wide, wide, pltpu.VMEM((devices, 2 * SHARE, hd), bf16), wide,
            pltpu.VMEM((3, HALO, width), bf16), pltpu.VMEM(conv_weight.shape, f32),
            pltpu.VMEM((1, width), f32),
        ],
        [pltpu.VMEM((2, rows, width), bf16), pltpu.VMEM((4, HALO, width), bf16), dma((8,))],
        raw, rim, cotangent, conv_weight, norm_gain.reshape(1, width),
    )

    def swap(parts):
        return lax.all_to_all(parts, "seq", 0, 0, tiled=True)

    def scan(body, parts):
        (found,) = flat_call(
            functools.partial(body, rows), [vmem], [pltpu.VMEM(parts.shape, bf16)], [], parts
        )
        return found

    queries, local = flat_call(
        local_kernel, [vmem] * 5, [wide, pltpu.VMEM((rows, width), f32)], [],
        raw_q, rim, taps, keys, values,
    )
    message, queries, local = lax.optimization_barrier((swap(message), queries, local))
    message = scan(forward_kernel, message)
    slope_q, slope_k = flat_call(
        slope_kernel, [hbm, vmem, vmem], [pltpu.VMEM((rows, width), f32)] * 2,
        [pltpu.VMEM((2, rows, width), bf16), dma((2,))],
        raw, rim, taps,
    )
    incoming, slope_q, slope_k = lax.optimization_barrier((swap(message), slope_q, slope_k))
    attn_out, grad_norm, back = flat_call(
        norm_kernel,
        [vmem] * 5,
        [
            pltpu.VMEM((columns, piece, width), bf16), pltpu.VMEM((rows, width), bf16),
            pltpu.VMEM((heads * hd, hd), bf16),
        ],
        [],
        queries, local, incoming, cotangent, gain,
    )
    early, edge_qkv, edge_slope, edge_grad = flat_call(
        query_kernel,
        [vmem] * 9,
        [
            pltpu.HBM((columns, 2, piece, width), bf16), pltpu.VMEM((3, HALO, width), bf16),
            pltpu.VMEM((HALO, width), f32), pltpu.VMEM((HALO, width), bf16),
        ],
        [pltpu.VMEM((columns, piece, width), bf16), dma((heads + 1,))],
        keys, values, grad_norm, slope_q, incoming, raw_end, taps, gain, attn_out,
    )
    back = swap(back.reshape(devices, SHARE, hd))
    back, early, edge_qkv, edge_slope, edge_grad = lax.optimization_barrier(
        (back, early, edge_qkv, edge_slope, edge_grad)
    )
    back = scan(backward_kernel, back.reshape(devices // 2, 2 * SHARE, hd))
    local_k, local_v = flat_call(
        key_kernel, [vmem] * 6, [pltpu.VMEM((total, width), f32)] * 2, [],
        queries, keys, values, grad_norm, edge_qkv, edge_grad,
    )
    future, local_k, local_v = lax.optimization_barrier((swap(back.reshape(devices, SHARE, hd)), local_k, local_v))
    (sent,) = flat_call(
        last_kernel, [vmem] * 9 + [hbm], [pltpu.VMEM((columns, 4, piece, width), bf16)], [dma(())],
        keys, values, edge_qkv, slope_k, edge_slope, local_k, local_v,
        future.reshape(heads * hd, hd), taps, early,
    )
    sent = lax.all_to_all(sent, "head", 0, 0, tiled=True)
    out, grad = pl.pallas_call(
        gather_kernel,
        out_shape=[
            jax.ShapeDtypeStruct((piece, columns * width), bf16),
            jax.ShapeDtypeStruct((3, piece, columns * width), bf16),
        ],
        compiler_params=params,
    )(sent)
    return out, grad.transpose(1, 0, 2)


def solution(mesh):
    return jax.shard_map(
        shards,
        mesh=mesh,
        in_specs=(P("seq", None, "head"), P(None, None, "head"), P("head"), P(), P("seq", "head")),
        out_specs=(P(("seq", "head"), None), P(("seq", "head"), None, None)),
        check_vma=False,
    )
```

time: 126 us -> 122 us (0.968)
  Pallas kernels: 25.3 us -> 21.9 us
  local copies, waits for them, and re-layouts: 2.6 us -> 0.76 us
  waiting for transfers between devices: 23.8 us -> 25.6 us
    pallas_call x10, Pallas kernels: 25.3 us -> 21.9 us  [the longest x9 20.8 us: flat_call(): pl.pallas_call(body, in_specs=[smem] + ins, out_specs=[hbm if out.memory_...]
    unnamed x12 -> x4, local copies, waits for them, and re-layouts: 1.85 us -> 0.01 us
    all_to_all x4, waiting for transfers between devices: 22.9 us -> 24.7 us  [swap(): return lax.all_to_all(parts, 'seq', 0, 0, tiled=True)]
  transfers between devices with their start and end apart: 5 -> 5, of which waited for: 5 -> 5; matrix products, arithmetic and copies ran while one was open for 0% -> 0% of each run, Pallas kernels for 10% -> 9%
where the time goes in v3:
time: 122 us
  blocking collectives  44.9 us (37%)
  starting transfers between devices  27.8 us (23%)
  waiting for transfers between devices  25.6 us (21%)
  Pallas kernels  21.9 us (18%)
    all_to_all x1, blocking collectives, shards(): sent = lax.all_to_all(sent, 'head', 0, 0, tiled=True)  44.9 us
    all_to_all x4, waiting for transfers between devices, swap(): return lax.all_to_all(parts, 'seq', 0, 0, tiled=True)  24.7 us
    all_to_all x4, starting transfers between devices, swap(): return lax.all_to_all(parts, 'seq', 0, 0, tiled=True)  23.6 us
    pallas_call x9, Pallas kernels, flat_call(): pl.pallas_call(body, in_specs=[smem] + ins, out_specs=[hbm if out.memory_...  20.8 us
    ppermute x1, starting transfers between devices, shards(): rim = lax.ppermute(raw[:, rows - HALO:], 'seq', ahead)  4.15 us
  transfers between devices with their start and end apart: 5, of which 5 were waited for; matrix products, arithmetic and copies ran while one was open for 0% of the time, Pallas kernels for 9%

profile of v3, /device:TPU:1, one launch (start us, length us, event | category | flops | bytes accessed | tf_op | source)
XLA Modules:
  0.0 121.6 jit_solution(11308289806501460368)
XLA Ops:
  0.6 0.7 slice.4
  1.4 0.0 copy-start.1
  1.4 4.2 %collective-permute-start = (bf16[3,16,256]{2,1,0:T(8,128)(2,1)S(1)}, bf16[3,16,256]{2,1,0:T(8,128)(2,1)S(1)}, u32[]{:S(2)}, u32[]{:S(2)}) collective-permute-start(bf16[3,16,256]{2,1,0:T(8,128)(2,1)S(1)} %slice.4), channel_id=1, source_target_pairs={{0,16},{16,32},{32,48},{48,64},{64,80},{80,96},{96,112},{112,128},... | collective-permute-start | bytes 73736 | tf_op jit(solution)/shard_map/ppermute | solution.py:404
  5.5 0.9 collective-permute-done.rim
  6.5 0.0 copy-done.1
  6.5 3.2 %shard_map.68 = (bf16[512,256]{1,0:T(8,128)(2,1)S(1)}, bf16[512,256]{1,0:T(8,128)(2,1)S(1)}, bf16[32,16,128]{2,1,0:T(8,128)(2,1)}, bf16[512,256]{1,0:T(8,128)(2,...) custom-call(s32[4]{0:T(128)S(1)} %copy-done.1, ...), custom_call_target="tpu_custom_call" | custom-call | tf_op jit(solution)/shard_map/pallas_call | solution.py:414
  9.6 11.3 %all-to-all-start = ((bf16[32,16,128]{2,1,0:T(8,128)(2,1)}), bf16[32,16,128]{2,1,0:T(8,128)(2,1)S(1)}, u32[]{:S(2)}, u32[]{:S(2)}) async-start(bf16[32,16,128]{2,1,0:T(8,128)(2,1)} %get-tuple-element.40), calls=%async_computation | async-start | bytes 262144 | tf_op jit(solution)/shard_map/all_to_all | solution.py:438
  21.0 1.8 %shard_map.69 = (bf16[512,256]{1,0:T(8,128)(2,1)S(1)}, f32[512,256]{1,0:T(8,128)S(1)}) custom-call(s32[4]{0:T(128)S(1)} %copy-done.1, bf16[512,256]{1,0:T(8,128)(2,1)S(1)} %get-tuple-element.41.raw_q, bf16[3,16,256]{2,1,0:T(8,128)(2,1)S(1)} %collective-permute-done.rim, f32[3,4,256]{2,1,0:T(4,128)S(1)} %get-tuple-element.42.taps, ...), custom_call_target="tpu_custom_call" | custom-call | tf_op jit(solution)/shard_map/pallas_call | solution.py:414
  22.8 7.3 %all-to-all-done.sums = bf16[32,16,128]{2,1,0:T(8,128)(2,1)S(1)} async-done(((bf16[32,16,128]{2,1,0:T(8,128)(2,1)}), bf16[32,16,128]{2,1,0:T(8,128)(2,1)S(1)}, u32[]{:S(2)}, u32[]{:S(2)}) %all-to-all-start) | async-done | bytes 131104 | tf_op jit(solution)/shard_map/all_to_all | solution.py:438
  30.1 1.4 %shard_map.70 = bf16[32,16,128]{2,1,0:T(8,128)(2,1)} custom-call(s32[4]{0:T(128)S(1)} %copy-done.1, bf16[32,16,128]{2,1,0:T(8,128)(2,1)S(1)} %all-to-all-done.sums), custom_call_target="tpu_custom_call" | custom-call | tf_op jit(solution)/shard_map/pallas_call | solution.py:414
  31.5 3.9 %all-to-all-start.1 = ((bf16[32,16,128]{2,1,0:T(8,128)(2,1)}), bf16[32,16,128]{2,1,0:T(8,128)(2,1)S(1)}, u32[]{:S(2)}, u32[]{:S(2)}) async-start(bf16[32,16,128]{2,1,0:T(8,128)(2,1)} %shard_map.70), calls=%async_computation.1 | async-start | bytes 262144 | tf_op jit(solution)/shard_map/all_to_all | solution.py:438
  35.4 0.0 copy-start
  35.4 2.3 %shard_map.71 = (f32[512,256]{1,0:T(8,128)S(1)}, f32[512,256]{1,0:T(8,128)S(1)}) custom-call(s32[4]{0:T(128)S(1)} %copy-done.1, bf16[3,512,256]{2,1,0:T(8,128)(2,1)} %bitcast.11, bf16[3,16,256]{2,1,0:T(8,128)(2,1)S(1)} %collective-permute-done.rim, f32[3,4,256]{2,1,0:T(4,128)S(1)} %get-tuple-element.42.taps), custom_call_target="tpu_custom_call" | custom-call | tf_op jit(solution)/shard_map/pallas_call | solution.py:414
  37.7 6.8 %all-to-all-done.1.incoming = bf16[32,16,128]{2,1,0:T(8,128)(2,1)S(1)} async-done(((bf16[32,16,128]{2,1,0:T(8,128)(2,1)}), bf16[32,16,128]{2,1,0:T(8,128)(2,1)S(1)}, u32[]{:S(2)}, u32[]{:S(2)}) %all-to-all-start.1) | async-done | bytes 131104 | tf_op jit(solution)/shard_map/all_to_all | solution.py:438
  44.5 0.0 copy-done
  44.5 2.0 %shard_map.72 = (bf16[16,32,256]{2,1,0:T(8,128)(2,1)S(1)}, bf16[512,256]{1,0:T(8,128)(2,1)S(1)}, bf16[256,128]{1,0:T(8,128)(2,1)}) custom-call(s32[4]{0:T(128)S(1)} %copy-done.1, bf16[512,256]{1,0:T(8,128)(2,1)S(1)} %get-tuple-element.45.queries, f32[512,256]{1,0:T(8,128)S(1)} %get-tuple-element.46.local, bf16[32,16,128]{2,1,0:T(8,128)(2,1)S(1)} %all-to-all-done.1.incoming, ...), custom_call_target="tpu_custom_call" | custom-call | tf_op jit(solution)/shard_map/pallas_call | solution.py:414
  46.6 3.9 %all-to-all-start.2 = ((bf16[32,8,128]{2,1,0:T(8,128)(2,1)}), bf16[32,8,128]{2,1,0:T(8,128)(2,1)S(1)}, u32[]{:S(2)}, u32[]{:S(2)}) async-start(bf16[32,8,128]{2,1,0:T(8,128)(2,1)} %bitcast.2), calls=%async_computation.2 | async-start | bytes 131072 | tf_op jit(solution)/shard_map/all_to_all | solution.py:438
  50.4 4.2 %shard_map.73 = (bf16[16,2,32,256]{3,2,1,0:T(8,128)(2,1)}, bf16[3,16,256]{2,1,0:T(8,128)(2,1)S(1)}, f32[16,256]{1,0:T(8,128)S(1)}, bf16[16,256]{1,0:T(8,128)(2,1)S(1)}) custom-call(s32[4]{0:T(128)S(1)} %copy-done.1, bf16[512,256]{1,0:T(8,128)(2,1)S(1)} %get-tuple-element.38.keys, bf16[512,256]{1,0:T(8,128)(2,1)S(1)} %get-tuple-element.39.values, ...), custom_call_target="tpu_custom_call" | custom-call | tf_op jit(solution)/shard_map/pallas_call | solution.py:414
  54.7 4.6 %all-to-all-done.2 = bf16[32,8,128]{2,1,0:T(8,128)(2,1)S(1)} async-done(((bf16[32,8,128]{2,1,0:T(8,128)(2,1)}), bf16[32,8,128]{2,1,0:T(8,128)(2,1)S(1)}, u32[]{:S(2)}, u32[]{:S(2)}) %all-to-all-start.2) | async-done | bytes 65568 | tf_op jit(solution)/shard_map/all_to_all | solution.py:438
  59.3 1.3 %shard_map.74 = bf16[16,16,128]{2,1,0:T(8,128)(2,1)} custom-call(s32[4]{0:T(128)S(1)} %copy-done.1, bf16[16,16,128]{2,1,0:T(8,128)(2,1)S(1)} %bitcast.8), custom_call_target="tpu_custom_call" | custom-call | tf_op jit(solution)/shard_map/pallas_call | solution.py:414
  60.6 4.6 %all-to-all-start.3 = ((bf16[32,8,128]{2,1,0:T(8,128)(2,1)}), bf16[32,8,128]{2,1,0:T(8,128)(2,1)S(1)}, u32[]{:S(2)}, u32[]{:S(2)}) async-start(bf16[32,8,128]{2,1,0:T(8,128)(2,1)} %bitcast.4), calls=%async_computation.3 | async-start | bytes 131072 | tf_op jit(solution)/shard_map/all_to_all | solution.py:438
  65.2 2.9 %shard_map.75 = (f32[528,256]{1,0:T(8,128)S(1)}, f32[528,256]{1,0:T(8,128)S(1)}) custom-call(s32[4]{0:T(128)S(1)} %copy-done.1, bf16[512,256]{1,0:T(8,128)(2,1)S(1)} %get-tuple-element.45.queries, bf16[512,256]{1,0:T(8,128)(2,1)S(1)} %get-tuple-element.38.keys, bf16[512,256]{1,0:T(8,128)(2,1)S(1)} %get-tuple-element.39.values, ...), custom_call_target="tpu_custom_call" | custom-call | tf_op jit(solution)/shard_map/pallas_call | solution.py:414
  68.1 6.0 %all-to-all-done.3 = bf16[32,8,128]{2,1,0:T(8,128)(2,1)S(1)} async-done(((bf16[32,8,128]{2,1,0:T(8,128)(2,1)}), bf16[32,8,128]{2,1,0:T(8,128)(2,1)S(1)}, u32[]{:S(2)}, u32[]{:S(2)}) %all-to-all-start.3) | async-done | bytes 65568 | tf_op jit(solution)/shard_map/all_to_all | solution.py:438
  74.1 1.6 %shard_map.76 = bf16[16,4,32,256]{3,2,1,0:T(8,128)(2,1)S(1)} custom-call(s32[4]{0:T(128)S(1)} %copy-done.1, bf16[512,256]{1,0:T(8,128)(2,1)S(1)} %get-tuple-element.38.keys, bf16[512,256]{1,0:T(8,128)(2,1)S(1)} %get-tuple-element.39.values, bf16[3,16,256]{2,1,0:T(8,128)(2,1)S(1)} %get-tuple-element.61.edge_qkv, f32[512,256]{1,0:T(8,128)S(1)} %get-tuple-element.62.slope, ...), custom_call_target="tpu_custom_call" | custom-call | tf_op jit(solution)/shard_map/pallas_call | solution.py:414
  75.7 44.9 %all_to_all.25.sent = bf16[16,4,32,256]{3,2,1,0:T(8,128)(2,1)S(1)} all-to-all(bf16[16,4,32,256]{3,2,1,0:T(8,128)(2,1)S(1)} %shard_map.76), channel_id=1, replica_groups=mesh['seq'=32,'head'=16] {'head'}, dimensions={0} | all-to-all | bytes 2097152 | tf_op jit(solution)/shard_map/all_to_all | solution.py:493
  120.6 1.1 shard_map.77
Async XLA Ops:
  1.4 5.1 %copy-start.1 = (s32[4]{0:T(128)S(1)}, s32[4]{0:T(128)}, u32[]{:S(2)}) copy-start(s32[4]{0:T(128)} %starts.17) | copy-start | bytes 52
  1.4 5.1 %collective-permute-start = (bf16[3,16,256]{2,1,0:T(8,128)(2,1)S(1)}, bf16[3,16,256]{2,1,0:T(8,128)(2,1)S(1)}, u32[]{:S(2)}, u32[]{:S(2)}) collective-permute-start(bf16[3,16,256]{2,1,0:T(8,128)(2,1)S(1)} %slice.4), channel_id=1, source_target_pairs={{0,16},{16,32},{32,48},{48,64},{64,80},{80,96},{96,112},{112,128},... | collective-permute-start | bytes 73736 | tf_op jit(solution)/shard_map/ppermute | solution.py:404
  9.6 20.5 %all-to-all-start = ((bf16[32,16,128]{2,1,0:T(8,128)(2,1)}), bf16[32,16,128]{2,1,0:T(8,128)(2,1)S(1)}, u32[]{:S(2)}, u32[]{:S(2)}) async-start(bf16[32,16,128]{2,1,0:T(8,128)(2,1)} %get-tuple-element.40), calls=%async_computation | async-start | bytes 262144 | tf_op jit(solution)/shard_map/all_to_all | solution.py:438
  31.5 13.0 %all-to-all-start.1 = ((bf16[32,16,128]{2,1,0:T(8,128)(2,1)}), bf16[32,16,128]{2,1,0:T(8,128)(2,1)S(1)}, u32[]{:S(2)}, u32[]{:S(2)}) async-start(bf16[32,16,128]{2,1,0:T(8,128)(2,1)} %shard_map.70), calls=%async_computation.1 | async-start | bytes 262144 | tf_op jit(solution)/shard_map/all_to_all | solution.py:438
  35.4 9.1 %copy-start = (bf16[512,256]{1,0:T(8,128)(2,1)S(1)}, bf16[512,256]{1,0:T(8,128)(2,1)}, u32[]{:S(2)}) copy-start(bf16[512,256]{1,0:T(8,128)(2,1)} %cot.1) | copy-start | bytes 786436
  46.6 12.7 %all-to-all-start.2 = ((bf16[32,8,128]{2,1,0:T(8,128)(2,1)}), bf16[32,8,128]{2,1,0:T(8,128)(2,1)S(1)}, u32[]{:S(2)}, u32[]{:S(2)}) async-start(bf16[32,8,128]{2,1,0:T(8,128)(2,1)} %bitcast.2), calls=%async_computation.2 | async-start | bytes 131072 | tf_op jit(solution)/shard_map/all_to_all | solution.py:438
  60.6 13.5 %all-to-all-start.3 = ((bf16[32,8,128]{2,1,0:T(8,128)(2,1)}), bf16[32,8,128]{2,1,0:T(8,128)(2,1)S(1)}, u32[]{:S(2)}, u32[]{:S(2)}) async-start(bf16[32,8,128]{2,1,0:T(8,128)(2,1)} %bitcast.4), calls=%async_computation.3 | async-start | bytes 131072 | tf_op jit(solution)/shard_map/all_to_all | solution.py:438

commit v4 on v3

--- a/solution.py
+++ b/solution.py
@@ -92,39 +92,38 @@
     return slice(h * HEAD_DIM, (h + 1) * HEAD_DIM)
 
 
-def conv_kernel(
-    starts, raw_far, rim, cot_far, taps_far, gain_far,
-    keys, values, message, raw_q, raw_end, taps, gain, raw, tops, sems,
-):
+def fetch_kernel(starts, raw_far, cot_far, taps_far, gain_far, raw, raw_end, tops, taps, gain, sems):
+    rows = raw.shape[1]
+    loads = [
+        (raw_far, raw),
+        (raw_far.at[:, pl.ds(rows - HALO, HALO)], raw_end),
+        (raw_far.at[:, pl.ds(0, HALO)], tops.at[pl.ds(0, 3)]),
+        (cot_far.at[pl.ds(0, HALO)], tops.at[3]),
+        (taps_far, taps),
+        (gain_far, gain),
+    ]
+    loads = [pltpu.make_async_copy(*ends, sems.at[n]) for n, ends in enumerate(loads)]
+    for load in loads:
+        load.start()
+    for load in loads:
+        load.wait()
+
+
+def conv_kernel(starts, raw, rim, tops, taps, keys, values, message):
     _, rows, width = raw.shape
     heads = range(width // HEAD_DIM)
     first = lax.axis_index("seq") * rows
-    taps_load = pltpu.make_async_copy(taps_far, taps, sems.at[0])
-    loads = [pltpu.make_async_copy(raw_far.at[m], raw.at[m - 1], sems.at[m]) for m in (1, 2)]
-    others = [
-        pltpu.make_async_copy(raw_far.at[:, pl.ds(0, HALO)], tops.at[pl.ds(0, 3)], sems.at[3]),
-        pltpu.make_async_copy(cot_far.at[pl.ds(0, HALO)], tops.at[3], sems.at[4]),
-        pltpu.make_async_copy(raw_far.at[:, pl.ds(rows - HALO, HALO)], raw_end, sems.at[5]),
-        pltpu.make_async_copy(raw_far.at[0], raw_q, sems.at[6]),
-        pltpu.make_async_copy(gain_far, gain, sems.at[7]),
-    ]
-    for load in [loads[0], taps_load, loads[1]] + others:
-        load.start()
-    taps_load.wait()
     keep = iota((rows, HEAD_DIM), 0) >= doc_start(starts, first, rows - 1)
     made = {}
     for m, out in ((1, keys), (2, values)):
-        loads[m - 1].wait()
         for h in heads:
             at = head_columns(h)
-            ext = jnp.concatenate([rim[m, :, at], raw[m - 1, :, at]], axis=0).astype(f32)
+            ext = jnp.concatenate([rim[m, :, at], raw[m, :, at]], axis=0).astype(f32)
             conv = conv_docs(ext, taps.at[:, :, at], m, starts, first)
             if m == 1:
                 conv = conv * logistic(conv)
             made[m, h] = conv.astype(bf16)
             out[:, at] = made[m, h]
-    for load in others:
-        load.wait()
     share = HEAD_DIM // SHARE
     for h in heads:
         at = head_columns(h)
@@ -136,14 +135,10 @@
             message[h * share + n] = both.astype(bf16)
 
 
-def slope_kernel(starts, raw_far, rim, taps, slope_q, slope_k, raw, sems):
+def slope_kernel(starts, raw, rim, taps, slope_q, slope_k):
     _, rows, width = raw.shape
     first = lax.axis_index("seq") * rows
-    loads = [pltpu.make_async_copy(raw_far.at[m], raw.at[m], sems.at[m]) for m in range(2)]
-    for load in loads:
-        load.start()
     for m, out in ((0, slope_q), (1, slope_k)):
-        loads[m].wait()
         for h in range(width // HEAD_DIM):
             at = head_columns(h)
             ext = jnp.concatenate([rim[m, :, at], raw[m, :, at]], axis=0).astype(f32)
@@ -151,12 +146,12 @@
             out[:, at] = silu_slope(conv, logistic(conv))
 
 
-def local_kernel(starts, raw_q, rim, taps, keys, values, queries, local):
+def local_kernel(starts, raw, rim, taps, keys, values, queries, local):
     rows, width = local.shape
     first = lax.axis_index("seq") * rows
     for h in range(width // HEAD_DIM):
         at = head_columns(h)
-        ext = jnp.concatenate([rim[0, :, at], raw_q[:, at]], axis=0).astype(f32)
+        ext = jnp.concatenate([rim[0, :, at], raw[0, :, at]], axis=0).astype(f32)
         conv = conv_docs(ext, taps.at[:, :, at], 0, starts, first)
         q = (conv * logistic(conv)).astype(bf16)
         queries[:, at] = q
@@ -234,14 +229,14 @@
 
 def query_kernel(
     starts, keys, values, grad_norm, slope, incoming, raw_end, taps, gain, attn_out,
-    early, edge_qkv, edge_slope, edge_grad, out_rows, sems,
+    early, edge_qkv, edge_slope, edge_grad, sem,
 ):
     rows, width = grad_norm.shape
     heads = range(width // HEAD_DIM)
     share = HEAD_DIM // SHARE
     first = lax.axis_index("seq") * rows
-    stores = [pltpu.make_async_copy(attn_out, early.at[:, 0], sems.at[0])]
-    stores[0].start()
+    copy = pltpu.make_async_copy(attn_out, early.at[:, 0], sem)
+    copy.start()
     carry = row_starts(starts, first, iota((rows, HEAD_DIM), 0)) < 0
     start = doc_start(starts, first, rows)
     edge_age = iota((2 * HALO, HEAD_DIM), 0, rows - HALO)
@@ -289,13 +284,8 @@
         grad_q = (jnp.concatenate(parts, axis=0) + carried) * slope[:, at]
         both = jnp.concatenate([grad_q, grad_q_e], axis=0)
         out = conv_back(both, taps.at[:, :, at], 0, starts, first, rows)
-        out_rows[:, :, at] = out.reshape(out_rows.shape[:2] + (HEAD_DIM,))
-        lanes = pl.ds(h * HEAD_DIM, HEAD_DIM)
-        part = out_rows.at[:, :, lanes]
-        stores.append(pltpu.make_async_copy(part, early.at[:, 1, :, lanes], sems.at[h + 1]))
-        stores[-1].start()
-    for store in stores:
-        store.wait()
+        early[:, 1, :, at] = out.reshape((early.shape[0], early.shape[2], HEAD_DIM))
+    copy.wait()
 
 
 def key_kernel(starts, queries, keys, values, grad_norm, edge_qkv, edge_grad, local_k, local_v):
@@ -310,16 +300,16 @@
             s, t = iota((CHUNK, rows - low), 0, low), iota((CHUNK, rows - low), 1, low)
             keep = (t >= s) & (t < end)
             scores = jnp.where(keep, nt(v[low:high], g[low:]), 0.0).astype(bf16)
-            local_k[low:high, at] = nn(scores, q[low:])
+            local_k[low:high, at] = nn(scores, q[low:]).astype(bf16)
             scores = jnp.where(keep, nt(k[low:high], q[low:]), 0.0).astype(bf16)
-            local_v[low:high, at] = nn(scores, g[low:])
+            local_v[low:high, at] = nn(scores, g[low:]).astype(bf16)
         q_e, k_e, v_e = edge_qkv[0, :, at], edge_qkv[1, :, at], edge_qkv[2, :, at]
         g_e = edge_grad[:, at]
         earlier = iota((HALO, HALO), 1) < iota((HALO, HALO), 0)
         scores = jnp.where(earlier, -nt(v_e, g_e), 0.0).astype(bf16)
-        local_k[rows:, at] = nn(scores, q_e)
+        local_k[rows:, at] = nn(scores, q_e).astype(bf16)
         scores = jnp.where(earlier, -nt(k_e, q_e), 0.0).astype(bf16)
-        local_v[rows:, at] = nn(scores, g_e)
+        local_v[rows:, at] = nn(scores, g_e).astype(bf16)
 
 
 def last_kernel(
@@ -333,15 +323,17 @@
     copy.start()
     after = iota((total, HEAD_DIM), 0) >= doc_start(starts, first, rows)
     shape = (sent.shape[0], sent.shape[2], HEAD_DIM)
-    for h in range(width // HEAD_DIM):
-        at = head_columns(h)
-        state = future[h * HEAD_DIM : (h + 1) * HEAD_DIM]
-        k = jnp.concatenate([keys[:, at], edge_qkv[1, :, at]], axis=0)
-        v = jnp.concatenate([values[:, at], edge_qkv[2, :, at]], axis=0)
-        slopes = jnp.concatenate([slope[:, at], edge_slope[:, at]], axis=0)
-        grad_k = (local_k[:, at] + jnp.where(after, nt(v, state), 0.0)) * slopes
-        grad_v = local_v[:, at] + jnp.where(after, nn(k, state), 0.0)
-        for m, grad in ((1, grad_k), (2, grad_v)):
+    for m in (2, 1):
+        for h in range(width // HEAD_DIM):
+            at = head_columns(h)
+            state = future[h * HEAD_DIM : (h + 1) * HEAD_DIM]
+            if m == 2:
+                k = jnp.concatenate([keys[:, at], edge_qkv[1, :, at]], axis=0)
+                grad = local_v[:, at].astype(f32) + jnp.where(after, nn(k, state), 0.0)
+            else:
+                v = jnp.concatenate([values[:, at], edge_qkv[2, :, at]], axis=0)
+                slopes = jnp.concatenate([slope[:, at], edge_slope[:, at]], axis=0)
+                grad = (local_k[:, at].astype(f32) + jnp.where(after, nt(v, state), 0.0)) * slopes
             out = conv_back(grad, taps.at[:, :, at], m, starts, first, rows)
             sent[:, m + 1, :, at] = out.reshape(shape)
     copy.wait()
@@ -422,16 +414,25 @@
         )(doc_starts, *[in_hbm(a) if spec is hbm else a for a, spec in zip(args, ins)])
 
     wide = pltpu.VMEM((rows, width), bf16)
-    keys, values, message, raw_q, raw_end, taps, gain = flat_call(
-        conv_kernel,
-        [hbm, vmem, hbm, hbm, hbm],
+    fetched = flat_call(
+        fetch_kernel,
+        [hbm] * 4,
         [
-            wide, wide, pltpu.VMEM((devices, 2 * SHARE, hd), bf16), wide,
-            pltpu.VMEM((3, HALO, width), bf16), pltpu.VMEM(conv_weight.shape, f32),
+            pltpu.VMEM(raw.shape, bf16), pltpu.VMEM((3, HALO, width), bf16),
+            pltpu.VMEM((4, HALO, width), bf16), pltpu.VMEM(conv_weight.shape, f32),
             pltpu.VMEM((1, width), f32),
         ],
-        [pltpu.VMEM((2, rows, width), bf16), pltpu.VMEM((4, HALO, width), bf16), dma((8,))],
-        raw, rim, cotangent, conv_weight, norm_gain.reshape(1, width),
+        [dma((6,))],
+        raw, cotangent, conv_weight, norm_gain.reshape(1, width),
+    )
+    rim, fetched = lax.optimization_barrier((rim, fetched))
+    near, raw_end, tops, taps, gain = fetched
+    keys, values, message = flat_call(
+        conv_kernel,
+        [vmem] * 4,
+        [wide, wide, pltpu.VMEM((devices, 2 * SHARE, hd), bf16)],
+        [],
+        near, rim, tops, taps,
     )
 
     def swap(parts):
@@ -445,16 +446,17 @@
 
     queries, local = flat_call(
         local_kernel, [vmem] * 5, [wide, pltpu.VMEM((rows, width), f32)], [],
-        raw_q, rim, taps, keys, values,
-    )
-    message, queries, local = lax.optimization_barrier((swap(message), queries, local))
+        near, rim, taps, keys, values,
+    )
+    slope_q, slope_k = flat_call(
+        slope_kernel, [vmem] * 3, [pltpu.VMEM((rows, width), f32)] * 2, [],
+        near, rim, taps,
+    )
+    message, queries, local, slope_q, slope_k = lax.optimization_barrier(
+        (swap(message), queries, local, slope_q, slope_k)
+    )
     message = scan(forward_kernel, message)
-    slope_q, slope_k = flat_call(
-        slope_kernel, [hbm, vmem, vmem], [pltpu.VMEM((rows, width), f32)] * 2,
-        [pltpu.VMEM((2, rows, width), bf16), dma((2,))],
-        raw, rim, taps,
-    )
-    incoming, slope_q, slope_k = lax.optimization_barrier((swap(message), slope_q, slope_k))
+    incoming = swap(message)
     attn_out, grad_norm, back = flat_call(
         norm_kernel,
         [vmem] * 5,
@@ -469,10 +471,10 @@
         query_kernel,
         [vmem] * 9,
         [
-            pltpu.HBM((columns, 2, piece, width), bf16), pltpu.VMEM((3, HALO, width), bf16),
+            pltpu.VMEM((columns, 2, piece, width), bf16), pltpu.VMEM((3, HALO, width), bf16),
             pltpu.VMEM((HALO, width), f32), pltpu.VMEM((HALO, width), bf16),
         ],
-        [pltpu.VMEM((columns, piece, width), bf16), dma((heads + 1,))],
+        [dma(())],
         keys, values, grad_norm, slope_q, incoming, raw_end, taps, gain, attn_out,
     )
     back = swap(back.reshape(devices, SHARE, hd))
@@ -481,12 +483,12 @@
     )
     back = scan(backward_kernel, back.reshape(devices // 2, 2 * SHARE, hd))
     local_k, local_v = flat_call(
-        key_kernel, [vmem] * 6, [pltpu.VMEM((total, width), f32)] * 2, [],
+        key_kernel, [vmem] * 6, [pltpu.VMEM((total, width), bf16)] * 2, [],
         queries, keys, values, grad_norm, edge_qkv, edge_grad,
     )
     future, local_k, local_v = lax.optimization_barrier((swap(back.reshape(devices, SHARE, hd)), local_k, local_v))
     (sent,) = flat_call(
-        last_kernel, [vmem] * 9 + [hbm], [pltpu.VMEM((columns, 4, piece, width), bf16)], [dma(())],
+        last_kernel, [vmem] * 10, [pltpu.VMEM((columns, 4, piece, width), bf16)], [dma(())],
         keys, values, edge_qkv, slope_k, edge_slope, local_k, local_v,
         future.reshape(heads * hd, hd), taps, early,
     )

time: 122 us -> 120 us (0.984)
  blocking collectives: 44.9 us -> 58.2 us
  waiting for transfers between devices: 25.6 us -> 17.6 us
  starting transfers between devices: 27.8 us -> 21.9 us
  Pallas kernels: 21.9 us -> 19.8 us
    all_to_all x0 -> x1, blocking collectives: none -> 12.8 us  [swap(): return lax.all_to_all(parts, 'seq', 0, 0, tiled=True)]
    all_to_all x4 -> x3, waiting for transfers between devices: 24.7 us -> 17.6 us  [swap(): return lax.all_to_all(parts, 'seq', 0, 0, tiled=True)]
    all_to_all x4 -> x3, starting transfers between devices: 23.6 us -> 17.7 us  [swap(): return lax.all_to_all(parts, 'seq', 0, 0, tiled=True)]
    pallas_call x9 -> x10, Pallas kernels: 20.8 us -> 18.7 us  [flat_call(): pl.pallas_call(body, in_specs=[smem] + ins, out_specs=[hbm if out.memory_...]
  transfers between devices with their start and end apart: 5 -> 4, of which waited for: 5 -> 3; matrix products, arithmetic and copies ran while one was open for 0% -> 0% of each run, Pallas kernels for 9% -> 9%
where the time goes in v4:
time: 120 us; the launch traced here: 119 us
  blocking collectives  58.2 us (48%)
  starting transfers between devices  21.9 us (18%)
  Pallas kernels  19.8 us (16%)
  waiting for transfers between devices  17.6 us (15%)
  local copies, waits for them, and re-layouts  1.35 us (1%)
    all_to_all x1, blocking collectives, shards(): sent = lax.all_to_all(sent, 'head', 0, 0, tiled=True)  45.4 us
    pallas_call x10, Pallas kernels, flat_call(): pl.pallas_call(body, in_specs=[smem] + ins, out_specs=[hbm if out.memory_...  18.7 us
    all_to_all x3, starting transfers between devices, swap(): return lax.all_to_all(parts, 'seq', 0, 0, tiled=True)  17.7 us
    all_to_all x3, waiting for transfers between devices, swap(): return lax.all_to_all(parts, 'seq', 0, 0, tiled=True)  17.6 us
    all_to_all x1, blocking collectives, swap(): return lax.all_to_all(parts, 'seq', 0, 0, tiled=True)  12.8 us
    ppermute x1, starting transfers between devices, shards(): rim = lax.ppermute(raw[:, rows - HALO:], 'seq', ahead)  4.15 us
  transfers between devices with their start and end apart: 4, of which 3 were waited for; matrix products, arithmetic and copies ran while one was open for 0% of the time, Pallas kernels for 9%

profile of v4, /device:TPU:1, one launch (start us, length us, event | category | flops | bytes accessed | tf_op | source)
XLA Modules:
  0.0 119.5 jit_solution(1080902797097067594)
XLA Ops:
  0.6 0.7 slice.4
  1.4 0.0 copy-start.1
  1.4 4.2 %collective-permute-start = (bf16[3,16,256]{2,1,0:T(8,128)(2,1)S(1)}, bf16[3,16,256]{2,1,0:T(8,128)(2,1)S(1)}, u32[]{:S(2)}, u32[]{:S(2)}) collective-permute-start(bf16[3,16,256]{2,1,0:T(8,128)(2,1)S(1)} %slice.4), channel_id=1, source_target_pairs={{0,16},{16,32},{32,48},{48,64},{64,80},{80,96},{96,112},{112,128},... | collective-permute-start | bytes 73736 | tf_op jit(solution)/shard_map/ppermute | solution.py:396
  5.5 0.0 copy-done.1
  5.5 1.7 %shard_map.68 = (bf16[3,512,256]{2,1,0:T(8,128)(2,1)S(1)}, bf16[3,16,256]{2,1,0:T(8,128)(2,1)S(1)}, bf16[4,16,256]{2,1,0:T(8,128)(2,1)S(1)}, f32[3,4,256]{2,1,0:T(4,128)S(1)}, f32[1,256]{1,0:T(1,128)S(1)}) custom-call(s32[4]{0:T(128)S(1)} %copy-done.1, bf16[3,512,256]{2,1,0:T(8,128)(2,1)} %bitcast.10, bf16[512,256]{1,0:T(8,128)(2,1)} %cot.1, ...), custom_call_target="tpu_custom_call" | custom-call | tf_op jit(solution)/shard_map/pallas_call | solution.py:406
  7.3 0.0 copy-start.4
  7.3 0.6 copy-done.4
  7.9 0.0 copy-start.2
  7.9 0.0 collective-permute-done.rim
  7.9 2.1 %shard_map.69 = (bf16[512,256]{1,0:T(8,128)(2,1)S(1)}, bf16[512,256]{1,0:T(8,128)(2,1)S(1)}, bf16[32,16,128]{2,1,0:T(8,128)(2,1)}) custom-call(s32[4]{0:T(128)S(1)} %copy-done.1, bf16[3,512,256]{2,1,0:T(8,128)(2,1)S(1)} %get-tuple-element.49.raw, bf16[3,16,256]{2,1,0:T(8,128)(2,1)S(1)} %collective-permute-done.rim, ...), custom_call_target="tpu_custom_call" | custom-call | tf_op jit(solution)/shard_map/pallas_call | solution.py:406
  10.0 0.0 copy-done.2
  10.0 9.9 %all-to-all-start = ((bf16[32,16,128]{2,1,0:T(8,128)(2,1)}), bf16[32,16,128]{2,1,0:T(8,128)(2,1)S(1)}, u32[]{:S(2)}, u32[]{:S(2)}) async-start(bf16[32,16,128]{2,1,0:T(8,128)(2,1)} %get-tuple-element.55), calls=%async_computation | async-start | bytes 262144 | tf_op jit(solution)/shard_map/all_to_all | solution.py:439
  19.9 1.4 %shard_map.71 = (f32[512,256]{1,0:T(8,128)S(1)}, f32[512,256]{1,0:T(8,128)S(1)}) custom-call(s32[4]{0:T(128)S(1)} %copy-done.1, bf16[3,512,256]{2,1,0:T(8,128)(2,1)S(1)} %get-tuple-element.49.raw, bf16[3,16,256]{2,1,0:T(8,128)(2,1)S(1)} %collective-permute-done.rim, f32[3,4,256]{2,1,0:T(4,128)S(1)} %get-tuple-element.52.taps), custom_call_target="tpu_custom_call" | custom-call | tf_op jit(solution)/shard_map/pallas_call | solution.py:406
  21.3 1.8 %shard_map.70 = (bf16[512,256]{1,0:T(8,128)(2,1)S(1)}, f32[512,256]{1,0:T(8,128)S(1)}) custom-call(s32[4]{0:T(128)S(1)} %copy-done.1, bf16[3,512,256]{2,1,0:T(8,128)(2,1)S(1)} %get-tuple-element.49.raw, bf16[3,16,256]{2,1,0:T(8,128)(2,1)S(1)} %collective-permute-done.rim, f32[3,4,256]{2,1,0:T(4,128)S(1)} %get-tuple-element.52.taps, ...), custom_call_target="tpu_custom_call" | custom-call | tf_op jit(solution)/shard_map/pallas_call | solution.py:406
  23.1 6.0 %all-to-all-done.sums = bf16[32,16,128]{2,1,0:T(8,128)(2,1)S(1)} async-done(((bf16[32,16,128]{2,1,0:T(8,128)(2,1)}), bf16[32,16,128]{2,1,0:T(8,128)(2,1)S(1)}, u32[]{:S(2)}, u32[]{:S(2)}) %all-to-all-start) | async-done | bytes 131104 | tf_op jit(solution)/shard_map/all_to_all | solution.py:439
  29.0 0.0 copy-start
  29.0 0.7 shard_map.72
  29.8 0.0 copy-start.5
  29.8 12.8 %all_to_all.25.incoming = bf16[32,16,128]{2,1,0:T(8,128)(2,1)S(1)} all-to-all(bf16[32,16,128]{2,1,0:T(8,128)(2,1)S(1)} %shard_map.72), channel_id=1, replica_groups=mesh['seq'=32,'head'=16] {'seq'}, dimensions={0} | all-to-all | bytes 262144 | tf_op jit(solution)/shard_map/all_to_all | solution.py:439
  42.5 0.0 copy-done
  42.5 0.0 copy-done.5
  42.5 2.0 %shard_map.73 = (bf16[16,32,256]{2,1,0:T(8,128)(2,1)S(1)}, bf16[512,256]{1,0:T(8,128)(2,1)S(1)}, bf16[256,128]{1,0:T(8,128)(2,1)}) custom-call(s32[4]{0:T(128)S(1)} %copy-done.1, bf16[512,256]{1,0:T(8,128)(2,1)S(1)} %get-tuple-element.60.queries, f32[512,256]{1,0:T(8,128)S(1)} %get-tuple-element.61.local, bf16[32,16,128]{2,1,0:T(8,128)(2,1)S(1)} %all_to_all.25.incoming, ...), custom_call_target="tpu_custom_call" | custom-call | tf_op jit(solution)/shard_map/pallas_call | solution.py:406
  44.6 0.0 copy-start.3
  44.6 4.0 %all-to-all-start.2 = ((bf16[32,8,128]{2,1,0:T(8,128)(2,1)}), bf16[32,8,128]{2,1,0:T(8,128)(2,1)S(1)}, u32[]{:S(2)}, u32[]{:S(2)}) async-start(bf16[32,8,128]{2,1,0:T(8,128)(2,1)} %bitcast.2), calls=%async_computation.2 | async-start | bytes 131072 | tf_op jit(solution)/shard_map/all_to_all | solution.py:439
  48.6 0.0 copy-done.3
  48.6 3.2 %shard_map.74 = (bf16[16,2,32,256]{3,2,1,0:T(8,128)(2,1)S(1)}, bf16[3,16,256]{2,1,0:T(8,128)(2,1)S(1)}, f32[16,256]{1,0:T(8,128)S(1)}, bf16[16,256]{1,0:T(8,128)(2,1)S(1)}) custom-call(s32[4]{0:T(128)S(1)} %copy-done.1, bf16[512,256]{1,0:T(8,128)(2,1)S(1)} %get-tuple-element.53.keys, bf16[512,256]{1,0:T(8,128)(2,1)S(1)} %get-tuple-element.54.values, ...), custom_call_target="tpu_custom_call" | custom-call | tf_op jit(solution)/shard_map/pallas_call | solution.py:406
  51.8 5.7 %all-to-all-done.2 = bf16[32,8,128]{2,1,0:T(8,128)(2,1)S(1)} async-done(((bf16[32,8,128]{2,1,0:T(8,128)(2,1)}), bf16[32,8,128]{2,1,0:T(8,128)(2,1)S(1)}, u32[]{:S(2)}, u32[]{:S(2)}) %all-to-all-start.2) | async-done | bytes 65568 | tf_op jit(solution)/shard_map/all_to_all | solution.py:439
  57.4 1.3 %shard_map.75 = bf16[16,16,128]{2,1,0:T(8,128)(2,1)} custom-call(s32[4]{0:T(128)S(1)} %copy-done.1, bf16[16,16,128]{2,1,0:T(8,128)(2,1)S(1)} %bitcast.8), custom_call_target="tpu_custom_call" | custom-call | tf_op jit(solution)/shard_map/pallas_call | solution.py:406
  58.8 3.9 %all-to-all-start.3 = ((bf16[32,8,128]{2,1,0:T(8,128)(2,1)}), bf16[32,8,128]{2,1,0:T(8,128)(2,1)S(1)}, u32[]{:S(2)}, u32[]{:S(2)}) async-start(bf16[32,8,128]{2,1,0:T(8,128)(2,1)} %bitcast.4), calls=%async_computation.3 | async-start | bytes 131072 | tf_op jit(solution)/shard_map/all_to_all | solution.py:439
  62.6 2.9 %shard_map.76 = (bf16[528,256]{1,0:T(8,128)(2,1)S(1)}, bf16[528,256]{1,0:T(8,128)(2,1)S(1)}) custom-call(s32[4]{0:T(128)S(1)} %copy-done.1, bf16[512,256]{1,0:T(8,128)(2,1)S(1)} %get-tuple-element.60.queries, bf16[512,256]{1,0:T(8,128)(2,1)S(1)} %get-tuple-element.53.keys, bf16[512,256]{1,0:T(8,128)(2,1)S(1)} %get-tuple-element.54.values, ...), custom_call_target="tpu_custom_call" | custom-call | tf_op jit(solution)/shard_map/pallas_call | solution.py:406
  65.5 6.0 %all-to-all-done.3 = bf16[32,8,128]{2,1,0:T(8,128)(2,1)S(1)} async-done(((bf16[32,8,128]{2,1,0:T(8,128)(2,1)}), bf16[32,8,128]{2,1,0:T(8,128)(2,1)S(1)}, u32[]{:S(2)}, u32[]{:S(2)}) %all-to-all-start.3) | async-done | bytes 65568 | tf_op jit(solution)/shard_map/all_to_all | solution.py:439
  71.5 1.5 %shard_map.77 = bf16[16,4,32,256]{3,2,1,0:T(8,128)(2,1)S(1)} custom-call(s32[4]{0:T(128)S(1)} %copy-done.1, bf16[512,256]{1,0:T(8,128)(2,1)S(1)} %get-tuple-element.53.keys, bf16[512,256]{1,0:T(8,128)(2,1)S(1)} %get-tuple-element.54.values, bf16[3,16,256]{2,1,0:T(8,128)(2,1)S(1)} %get-tuple-element.73.edge_qkv, f32[512,256]{1,0:T(8,128)S(1)} %get-tuple-element.74.slope, ...), custom_call_target="tpu_custom_call" | custom-call | tf_op jit(solution)/shard_map/pallas_call | solution.py:406
  73.0 45.4 %all_to_all.26.sent = bf16[16,4,32,256]{3,2,1,0:T(8,128)(2,1)S(1)} all-to-all(bf16[16,4,32,256]{3,2,1,0:T(8,128)(2,1)S(1)} %shard_map.77), channel_id=1, replica_groups=mesh['seq'=32,'head'=16] {'head'}, dimensions={0} | all-to-all | bytes 2097152 | tf_op jit(solution)/shard_map/all_to_all | solution.py:495
  118.4 1.1 shard_map.78
Async XLA Ops:
  1.4 4.2 %copy-start.1 = (s32[4]{0:T(128)S(1)}, s32[4]{0:T(128)}, u32[]{:S(2)}) copy-start(s32[4]{0:T(128)} %starts.19) | copy-start | bytes 52
  1.4 6.5 %collective-permute-start = (bf16[3,16,256]{2,1,0:T(8,128)(2,1)S(1)}, bf16[3,16,256]{2,1,0:T(8,128)(2,1)S(1)}, u32[]{:S(2)}, u32[]{:S(2)}) collective-permute-start(bf16[3,16,256]{2,1,0:T(8,128)(2,1)S(1)} %slice.4), channel_id=1, source_target_pairs={{0,16},{16,32},{32,48},{48,64},{64,80},{80,96},{96,112},{112,128},... | collective-permute-start | bytes 73736 | tf_op jit(solution)/shard_map/ppermute | solution.py:396
  7.3 0.6 copy-start.4
  7.9 2.1 %copy-start.2 = (bf16[3,16,256]{2,1,0:T(8,128)(2,1)}, bf16[3,16,256]{2,1,0:T(8,128)(2,1)S(1)}, u32[]{:S(2)}) copy-start(bf16[3,16,256]{2,1,0:T(8,128)(2,1)S(1)} %get-tuple-element.67.raw_end) | copy-start | bytes 73732
  10.0 19.0 %all-to-all-start = ((bf16[32,16,128]{2,1,0:T(8,128)(2,1)}), bf16[32,16,128]{2,1,0:T(8,128)(2,1)S(1)}, u32[]{:S(2)}, u32[]{:S(2)}) async-start(bf16[32,16,128]{2,1,0:T(8,128)(2,1)} %get-tuple-element.55), calls=%async_computation | async-start | bytes 262144 | tf_op jit(solution)/shard_map/all_to_all | solution.py:439
  29.0 13.5 %copy-start = (bf16[512,256]{1,0:T(8,128)(2,1)S(1)}, bf16[512,256]{1,0:T(8,128)(2,1)}, u32[]{:S(2)}) copy-start(bf16[512,256]{1,0:T(8,128)(2,1)} %cot.1) | copy-start | bytes 786436
  29.8 12.8 %copy-start.5 = (f32[1,256]{1,0:T(1,128)S(1)}, f32[1,256]{1,0:T(1,128)}, u32[]{:S(2)}) copy-start(f32[1,256]{1,0:T(1,128)} %copy-done.4) | copy-start | bytes 3076
  44.6 4.0 %copy-start.3 = (bf16[3,16,256]{2,1,0:T(8,128)(2,1)S(1)}, bf16[3,16,256]{2,1,0:T(8,128)(2,1)}, u32[]{:S(2)}) copy-start(bf16[3,16,256]{2,1,0:T(8,128)(2,1)} %copy-done.2) | copy-start | bytes 73732
  44.6 12.9 %all-to-all-start.2 = ((bf16[32,8,128]{2,1,0:T(8,128)(2,1)}), bf16[32,8,128]{2,1,0:T(8,128)(2,1)S(1)}, u32[]{:S(2)}, u32[]{:S(2)}) async-start(bf16[32,8,128]{2,1,0:T(8,128)(2,1)} %bitcast.2), calls=%async_computation.2 | async-start | bytes 131072 | tf_op jit(solution)/shard_map/all_to_all | solution.py:439
  58.8 12.7 %all-to-all-start.3 = ((bf16[32,8,128]{2,1,0:T(8,128)(2,1)}), bf16[32,8,128]{2,1,0:T(8,128)(2,1)S(1)}, u32[]{:S(2)}, u32[]{:S(2)}) async-start(bf16[32,8,128]{2,1,0:T(8,128)(2,1)} %bitcast.4), calls=%async_computation.3 | async-start | bytes 131072 | tf_op jit(solution)/shard_map/all_to_all | solution.py:439

commit v5 on v4

v5 whole, which is shorter than its diff:
```python
import functools

import jax
import jax.numpy as jnp
from jax import lax
from jax.experimental import pallas as pl
from jax.experimental.pallas import tpu as pltpu
from jax.sharding import PartitionSpec as P

HEAD_DIM = 128
TAPS = 4
CHUNK = 128
HALO = 16
EDGE = TAPS - 1
ROUTE = 2 * EDGE
SHARE = 8
FAR = 1 << 30

f32 = jnp.float32
bf16 = jnp.bfloat16


def nt(a, b):
    return lax.dot_general(a, b, (((1,), (1,)), ((), ())), preferred_element_type=f32)


def nn(a, b):
    return lax.dot_general(a, b, (((1,), (0,)), ((), ())), preferred_element_type=f32)


def tn(a, b):
    return lax.dot_general(a, b, (((0,), (0,)), ((), ())), preferred_element_type=f32)


def doc_start(starts, first, pos):
    found = jnp.int32(-FAR)
    for d in range(starts.shape[0]):
        rel = starts[d] - first
        found = jnp.maximum(found, jnp.where(rel <= pos, rel, -FAR))
    return found


def doc_end(starts, first, pos):
    found = jnp.int32(FAR)
    for d in range(starts.shape[0]):
        rel = starts[d] - first
        found = jnp.minimum(found, jnp.where(rel > pos, rel, FAR))
    return found


def row_starts(starts, first, rows):
    found = jnp.full(rows.shape, -FAR, jnp.int32)
    for d in range(starts.shape[0]):
        rel = starts[d] - first
        found = jnp.maximum(found, jnp.where(rows >= rel, rel, -FAR))
    return found


def iota(shape, axis, base=0):
    return lax.broadcasted_iota(jnp.int32, shape, axis) + base


def conv_rows(ext, taps, m, age):
    conv = taps[m, 0:1] * ext
    for j in range(1, TAPS):
        conv = conv + jnp.where(age >= j, taps[m, j : j + 1] * pltpu.roll(ext, j, 0), 0.0)
    return conv


def logistic(x):
    return 1.0 / (1.0 + jnp.exp(-x))


def silu_slope(conv, sigma):
    return sigma * (1.0 + conv * (1.0 - sigma))


def conv_docs(ext, taps, m, starts, first):
    rows = ext.shape[0] - HALO
    conv = taps[m, 0:1] * ext
    for j in range(1, TAPS):
        conv = conv + taps[m, j : j + 1] * pltpu.roll(ext, j, 0)
    parts = []
    for low in range(0, rows, CHUNK):
        top = ext[HALO + low - SHARE : HALO + low + SHARE]
        age = iota((2 * SHARE, HEAD_DIM), 0, low - SHARE) - doc_start(starts, first, low)
        parts.append(conv_rows(top, taps, m, age)[SHARE:])
        parts.append(conv[HALO + low + SHARE : HALO + low + CHUNK])
    return jnp.concatenate(parts, axis=0)


def behind_mask(scores, begin):
    size, high = scores.shape
    parts = [
        jnp.where(at >= begin, scores[:, at : at + size], 0.0) for at in range(0, high - size, size)
    ]
    causal = iota((size, size), 1) <= iota((size, size), 0)
    parts.append(jnp.where(causal, scores[:, high - size :], 0.0))
    return jnp.concatenate(parts, axis=1).astype(bf16)


def ahead_mask(scores, low, end):
    size, length = scores.shape
    causal = iota((size, size), 1) >= iota((size, size), 0)
    parts = [jnp.where(causal, scores[:, :size], 0.0)]
    for at in range(size, length, size):
        parts.append(jnp.where(low + at < end, scores[:, at : at + size], 0.0))
    return jnp.concatenate(parts, axis=1).astype(bf16)


def head_columns(h):
    return slice(h * HEAD_DIM, (h + 1) * HEAD_DIM)


def spread(row):
    return jnp.broadcast_to(row, (SHARE, HEAD_DIM))


def only_top(block):
    return jnp.where(iota(block.shape, 0) < EDGE, block, jnp.zeros((), block.dtype))


def conv_kernel(
    starts, raw_far, cot_far, taps_far, gain_far,
    keys, values, slope_k, message, raw_q, raw_end, tops, taps, gain, raw, sems,
):
    _, rows, width = raw.shape
    heads = range(width // HEAD_DIM)
    first = lax.axis_index("seq") * rows
    taps_load = pltpu.make_async_copy(taps_far, taps, sems.at[0])
    loads = [pltpu.make_async_copy(raw_far.at[m], raw.at[m - 1], sems.at[m]) for m in (1, 2)]
    others = [
        pltpu.make_async_copy(raw_far.at[:, pl.ds(0, HALO)], tops.at[pl.ds(0, 3)], sems.at[3]),
        pltpu.make_async_copy(cot_far.at[pl.ds(0, HALO)], tops.at[3], sems.at[4]),
        pltpu.make_async_copy(raw_far.at[:, pl.ds(rows - HALO, HALO)], raw_end, sems.at[5]),
        pltpu.make_async_copy(raw_far.at[0], raw_q, sems.at[6]),
        pltpu.make_async_copy(gain_far, gain, sems.at[7]),
    ]
    for load in [loads[0], taps_load, loads[1]] + others:
        load.start()
    taps_load.wait()
    begin = jnp.maximum(doc_start(starts, first, rows - 1), EDGE)
    keep = iota((rows, HEAD_DIM), 0) >= begin
    made = {}
    for m, out in ((1, keys), (2, values)):
        loads[m - 1].wait()
        for h in heads:
            at = head_columns(h)
            ext = jnp.concatenate(
                [jnp.zeros((HALO, HEAD_DIM), f32), raw[m - 1, :, at].astype(f32)], axis=0
            )
            conv = conv_docs(ext, taps.at[:, :, at], m, starts, first)
            if m == 1:
                sigma = logistic(conv)
                slope_k[:, at] = silu_slope(conv, sigma)
                conv = conv * sigma
            made[m, h] = conv.astype(bf16)
            out[:, at] = made[m, h]
    for load in others:
        load.wait()
    share = HEAD_DIM // SHARE
    line = iota((SHARE, HEAD_DIM), 0)
    ends, routed = {}, []
    for h in heads:
        at = head_columns(h)
        for m in range(3):
            low = raw_end[m, :, at].astype(f32)[HALO - SHARE :]
            top = tops[m, :, at].astype(f32)[:SHARE]
            ends[m, h] = pltpu.roll(jnp.where(line >= SHARE - EDGE, low, top), EDGE, 0)
    for base in (0, EDGE):
        for h in heads:
            routed += [ends[0, h][base + a : base + a + 1] for a in range(EDGE)]
    for h in heads:
        top = tops[3, :, head_columns(h)].astype(f32)
        routed += [top[a : a + 1] for a in range(EDGE)]
    for h in heads:
        summary = tn(jnp.where(keep, made[1, h], jnp.zeros((), bf16)), made[2, h])
        for n in range(share):
            r = h * share + n
            k_ends = ends[1, h]
            if r < len(routed):
                k_ends = jnp.where(line == ROUTE, spread(routed[r]), k_ends)
            part = summary[n * SHARE : (n + 1) * SHARE]
            message[r] = jnp.concatenate([part, k_ends, ends[2, h]], axis=0).astype(bf16)


def local_kernel(starts, raw_q, taps, keys, values, queries, slope_q, local):
    rows, width = local.shape
    first = lax.axis_index("seq") * rows
    for h in range(width // HEAD_DIM):
        at = head_columns(h)
        ext = jnp.concatenate(
            [jnp.zeros((HALO, HEAD_DIM), f32), raw_q[:, at].astype(f32)], axis=0
        )
        conv = conv_docs(ext, taps.at[:, :, at], 0, starts, first)
        sigma = logistic(conv)
        slope_q[:, at] = silu_slope(conv, sigma)
        q = (conv * sigma).astype(bf16)
        queries[:, at] = q
        for low in range(0, rows, CHUNK):
            high = low + CHUNK
            start = doc_start(starts, first, low)
            scores = behind_mask(nt(q[low:high], keys[:high, at]), start)
            scores = jnp.where(iota(scores.shape, 1) >= EDGE, scores, jnp.zeros((), bf16))
            local[low:high, at] = nn(scores, values[:high, at])


def state_of(message):
    return message.astype(f32)[:, :SHARE].reshape(HEAD_DIM, HEAD_DIM)


def heard_ends(incoming, m, h, heads):
    share = HEAD_DIM // SHARE
    if m:
        return incoming[h * share + m - 1].astype(f32)[SHARE:]
    line = iota((SHARE, HEAD_DIM), 0)
    block = jnp.zeros((SHARE, HEAD_DIM), f32)
    for a in range(2 * EDGE):
        r = (a // EDGE * heads + h) * EDGE + a % EDGE
        row = incoming[r].astype(f32)[SHARE + ROUTE : SHARE + ROUTE + 1]
        block = jnp.where(line == a, spread(row), block)
    return block


def next_cot(incoming, h, heads):
    line = iota((SHARE, HEAD_DIM), 0)
    block = jnp.zeros((SHARE, HEAD_DIM), f32)
    for a in range(EDGE):
        r = (2 * heads + h) * EDGE + a
        row = incoming[r].astype(f32)[SHARE + ROUTE : SHARE + ROUTE + 1]
        block = jnp.where(line == a, spread(row), block)
    return block


def to_halo(block):
    return jnp.concatenate([block, jnp.zeros((HALO - SHARE, HEAD_DIM), block.dtype)], axis=0)


def patched(top, column):
    return jnp.concatenate([top, column[top.shape[0] :]], axis=0)


def normed(attn, gains, cots):
    msq = jnp.mean(attn * attn, axis=-1, keepdims=True)
    scale = lax.rsqrt(jnp.maximum(msq, 1.0))
    scaled = cots * gains
    inner = jnp.mean(scaled * attn, axis=-1, keepdims=True)
    factor = jnp.where(msq > 1.0, scale * scale * scale * inner, 0.0)
    return scale, (scale * scaled - attn * factor).astype(bf16)


def norm_kernel(
    starts, queries, local, incoming, cot, gain, tops, taps, slope_q, slope_k, keys, values,
    attn_out, grad_norm, back, top_qkv, top_slope,
):
    rows, width = local.shape
    heads = width // HEAD_DIM
    share = HEAD_DIM // SHARE
    first = lax.axis_index("seq") * rows
    begin = row_starts(starts, first, iota((rows, HEAD_DIM), 0))
    joined = doc_start(starts, first, 0) < 0
    line = iota((SHARE, HEAD_DIM), 0)
    causal = iota((HALO, HALO), 1) <= iota((HALO, HALO), 0)
    for h in range(heads):
        at = head_columns(h)
        top = []
        for m, made in enumerate((queries, keys, values)):
            behind = jnp.where(joined, heard_ends(incoming, m, h, heads), 0.0)
            own = pltpu.roll(tops[m, :, at].astype(f32)[:SHARE], EDGE, 0)
            ext = jnp.where(line < EDGE, behind, own)
            conv = taps[m, 0:1, at] * ext
            for j in range(1, TAPS):
                conv = conv + taps[m, j : j + 1, at] * pltpu.roll(ext, j, 0)
            conv = pltpu.roll(conv, SHARE - EDGE, 0)
            if m < 2:
                sigma = logistic(conv)
                old = (slope_q, slope_k)[m][:SHARE, at]
                top_slope[m, :, at] = jnp.where(line < EDGE, silu_slope(conv, sigma), old)
                conv = conv * sigma
            fresh = to_halo(only_top(conv)).astype(bf16)
            top.append(fresh)
            old = made[:HALO, at]
            top_qkv[m, :, at] = jnp.where(iota((HALO, HEAD_DIM), 0) < EDGE, fresh, old)
        q_top, k_top, v_top = top
        state = jnp.where(joined, state_of(incoming[h * share : (h + 1) * share]), 0.0)
        carried = nn(queries[:, at], (state + tn(k_top, v_top)).astype(bf16))
        attn = local[:, at] + jnp.where(begin <= 0, carried, 0.0)
        scores = jnp.where(causal, nt(q_top, k_top), 0.0).astype(bf16)
        attn_top = nn(scores, v_top) + nn(q_top, state.astype(bf16))
        attn = patched(jnp.where(line < EDGE, attn_top[:SHARE], attn[:SHARE]), attn)
        scale, grad = normed(attn, gain[:, at], cot[:, at].astype(f32))
        out = (attn * scale * gain[:, at]).astype(bf16)
        attn_out[:, :, at] = out.reshape(attn_out.shape[:2] + (HEAD_DIM,))
        grad_norm[:, at] = grad
        q = patched(top_qkv[0, :, at], queries[:, at])
        masked_q = jnp.where(begin < 0, q, jnp.zeros((), bf16))
        back[h * HEAD_DIM : (h + 1) * HEAD_DIM] = tn(masked_q, grad).astype(bf16)


def conv_back(grad, taps, m, starts, first, rows):
    total = grad.shape[0]
    out = taps[m, 0:1] * grad[:rows]
    for j in range(1, TAPS):
        out = out + pltpu.roll(taps[m, j : j + 1] * grad, total - j, 0)[:rows]
    parts = []
    for high in range(CHUNK, rows + 1, CHUNK):
        near = grad[high - SHARE : high + SHARE]
        age = iota((2 * SHARE, HEAD_DIM), 0, high - SHARE)
        age = age - row_starts(starts, first, age)
        end = taps[m, 0:1] * near[:SHARE]
        for j in range(1, TAPS):
            term = jnp.where(age >= j, taps[m, j : j + 1] * near, 0.0)
            end = end + pltpu.roll(term, 2 * SHARE - j, 0)[:SHARE]
        parts.append(out[high - CHUNK : high - SHARE])
        parts.append(end)
    return jnp.concatenate(parts, axis=0).astype(bf16)


def query_kernel(
    starts, keys, values, top_qkv, top_slope, grad_norm, slope, incoming, raw_end, taps, gain,
    attn_out, early, edge_qkv, edge_slope, edge_grad, sem,
):
    rows, width = grad_norm.shape
    heads = width // HEAD_DIM
    share = HEAD_DIM // SHARE
    first = lax.axis_index("seq") * rows
    copy = pltpu.make_async_copy(attn_out, early.at[:, 0], sem)
    copy.start()
    carry = row_starts(starts, first, iota((rows, HEAD_DIM), 0)) < 0
    start = doc_start(starts, first, rows)
    edge_age = iota((2 * HALO, HEAD_DIM), 0, rows - HALO)
    edge_age = edge_age - row_starts(starts, first, edge_age)
    reach = iota((HALO, rows), 1) >= start
    causal = iota((HALO, HALO), 1) <= iota((HALO, HALO), 0)
    for h in range(heads):
        at = head_columns(h)
        state = state_of(incoming[h * share : (h + 1) * share]).astype(bf16)
        k = patched(top_qkv[1, :, at], keys[:, at])
        v = patched(top_qkv[2, :, at], values[:, at])
        g = grad_norm[:, at]
        slope_top = patched(top_slope[0, :, at], slope[:, at])
        edges, slopes = [], []
        for m in range(3):
            after = pltpu.roll(heard_ends(incoming, m, h, heads), SHARE - EDGE, 0)
            after = to_halo(only_top(after))
            ext = jnp.concatenate([raw_end[m, :, at].astype(f32), after], axis=0)
            conv = conv_rows(ext, taps.at[:, :, at], m, edge_age)[HALO:]
            if m < 2:
                sigma = logistic(conv)
                slopes.append(silu_slope(conv, sigma))
                conv = conv * sigma
            edges.append(conv.astype(bf16))
            edge_qkv[m, :, at] = edges[m]
        edge_slope[:, at] = slopes[1]
        q_e, k_e, v_e = edges

        def edge_sums(left, right, right_e, values, values_e, carried):
            scores = jnp.where(reach, nt(left, right), 0.0).astype(bf16)
            scores_e = jnp.where(causal, nt(left, right_e), 0.0).astype(bf16)
            added = jnp.where(start < 0, carried, 0.0)
            return nn(scores, values) + nn(scores_e, values_e) + added

        attn_e = edge_sums(q_e, k, k_e, v, v_e, nn(q_e, state))
        _, g_e = normed(attn_e, gain[:, at], to_halo(next_cot(incoming, h, heads)))
        edge_grad[:, at] = g_e
        grad_q_e = edge_sums(g_e, v, v_e, k, k_e, nt(g_e, state)) * slopes[0]

        parts = []
        for low in range(0, rows, CHUNK):
            high = low + CHUNK
            begin = doc_start(starts, first, low)
            parts.append(nn(behind_mask(nt(g[low:high], v[:high]), begin), k[:high]))
        carried = jnp.where(carry, nt(g, state), 0.0)
        grad_q = (jnp.concatenate(parts, axis=0) + carried) * slope_top
        both = jnp.concatenate([grad_q, grad_q_e], axis=0)
        out = conv_back(both, taps.at[:, :, at], 0, starts, first, rows)
        early[:, 1, :, at] = out.reshape((early.shape[0], early.shape[2], HEAD_DIM))
    copy.wait()


def key_kernel(
    starts, queries, keys, values, top_qkv, grad_norm, edge_qkv, edge_grad, local_k, local_v
):
    rows, width = grad_norm.shape
    first = lax.axis_index("seq") * rows
    for h in range(width // HEAD_DIM):
        at = head_columns(h)
        columns = (queries[:, at], keys[:, at], values[:, at])
        q, k, v = [patched(top_qkv[m, :, at], columns[m]) for m in range(3)]
        g = grad_norm[:, at]
        for low in range(0, rows, CHUNK):
            high = low + CHUNK
            end = doc_end(starts, first, low)
            scores = ahead_mask(nt(v[low:high], g[low:]), low, end)
            local_k[low:high, at] = nn(scores, q[low:]).astype(bf16)
            scores = ahead_mask(nt(k[low:high], q[low:]), low, end)
            local_v[low:high, at] = nn(scores, g[low:]).astype(bf16)
        q_e, k_e, v_e = edge_qkv[0, :, at], edge_qkv[1, :, at], edge_qkv[2, :, at]
        g_e = edge_grad[:, at]
        earlier = iota((HALO, HALO), 1) < iota((HALO, HALO), 0)
        scores = jnp.where(earlier, -nt(v_e, g_e), 0.0).astype(bf16)
        local_k[rows:, at] = nn(scores, q_e).astype(bf16)
        scores = jnp.where(earlier, -nt(k_e, q_e), 0.0).astype(bf16)
        local_v[rows:, at] = nn(scores, g_e).astype(bf16)


def last_kernel(
    starts, keys, values, top_qkv, top_slope, edge_qkv, slope, edge_slope, local_k, local_v,
    future, taps, early, sent, sem,
):
    total, width = local_k.shape
    rows = total - HALO
    first = lax.axis_index("seq") * rows
    copy = pltpu.make_async_copy(early, sent.at[:, pl.ds(0, 2)], sem)
    copy.start()
    after = iota((total, HEAD_DIM), 0) >= doc_start(starts, first, rows)
    shape = (sent.shape[0], sent.shape[2], HEAD_DIM)
    for m in (2, 1):
        for h in range(width // HEAD_DIM):
            at = head_columns(h)
            state = future[h * HEAD_DIM : (h + 1) * HEAD_DIM]
            if m == 2:
                k = patched(top_qkv[1, :, at], keys[:, at])
                k = jnp.concatenate([k, edge_qkv[1, :, at]], axis=0)
                grad = local_v[:, at].astype(f32) + jnp.where(after, nn(k, state), 0.0)
            else:
                v = patched(top_qkv[2, :, at], values[:, at])
                v = jnp.concatenate([v, edge_qkv[2, :, at]], axis=0)
                slopes = patched(top_slope[1, :, at], slope[:, at])
                slopes = jnp.concatenate([slopes, edge_slope[:, at]], axis=0)
                grad = (local_k[:, at].astype(f32) + jnp.where(after, nt(v, state), 0.0)) * slopes
            out = conv_back(grad, taps.at[:, :, at], m, starts, first, rows)
            sent[:, m + 1, :, at] = out.reshape(shape)
    copy.wait()


def closed(starts, rows, i):
    found = jnp.bool_(False)
    for d in range(starts.shape[0]):
        found = found | ((starts[d] >= i * rows) & (starts[d] < (i + 1) * rows))
    return found


def forward_kernel(rows, starts, sums, taps, out):
    count = sums.shape[0]
    share = HEAD_DIM // SHARE
    place = lax.axis_index("seq")
    part, head = lax.rem(place, share), lax.div(place, share)
    line = iota((SHARE, HEAD_DIM), 0)
    inside = (line >= EDGE) & (line < 2 * EDGE)
    nothing = jnp.zeros((SHARE, HEAD_DIM), f32)

    def tap(m, j):
        row = taps[m, j : j + 1, :HEAD_DIM]
        for h in range(1, taps.shape[2] // HEAD_DIM):
            row = jnp.where(head == h, taps[m, j : j + 1, head_columns(h)], row)
        return row

    heard = [sums[i].astype(f32) for i in range(count)]
    ends = {m: [block[m * SHARE : (m + 1) * SHARE] for block in heard] for m in (1, 2)}
    tops = {1: [], 2: []}
    for m in (1, 2):
        weights = [tap(m, j) for j in range(TAPS)]
        for i in range(count):
            begun, split = jnp.bool_(False), jnp.bool_(False)
            for d in range(starts.shape[0]):
                begun = begun | (starts[d] == i * rows)
                split = split | ((starts[d] > i * rows) & (starts[d] < (i + 1) * rows))
            behind = jnp.where(begun, 0.0, ends[m][i - 1]) if i else nothing
            ext = jnp.where(line < EDGE, behind, ends[m][i])
            conv = weights[0] * ext
            for j in range(1, TAPS):
                conv = conv + weights[j] * pltpu.roll(ext, j, 0)
            if m == 1:
                conv = jnp.where(split, 0.0, conv * logistic(conv))
            tops[m].append(jnp.where(inside, conv, 0.0))
    k_tops, v_tops = [jnp.concatenate(tops[m], axis=0).astype(bf16) for m in (1, 2)]
    own = iota((SHARE, HEAD_DIM), 1) == line + part * SHARE
    picked = nt(jnp.where(own, 1.0, 0.0).astype(bf16), k_tops)
    size = count * SHARE
    same = lax.div(iota((size, size), 0), SHARE) == lax.div(iota((size, size), 1), SHARE)
    picked = jnp.where(same, jnp.concatenate([picked] * count, axis=0), 0.0).astype(bf16)
    added = nn(picked, v_tops)
    state = nothing
    for i in range(count):
        sides = []
        for j in (i - 1, i + 1):
            if 0 <= j < count:
                sides.append((jnp.where(lax.rem(part, 2) == 0, ends[1][j], ends[2][j]), ends[1][j]))
            else:
                sides.append((nothing, nothing))
        block = jnp.where(line < EDGE, sides[0][0], sides[1][0])
        route = jnp.where(place < EDGE * (taps.shape[2] // HEAD_DIM), sides[0][1], sides[1][1])
        block = jnp.where(line == ROUTE, route, block)
        out[i] = jnp.concatenate([state, block], axis=0).astype(bf16)
        new = heard[i][:SHARE] + added[i * SHARE : (i + 1) * SHARE]
        state = new + jnp.where(closed(starts, rows, i), 0.0, state)


def backward_kernel(rows, starts, sums, out):
    count = 2 * sums.shape[0]
    state = jnp.zeros((SHARE, HEAD_DIM), f32)
    for i in range(count - 1, 0, -2):
        pair = sums[i // 2].astype(f32)
        upper = state
        state = pair[SHARE:] + jnp.where(closed(starts, rows, i), 0.0, state)
        out[i // 2] = jnp.concatenate([state, upper], axis=0).astype(bf16)
        state = pair[:SHARE] + jnp.where(closed(starts, rows, i - 1), 0.0, state)


def gather_kernel(sent, out, grad):
    count, _, _, width = sent.shape
    for i in range(count):
        columns = slice(i * width, (i + 1) * width)
        out[:, columns] = sent[i, 0]
        for m in range(3):
            grad[m, :, columns] = sent[i, m + 1]


def shards(qkv_raw, conv_weight, norm_gain, doc_starts, cotangent):
    rows = qkv_raw.shape[0]
    width = qkv_raw.shape[2]
    heads = width // HEAD_DIM
    total = rows + HALO
    devices = lax.axis_size("seq")
    columns = lax.axis_size("head")
    piece = rows // columns
    share = devices // heads
    raw = qkv_raw.transpose(1, 0, 2)
    in_hbm = functools.partial(pltpu.with_memory_space_constraint, memory_space=pltpu.HBM)
    doc_starts = pltpu.with_memory_space_constraint(doc_starts, pltpu.SMEM)
    hd = HEAD_DIM


    smem = pl.BlockSpec(memory_space=pltpu.SMEM)
    params = pltpu.CompilerParams(vmem_limit_bytes=16 * 1024 * 1024)

    vmem = pl.BlockSpec(memory_space=pltpu.VMEM)
    hbm = pl.BlockSpec(memory_space=pltpu.HBM)
    dma = pltpu.SemaphoreType.DMA

    def flat_call(body, ins, outs, scratch, *args, alias={}):
        return pl.pallas_call(
            body,
            in_specs=[smem] + ins,
            out_specs=[hbm if out.memory_space == pltpu.HBM else vmem for out in outs],
            out_shape=outs,
            scratch_shapes=scratch,
            input_output_aliases=alias,
            compiler_params=params,
        )(doc_starts, *[in_hbm(a) if spec is hbm else a for a, spec in zip(args, ins)])

    wide = pltpu.VMEM((rows, width), bf16)
    tall = pltpu.VMEM((rows, width), f32)
    keys, values, slope_k, message, raw_q, raw_end, tops, taps, gain = flat_call(
        conv_kernel,
        [hbm] * 4,
        [
            wide, wide, tall, pltpu.VMEM((devices, 3 * SHARE, hd), bf16), wide,
            pltpu.VMEM((3, HALO, width), bf16), pltpu.VMEM((4, HALO, width), bf16),
            pltpu.VMEM(conv_weight.shape, f32), pltpu.VMEM((1, width), f32),
        ],
        [pltpu.VMEM((2, rows, width), bf16), dma((8,))],
        raw, cotangent, conv_weight, norm_gain.reshape(1, width),
    )

    def swap(parts):
        return lax.all_to_all(parts, "seq", 0, 0, tiled=True)

    def scan(body, shape, parts, *others):
        (found,) = flat_call(
            functools.partial(body, rows), [vmem] * (1 + len(others)),
            [pltpu.VMEM(shape, bf16)], [], parts, *others,
        )
        return found

    queries, slope_q, local = flat_call(
        local_kernel, [vmem] * 4, [wide, tall, tall], [],
        raw_q, taps, keys, values,
    )
    message, queries, slope_q, local = lax.optimization_barrier(
        (swap(message), queries, slope_q, local)
    )
    message = scan(forward_kernel, (devices, 2 * SHARE, hd), message, taps)
    incoming = swap(message)
    attn_out, grad_norm, back, top_qkv, top_slope = flat_call(
        norm_kernel,
        [vmem] * 11,
        [
            pltpu.VMEM((columns, piece, width), bf16), wide,
            pltpu.VMEM((heads * hd, hd), bf16), pltpu.VMEM((3, HALO, width), bf16),
            pltpu.VMEM((2, SHARE, width), f32),
        ],
        [],
        queries, local, incoming, cotangent, gain, tops, taps, slope_q, slope_k, keys, values,
    )
    early, edge_qkv, edge_slope, edge_grad = flat_call(
        query_kernel,
        [vmem] * 11,
        [
            pltpu.VMEM((columns, 2, piece, width), bf16), pltpu.VMEM((3, HALO, width), bf16),
            pltpu.VMEM((HALO, width), f32), pltpu.VMEM((HALO, width), bf16),
        ],
        [dma(())],
        keys, values, top_qkv, top_slope, grad_norm, slope_q, incoming, raw_end, taps, gain,
        attn_out,
    )
    back = swap(back.reshape(devices, SHARE, hd))
    back, early, edge_qkv, edge_slope, edge_grad = lax.optimization_barrier(
        (back, early, edge_qkv, edge_slope, edge_grad)
    )
    pairs = (devices // 2, 2 * SHARE, hd)
    back = scan(backward_kernel, pairs, back.reshape(pairs))
    local_k, local_v = flat_call(
        key_kernel, [vmem] * 7, [pltpu.VMEM((total, width), bf16)] * 2, [],
        queries, keys, values, top_qkv, grad_norm, edge_qkv, edge_grad,
    )
    future, local_k, local_v = lax.optimization_barrier((swap(back.reshape(devices, SHARE, hd)), local_k, local_v))
    (sent,) = flat_call(
        last_kernel, [vmem] * 12, [pltpu.VMEM((columns, 4, piece, width), bf16)], [dma(())],
        keys, values, top_qkv, top_slope, edge_qkv, slope_k, edge_slope, local_k, local_v,
        future.reshape(heads * hd, hd), taps, early,
    )
    sent = lax.all_to_all(sent, "head", 0, 0, tiled=True)
    out, grad = pl.pallas_call(
        gather_kernel,
        out_shape=[
            jax.ShapeDtypeStruct((piece, columns * width), bf16),
            jax.ShapeDtypeStruct((3, piece, columns * width), bf16),
        ],
        compiler_params=params,
    )(sent)
    return out, grad.transpose(1, 0, 2)


def solution(mesh):
    return jax.shard_map(
        shards,
        mesh=mesh,
        in_specs=(P("seq", None, "head"), P(None, None, "head"), P("head"), P(), P("seq", "head")),
        out_specs=(P(("seq", "head"), None), P(("seq", "head"), None, None)),
        check_vma=False,
    )
```

time: 120 us -> 116 us (0.967)
  starting transfers between devices: 21.9 us -> 18.2 us
  waiting for transfers between devices: 17.6 us -> 19.2 us
    ppermute x1 -> x0, starting transfers between devices: 4.15 us -> none  [shards(): rim = lax.ppermute(raw[:, rows - HALO:], 'seq', ahead)]
    all_to_all x1, blocking collectives: 12.8 us -> 14.4 us  [swap(): return lax.all_to_all(parts, 'seq', 0, 0, tiled=True)]
    all_to_all x3, waiting for transfers between devices: 17.6 us -> 19.2 us  [swap(): return lax.all_to_all(parts, 'seq', 0, 0, tiled=True)]
    all_to_all x1, blocking collectives: 45.4 us -> 43.9 us  [shards(): sent = lax.all_to_all(sent, 'head', 0, 0, tiled=True)]
    pallas_call x10 -> x8, Pallas kernels: 18.7 us -> 17.6 us  [flat_call(): pl.pallas_call(body, in_specs=[smem] + ins, out_specs=[hbm if out.memory_...]
  transfers between devices with their start and end apart: 4 -> 3, of which waited for: 3 -> 3; matrix products, arithmetic and copies ran while one was open for 0% -> 0% of each run, Pallas kernels for 9% -> 7%
where the time goes in v5:
time: 116 us
  blocking collectives  58.2 us (50%)
  waiting for transfers between devices  19.2 us (17%)
  Pallas kernels  18.7 us (16%)
  starting transfers between devices  18.2 us (16%)
    all_to_all x1, blocking collectives, shards(): sent = lax.all_to_all(sent, 'head', 0, 0, tiled=True)  43.9 us
    all_to_all x3, waiting for transfers between devices, swap(): return lax.all_to_all(parts, 'seq', 0, 0, tiled=True)  19.2 us
    all_to_all x3, starting transfers between devices, swap(): return lax.all_to_all(parts, 'seq', 0, 0, tiled=True)  18.2 us
    pallas_call x8, Pallas kernels, flat_call(): pl.pallas_call(body, in_specs=[smem] + ins, out_specs=[hbm if out.memory_...  17.6 us
    all_to_all x1, blocking collectives, swap(): return lax.all_to_all(parts, 'seq', 0, 0, tiled=True)  14.4 us
  transfers between devices with their start and end apart: 3, of which 3 were waited for; matrix products, arithmetic and copies ran while one was open for 0% of the time, Pallas kernels for 7%

profile of v5, /device:TPU:1, one launch (start us, length us, event | category | flops | bytes accessed | tf_op | source)
XLA Modules:
  0.0 115.7 jit_solution(4192836552825718980)
XLA Ops:
  0.6 0.0 copy-start.1
  0.6 0.6 copy-done.1
  1.3 3.3 %shard_map.68 = (bf16[512,256]{1,0:T(8,128)(2,1)S(1)}, bf16[512,256]{1,0:T(8,128)(2,1)S(1)}, f32[512,256]{1,0:T(8,128)S(1)}, bf16[32,24,128]{2,1,0:T(8,128)(2,1)...) custom-call(s32[4]{0:T(128)S(1)} %copy-done.1, ...), custom_call_target="tpu_custom_call" | custom-call | tf_op jit(solution)/shard_map/pallas_call | solution.py:543
  4.6 10.5 %all-to-all-start = ((bf16[32,24,128]{2,1,0:T(8,128)(2,1)}), bf16[32,24,128]{2,1,0:T(8,128)(2,1)S(1)}, u32[]{:S(2)}, u32[]{:S(2)}) async-start(bf16[32,24,128]{2,1,0:T(8,128)(2,1)} %get-tuple-element.41), calls=%async_computation | async-start | bytes 393216 | tf_op jit(solution)/shard_map/all_to_all | solution.py:568
  15.1 1.8 %shard_map.69 = (bf16[512,256]{1,0:T(8,128)(2,1)S(1)}, f32[512,256]{1,0:T(8,128)S(1)}, f32[512,256]{1,0:T(8,128)S(1)}) custom-call(s32[4]{0:T(128)S(1)} %copy-done.1, bf16[512,256]{1,0:T(8,128)(2,1)S(1)} %get-tuple-element.42.raw_q, f32[3,4,256]{2,1,0:T(4,128)S(1)} %get-tuple-element.43.taps, bf16[512,256]{1,0:T(8,128)(2,1)S(1)} %get-tuple-element.39.keys, ...), custom_call_target="tpu_custom_call" | custom-call | tf_op jit(solution)/shard_map/pallas_call | solution.py:543
  16.9 7.6 %all-to-all-done.sums = bf16[32,24,128]{2,1,0:T(8,128)(2,1)S(1)} async-done(((bf16[32,24,128]{2,1,0:T(8,128)(2,1)}), bf16[32,24,128]{2,1,0:T(8,128)(2,1)S(1)}, u32[]{:S(2)}, u32[]{:S(2)}) %all-to-all-start) | async-done | bytes 196640 | tf_op jit(solution)/shard_map/all_to_all | solution.py:568
  24.5 0.0 copy-start
  24.5 1.2 shard_map.70
  25.6 14.4 %all_to_all.25.incoming = bf16[32,16,128]{2,1,0:T(8,128)(2,1)S(1)} all-to-all(bf16[32,16,128]{2,1,0:T(8,128)(2,1)S(1)} %shard_map.70), channel_id=1, replica_groups=mesh['seq'=32,'head'=16] {'seq'}, dimensions={0} | all-to-all | bytes 262144 | tf_op jit(solution)/shard_map/all_to_all | solution.py:568
  40.0 0.0 copy-done
  40.0 2.5 %shard_map.71 = (bf16[16,32,256]{2,1,0:T(8,128)(2,1)S(1)}, bf16[512,256]{1,0:T(8,128)(2,1)S(1)}, bf16[256,128]{1,0:T(8,128)(2,1)}, bf16[3,16,256]{2,1,0:T(8,128)(2,1)S(1)}, f32[2,8,256]{2,1,0:T(8,128)S(1)}) custom-call(s32[4]{0:T(128)S(1)} %copy-done.1, bf16[512,256]{1,0:T(8,128)(2,1)S(1)} %get-tuple-element.47.queries, ...), custom_call_target="tpu_custom_call" | custom-call | tf_op jit(solution)/shard_map/pallas_call | solution.py:543
  42.5 3.9 %all-to-all-start.2 = ((bf16[32,8,128]{2,1,0:T(8,128)(2,1)}), bf16[32,8,128]{2,1,0:T(8,128)(2,1)S(1)}, u32[]{:S(2)}, u32[]{:S(2)}) async-start(bf16[32,8,128]{2,1,0:T(8,128)(2,1)} %bitcast.2), calls=%async_computation.2 | async-start | bytes 131072 | tf_op jit(solution)/shard_map/all_to_all | solution.py:568
  46.4 3.2 %shard_map.72 = (bf16[16,2,32,256]{3,2,1,0:T(8,128)(2,1)S(1)}, bf16[3,16,256]{2,1,0:T(8,128)(2,1)S(1)}, f32[16,256]{1,0:T(8,128)S(1)}, bf16[16,256]{1,0:T(8,128)(2,1)S(1)}) custom-call(s32[4]{0:T(128)S(1)} %copy-done.1, bf16[512,256]{1,0:T(8,128)(2,1)S(1)} %get-tuple-element.39.keys, bf16[512,256]{1,0:T(8,128)(2,1)S(1)} %get-tuple-element.40.values, ...), custom_call_target="tpu_custom_call" | custom-call | tf_op jit(solution)/shard_map/pallas_call | solution.py:543
  49.6 5.6 %all-to-all-done.2 = bf16[32,8,128]{2,1,0:T(8,128)(2,1)S(1)} async-done(((bf16[32,8,128]{2,1,0:T(8,128)(2,1)}), bf16[32,8,128]{2,1,0:T(8,128)(2,1)S(1)}, u32[]{:S(2)}, u32[]{:S(2)}) %all-to-all-start.2) | async-done | bytes 65568 | tf_op jit(solution)/shard_map/all_to_all | solution.py:568
  55.2 1.3 %shard_map.73 = bf16[16,16,128]{2,1,0:T(8,128)(2,1)} custom-call(s32[4]{0:T(128)S(1)} %copy-done.1, bf16[16,16,128]{2,1,0:T(8,128)(2,1)S(1)} %bitcast.8), custom_call_target="tpu_custom_call" | custom-call | tf_op jit(solution)/shard_map/pallas_call | solution.py:543
  56.6 3.9 %all-to-all-start.3 = ((bf16[32,8,128]{2,1,0:T(8,128)(2,1)}), bf16[32,8,128]{2,1,0:T(8,128)(2,1)S(1)}, u32[]{:S(2)}, u32[]{:S(2)}) async-start(bf16[32,8,128]{2,1,0:T(8,128)(2,1)} %bitcast.4), calls=%async_computation.3 | async-start | bytes 131072 | tf_op jit(solution)/shard_map/all_to_all | solution.py:568
  60.4 2.9 %shard_map.74 = (bf16[528,256]{1,0:T(8,128)(2,1)S(1)}, bf16[528,256]{1,0:T(8,128)(2,1)S(1)}) custom-call(s32[4]{0:T(128)S(1)} %copy-done.1, bf16[512,256]{1,0:T(8,128)(2,1)S(1)} %get-tuple-element.47.queries, bf16[512,256]{1,0:T(8,128)(2,1)S(1)} %get-tuple-element.39.keys, bf16[512,256]{1,0:T(8,128)(2,1)S(1)} %get-tuple-element.40.values, ...), custom_call_target="tpu_custom_call" | custom-call | tf_op jit(solution)/shard_map/pallas_call | solution.py:543
  63.3 6.0 %all-to-all-done.3 = bf16[32,8,128]{2,1,0:T(8,128)(2,1)S(1)} async-done(((bf16[32,8,128]{2,1,0:T(8,128)(2,1)}), bf16[32,8,128]{2,1,0:T(8,128)(2,1)S(1)}, u32[]{:S(2)}, u32[]{:S(2)}) %all-to-all-start.3) | async-done | bytes 65568 | tf_op jit(solution)/shard_map/all_to_all | solution.py:568
  69.3 1.5 %shard_map.75 = bf16[16,4,32,256]{3,2,1,0:T(8,128)(2,1)S(1)} custom-call(s32[4]{0:T(128)S(1)} %copy-done.1, bf16[512,256]{1,0:T(8,128)(2,1)S(1)} %get-tuple-element.39.keys, bf16[512,256]{1,0:T(8,128)(2,1)S(1)} %get-tuple-element.40.values, bf16[3,16,256]{2,1,0:T(8,128)(2,1)S(1)} %get-tuple-element.54.top_qkv, f32[2,8,256]{2,1,0:T(8,128)S(1)} %get-tuple-element.55.top_slope, ...), custom_call_target="tpu_custom_call" | custom-call | tf_op jit(solution)/shard_map/pallas_call | solution.py:543
  70.8 43.9 %all_to_all.26.sent = bf16[16,4,32,256]{3,2,1,0:T(8,128)(2,1)S(1)} all-to-all(bf16[16,4,32,256]{3,2,1,0:T(8,128)(2,1)S(1)} %shard_map.75), channel_id=1, replica_groups=mesh['seq'=32,'head'=16] {'head'}, dimensions={0} | all-to-all | bytes 2097152 | tf_op jit(solution)/shard_map/all_to_all | solution.py:624
  114.7 1.1 shard_map.76
Async XLA Ops:
  0.6 0.7 copy-start.1
  4.6 19.9 %all-to-all-start = ((bf16[32,24,128]{2,1,0:T(8,128)(2,1)}), bf16[32,24,128]{2,1,0:T(8,128)(2,1)S(1)}, u32[]{:S(2)}, u32[]{:S(2)}) async-start(bf16[32,24,128]{2,1,0:T(8,128)(2,1)} %get-tuple-element.41), calls=%async_computation | async-start | bytes 393216 | tf_op jit(solution)/shard_map/all_to_all | solution.py:568
  24.5 15.6 %copy-start = (bf16[512,256]{1,0:T(8,128)(2,1)S(1)}, bf16[512,256]{1,0:T(8,128)(2,1)}, u32[]{:S(2)}) copy-start(bf16[512,256]{1,0:T(8,128)(2,1)} %cot.1) | copy-start | bytes 786436
  42.5 12.7 %all-to-all-start.2 = ((bf16[32,8,128]{2,1,0:T(8,128)(2,1)}), bf16[32,8,128]{2,1,0:T(8,128)(2,1)S(1)}, u32[]{:S(2)}, u32[]{:S(2)}) async-start(bf16[32,8,128]{2,1,0:T(8,128)(2,1)} %bitcast.2), calls=%async_computation.2 | async-start | bytes 131072 | tf_op jit(solution)/shard_map/all_to_all | solution.py:568
  56.6 12.7 %all-to-all-start.3 = ((bf16[32,8,128]{2,1,0:T(8,128)(2,1)}), bf16[32,8,128]{2,1,0:T(8,128)(2,1)S(1)}, u32[]{:S(2)}, u32[]{:S(2)}) async-start(bf16[32,8,128]{2,1,0:T(8,128)(2,1)} %bitcast.4), calls=%async_computation.3 | async-start | bytes 131072 | tf_op jit(solution)/shard_map/all_to_all | solution.py:568

commit v6 on v5

--- a/solution.py
+++ b/solution.py
@@ -10,6 +10,7 @@
 HEAD_DIM = 128
 TAPS = 4
 CHUNK = 128
+SPAN = 256
 HALO = 16
 EDGE = TAPS - 1
 ROUTE = 2 * EDGE
@@ -89,23 +90,47 @@
     return jnp.concatenate(parts, axis=0)
 
 
-def behind_mask(scores, begin):
+def behind_mask(scores, low, starts, first, least=0):
     size, high = scores.shape
-    parts = [
-        jnp.where(at >= begin, scores[:, at : at + size], 0.0) for at in range(0, high - size, size)
-    ]
-    causal = iota((size, size), 1) <= iota((size, size), 0)
-    parts.append(jnp.where(causal, scores[:, high - size :], 0.0))
-    return jnp.concatenate(parts, axis=1).astype(bf16)
-
-
-def ahead_mask(scores, low, end):
+    causal = iota((CHUNK, CHUNK), 1) <= iota((CHUNK, CHUNK), 0)
+    late = iota((CHUNK, CHUNK), 1) >= least
+    bands = []
+    for top in range(low, low + size, CHUNK):
+        begin = doc_start(starts, first, top)
+        parts = []
+        for at in range(0, high, CHUNK):
+            part = scores[top - low : top - low + CHUNK, at : at + CHUNK]
+            if at > top:
+                part = jnp.zeros_like(part)
+            elif at == top:
+                part = jnp.where(causal & late if at == 0 and least else causal, part, 0.0)
+            else:
+                part = jnp.where(at >= begin, part, 0.0)
+                if at == 0 and least:
+                    part = jnp.where(late, part, 0.0)
+            parts.append(part)
+        bands.append(jnp.concatenate(parts, axis=1))
+    return jnp.concatenate(bands, axis=0).astype(bf16)
+
+
+def ahead_mask(scores, low, starts, first):
     size, length = scores.shape
-    causal = iota((size, size), 1) >= iota((size, size), 0)
-    parts = [jnp.where(causal, scores[:, :size], 0.0)]
-    for at in range(size, length, size):
-        parts.append(jnp.where(low + at < end, scores[:, at : at + size], 0.0))
-    return jnp.concatenate(parts, axis=1).astype(bf16)
+    causal = iota((CHUNK, CHUNK), 1) >= iota((CHUNK, CHUNK), 0)
+    bands = []
+    for top in range(low, low + size, CHUNK):
+        end = doc_end(starts, first, top)
+        parts = []
+        for at in range(low, low + length, CHUNK):
+            part = scores[top - low : top - low + CHUNK, at - low : at - low + CHUNK]
+            if at < top:
+                part = jnp.zeros_like(part)
+            elif at == top:
+                part = jnp.where(causal, part, 0.0)
+            else:
+                part = jnp.where(at < end, part, 0.0)
+            parts.append(part)
+        bands.append(jnp.concatenate(parts, axis=1))
+    return jnp.concatenate(bands, axis=0).astype(bf16)
 
 
 def head_columns(h):
@@ -121,8 +146,8 @@
 
 
 def conv_kernel(
-    starts, raw_far, cot_far, taps_far, gain_far,
-    keys, values, slope_k, message, raw_q, raw_end, tops, taps, gain, raw, sems,
+    starts_far, raw_far, cot_far, taps_far, gain_far,
+    keys, values, message, raw_end, tops, taps, gain, raw, starts, sems,
 ):
     _, rows, width = raw.shape
     heads = range(width // HEAD_DIM)
@@ -133,11 +158,12 @@
         pltpu.make_async_copy(raw_far.at[:, pl.ds(0, HALO)], tops.at[pl.ds(0, 3)], sems.at[3]),
         pltpu.make_async_copy(cot_far.at[pl.ds(0, HALO)], tops.at[3], sems.at[4]),
         pltpu.make_async_copy(raw_far.at[:, pl.ds(rows - HALO, HALO)], raw_end, sems.at[5]),
-        pltpu.make_async_copy(raw_far.at[0], raw_q, sems.at[6]),
-        pltpu.make_async_copy(gain_far, gain, sems.at[7]),
+        pltpu.make_async_copy(gain_far, gain, sems.at[6]),
     ]
-    for load in [loads[0], taps_load, loads[1]] + others:
+    starts_load = pltpu.make_async_copy(starts_far, starts, sems.at[7])
+    for load in [starts_load, loads[0], taps_load, loads[1]] + others:
         load.start()
+    starts_load.wait()
     taps_load.wait()
     begin = jnp.maximum(doc_start(starts, first, rows - 1), EDGE)
     keep = iota((rows, HEAD_DIM), 0) >= begin
@@ -151,9 +177,7 @@
             )
             conv = conv_docs(ext, taps.at[:, :, at], m, starts, first)
             if m == 1:
-                sigma = logistic(conv)
-                slope_k[:, at] = silu_slope(conv, sigma)
-                conv = conv * sigma
+                conv = conv * logistic(conv)
             made[m, h] = conv.astype(bf16)
             out[:, at] = made[m, h]
     for load in others:
@@ -184,24 +208,32 @@
             message[r] = jnp.concatenate([part, k_ends, ends[2, h]], axis=0).astype(bf16)
 
 
-def local_kernel(starts, raw_q, taps, keys, values, queries, slope_q, local):
+def local_kernel(
+    starts, raw_far, taps, keys, values, queries, slope_q, slope_k, local, raw, sems
+):
     rows, width = local.shape
     first = lax.axis_index("seq") * rows
+    loads = [pltpu.make_async_copy(raw_far.at[m], raw.at[m], sems.at[m]) for m in range(2)]
+    for load in loads:
+        load.start()
+    for m, slope in ((0, slope_q), (1, slope_k)):
+        loads[m].wait()
+        for h in range(width // HEAD_DIM):
+            at = head_columns(h)
+            ext = jnp.concatenate(
+                [jnp.zeros((HALO, HEAD_DIM), f32), raw[m, :, at].astype(f32)], axis=0
+            )
+            conv = conv_docs(ext, taps.at[:, :, at], m, starts, first)
+            sigma = logistic(conv)
+            slope[:, at] = silu_slope(conv, sigma)
+            if m == 0:
+                queries[:, at] = (conv * sigma).astype(bf16)
     for h in range(width // HEAD_DIM):
         at = head_columns(h)
-        ext = jnp.concatenate(
-            [jnp.zeros((HALO, HEAD_DIM), f32), raw_q[:, at].astype(f32)], axis=0
-        )
-        conv = conv_docs(ext, taps.at[:, :, at], 0, starts, first)
-        sigma = logistic(conv)
-        slope_q[:, at] = silu_slope(conv, sigma)
-        q = (conv * sigma).astype(bf16)
-        queries[:, at] = q
-        for low in range(0, rows, CHUNK):
-            high = low + CHUNK
-            start = doc_start(starts, first, low)
-            scores = behind_mask(nt(q[low:high], keys[:high, at]), start)
-            scores = jnp.where(iota(scores.shape, 1) >= EDGE, scores, jnp.zeros((), bf16))
+        for low in range(0, rows, SPAN):
+            high = low + SPAN
+            scores = nt(queries[low:high, at], keys[:high, at])
+            scores = behind_mask(scores, low, starts, first, EDGE)
             local[low:high, at] = nn(scores, values[:high, at])
 
 
@@ -366,10 +398,10 @@
         grad_q_e = edge_sums(g_e, v, v_e, k, k_e, nt(g_e, state)) * slopes[0]
 
         parts = []
-        for low in range(0, rows, CHUNK):
-            high = low + CHUNK
-            begin = doc_start(starts, first, low)
-            parts.append(nn(behind_mask(nt(g[low:high], v[:high]), begin), k[:high]))
+        for low in range(0, rows, SPAN):
+            high = low + SPAN
+            scores = behind_mask(nt(g[low:high], v[:high]), low, starts, first)
+            parts.append(nn(scores, k[:high]))
         carried = jnp.where(carry, nt(g, state), 0.0)
         grad_q = (jnp.concatenate(parts, axis=0) + carried) * slope_top
         both = jnp.concatenate([grad_q, grad_q_e], axis=0)
@@ -388,12 +420,11 @@
         columns = (queries[:, at], keys[:, at], values[:, at])
         q, k, v = [patched(top_qkv[m, :, at], columns[m]) for m in range(3)]
         g = grad_norm[:, at]
-        for low in range(0, rows, CHUNK):
-            high = low + CHUNK
-            end = doc_end(starts, first, low)
-            scores = ahead_mask(nt(v[low:high], g[low:]), low, end)
+        for low in range(0, rows, SPAN):
+            high = low + SPAN
+            scores = ahead_mask(nt(v[low:high], g[low:]), low, starts, first)
             local_k[low:high, at] = nn(scores, q[low:]).astype(bf16)
-            scores = ahead_mask(nt(k[low:high], q[low:]), low, end)
+            scores = ahead_mask(nt(k[low:high], q[low:]), low, starts, first)
             local_v[low:high, at] = nn(scores, g[low:]).astype(bf16)
         q_e, k_e, v_e = edge_qkv[0, :, at], edge_qkv[1, :, at], edge_qkv[2, :, at]
         g_e = edge_grad[:, at]
@@ -528,7 +559,6 @@
     share = devices // heads
     raw = qkv_raw.transpose(1, 0, 2)
     in_hbm = functools.partial(pltpu.with_memory_space_constraint, memory_space=pltpu.HBM)
-    doc_starts = pltpu.with_memory_space_constraint(doc_starts, pltpu.SMEM)
     hd = HEAD_DIM
 
 
@@ -539,28 +569,28 @@
     hbm = pl.BlockSpec(memory_space=pltpu.HBM)
     dma = pltpu.SemaphoreType.DMA
 
-    def flat_call(body, ins, outs, scratch, *args, alias={}):
+    def flat_call(body, ins, outs, scratch, *args):
+        spec = hbm if body is conv_kernel else smem
         return pl.pallas_call(
             body,
-            in_specs=[smem] + ins,
+            in_specs=[spec] + ins,
             out_specs=[hbm if out.memory_space == pltpu.HBM else vmem for out in outs],
             out_shape=outs,
             scratch_shapes=scratch,
-            input_output_aliases=alias,
             compiler_params=params,
-        )(doc_starts, *[in_hbm(a) if spec is hbm else a for a, spec in zip(args, ins)])
+        )(in_hbm(doc_starts) if spec is hbm else doc_starts, *[in_hbm(a) if spec is hbm else a for a, spec in zip(args, ins)])
 
     wide = pltpu.VMEM((rows, width), bf16)
     tall = pltpu.VMEM((rows, width), f32)
-    keys, values, slope_k, message, raw_q, raw_end, tops, taps, gain = flat_call(
+    keys, values, message, raw_end, tops, taps, gain = flat_call(
         conv_kernel,
         [hbm] * 4,
         [
-            wide, wide, tall, pltpu.VMEM((devices, 3 * SHARE, hd), bf16), wide,
+            wide, wide, pltpu.VMEM((devices, 3 * SHARE, hd), bf16),
             pltpu.VMEM((3, HALO, width), bf16), pltpu.VMEM((4, HALO, width), bf16),
             pltpu.VMEM(conv_weight.shape, f32), pltpu.VMEM((1, width), f32),
         ],
-        [pltpu.VMEM((2, rows, width), bf16), dma((8,))],
+        [pltpu.VMEM((2, rows, width), bf16), pltpu.SMEM(doc_starts.shape, jnp.int32), dma((8,))],
         raw, cotangent, conv_weight, norm_gain.reshape(1, width),
     )
 
@@ -574,13 +604,13 @@
         )
         return found
 
-    queries, slope_q, local = flat_call(
-        local_kernel, [vmem] * 4, [wide, tall, tall], [],
-        raw_q, taps, keys, values,
-    )
-    message, queries, slope_q, local = lax.optimization_barrier(
-        (swap(message), queries, slope_q, local)
-    )
+    beside = flat_call(
+        local_kernel, [hbm] + [vmem] * 3, [wide, tall, tall, tall],
+        [pltpu.VMEM((2, rows, width), bf16), dma((2,))],
+        raw, taps, keys, values,
+    )
+    message, beside = lax.optimization_barrier((swap(message), beside))
+    queries, slope_q, slope_k, local = beside
     message = scan(forward_kernel, (devices, 2 * SHARE, hd), message, taps)
     incoming = swap(message)
     attn_out, grad_norm, back, top_qkv, top_slope = flat_call(

time: 116 us -> 115 us (level)
  no operation moved by 1% of the time
where the time goes in v6:
time: 115 us; the launch traced here: 114 us
  blocking collectives  58.2 us (51%)
  waiting for transfers between devices  18.5 us (16%)
  Pallas kernels  18.2 us (16%)
  starting transfers between devices  18.2 us (16%)
    all_to_all x1, blocking collectives, shards(): sent = lax.all_to_all(sent, 'head', 0, 0, tiled=True)  43.8 us
    all_to_all x3, waiting for transfers between devices, swap(): return lax.all_to_all(parts, 'seq', 0, 0, tiled=True)  18.5 us
    all_to_all x3, starting transfers between devices, swap(): return lax.all_to_all(parts, 'seq', 0, 0, tiled=True)  18.2 us
    pallas_call x8, Pallas kernels, flat_call(): pl.pallas_call(body, in_specs=[spec] + ins, out_specs=[hbm if out.memory_...  17.1 us
    all_to_all x1, blocking collectives, swap(): return lax.all_to_all(parts, 'seq', 0, 0, tiled=True)  14.4 us
  transfers between devices with their start and end apart: 3, of which 3 were waited for; matrix products, arithmetic and copies ran while one was open for 0% of the time, Pallas kernels for 7%

profile of v6, /device:TPU:1, one launch (start us, length us, event | category | flops | bytes accessed | tf_op | source)
XLA Modules:
  0.0 114.5 jit_solution(2782149397384597310)
XLA Ops:
  0.6 2.7 %shard_map.68 = (bf16[512,256]{1,0:T(8,128)(2,1)S(1)}, bf16[512,256]{1,0:T(8,128)(2,1)S(1)}, bf16[32,24,128]{2,1,0:T(8,128)(2,1)}, bf16[3,16,256]{2,1,0:T(8,128)...) custom-call(s32[4]{0:T(128)} %starts.13, ...), custom_call_target="tpu_custom_call" | custom-call | tf_op jit(solution)/shard_map/pallas_call | solution.py:574
  3.3 10.5 %all-to-all-start = ((bf16[32,24,128]{2,1,0:T(8,128)(2,1)}), bf16[32,24,128]{2,1,0:T(8,128)(2,1)S(1)}, u32[]{:S(2)}, u32[]{:S(2)}) async-start(bf16[32,24,128]{2,1,0:T(8,128)(2,1)} %get-tuple-element.41), calls=%async_computation | async-start | bytes 393216 | tf_op jit(solution)/shard_map/all_to_all | solution.py:598
  13.8 0.0 copy-start.1
  13.8 0.6 copy-done.1
  14.5 3.3 %shard_map.69 = (bf16[512,256]{1,0:T(8,128)(2,1)S(1)}, f32[512,256]{1,0:T(8,128)S(1)}, f32[512,256]{1,0:T(8,128)S(1)}, f32[512,256]{1,0:T(8,128)S(1)}) custom-call(s32[4]{0:T(128)S(1)} %copy-done.1, bf16[3,512,256]{2,1,0:T(8,128)(2,1)} %bitcast.10, f32[3,4,256]{2,1,0:T(4,128)S(1)} %get-tuple-element.42.taps, bf16[512,256]{1,0:T(8,128)(2,1)S(1)} %get-tuple-element.39.keys, ...), custom_call_target="tpu_custom_call" | custom-call | tf_op jit(solution)/shard_map/pallas_call | solution.py:574
  17.7 5.5 %all-to-all-done.sums = bf16[32,24,128]{2,1,0:T(8,128)(2,1)S(1)} async-done(((bf16[32,24,128]{2,1,0:T(8,128)(2,1)}), bf16[32,24,128]{2,1,0:T(8,128)(2,1)S(1)}, u32[]{:S(2)}, u32[]{:S(2)}) %all-to-all-start) | async-done | bytes 196640 | tf_op jit(solution)/shard_map/all_to_all | solution.py:598
  23.2 0.0 copy-start
  23.2 1.1 %shard_map.70 = bf16[32,16,128]{2,1,0:T(8,128)(2,1)S(1)} custom-call(s32[4]{0:T(128)S(1)} %copy-done.1, bf16[32,24,128]{2,1,0:T(8,128)(2,1)S(1)} %all-to-all-done.sums, f32[3,4,256]{2,1,0:T(4,128)S(1)} %get-tuple-element.42.taps), custom_call_target="tpu_custom_call" | custom-call | tf_op jit(solution)/shard_map/pallas_call | solution.py:574
  24.4 14.4 %all_to_all.25.incoming = bf16[32,16,128]{2,1,0:T(8,128)(2,1)S(1)} all-to-all(bf16[32,16,128]{2,1,0:T(8,128)(2,1)S(1)} %shard_map.70), channel_id=1, replica_groups=mesh['seq'=32,'head'=16] {'seq'}, dimensions={0} | all-to-all | bytes 262144 | tf_op jit(solution)/shard_map/all_to_all | solution.py:598
  38.8 0.0 copy-done
  38.8 2.5 %shard_map.71 = (bf16[16,32,256]{2,1,0:T(8,128)(2,1)S(1)}, bf16[512,256]{1,0:T(8,128)(2,1)S(1)}, bf16[256,128]{1,0:T(8,128)(2,1)}, bf16[3,16,256]{2,1,0:T(8,128)(2,1)S(1)}, f32[2,8,256]{2,1,0:T(8,128)S(1)}) custom-call(s32[4]{0:T(128)S(1)} %copy-done.1, bf16[512,256]{1,0:T(8,128)(2,1)S(1)} %get-tuple-element.47.queries, ...), custom_call_target="tpu_custom_call" | custom-call | tf_op jit(solution)/shard_map/pallas_call | solution.py:574
  41.2 3.9 %all-to-all-start.2 = ((bf16[32,8,128]{2,1,0:T(8,128)(2,1)}), bf16[32,8,128]{2,1,0:T(8,128)(2,1)S(1)}, u32[]{:S(2)}, u32[]{:S(2)}) async-start(bf16[32,8,128]{2,1,0:T(8,128)(2,1)} %bitcast.2), calls=%async_computation.2 | async-start | bytes 131072 | tf_op jit(solution)/shard_map/all_to_all | solution.py:598
  45.1 2.8 %shard_map.72 = (bf16[16,2,32,256]{3,2,1,0:T(8,128)(2,1)S(1)}, bf16[3,16,256]{2,1,0:T(8,128)(2,1)S(1)}, f32[16,256]{1,0:T(8,128)S(1)}, bf16[16,256]{1,0:T(8,128)(2,1)S(1)}) custom-call(s32[4]{0:T(128)S(1)} %copy-done.1, bf16[512,256]{1,0:T(8,128)(2,1)S(1)} %get-tuple-element.39.keys, bf16[512,256]{1,0:T(8,128)(2,1)S(1)} %get-tuple-element.40.values, ...), custom_call_target="tpu_custom_call" | custom-call | tf_op jit(solution)/shard_map/pallas_call | solution.py:574
  47.9 6.1 %all-to-all-done.2 = bf16[32,8,128]{2,1,0:T(8,128)(2,1)S(1)} async-done(((bf16[32,8,128]{2,1,0:T(8,128)(2,1)}), bf16[32,8,128]{2,1,0:T(8,128)(2,1)S(1)}, u32[]{:S(2)}, u32[]{:S(2)}) %all-to-all-start.2) | async-done | bytes 65568 | tf_op jit(solution)/shard_map/all_to_all | solution.py:598
  54.0 1.3 %shard_map.73 = bf16[16,16,128]{2,1,0:T(8,128)(2,1)} custom-call(s32[4]{0:T(128)S(1)} %copy-done.1, bf16[16,16,128]{2,1,0:T(8,128)(2,1)S(1)} %bitcast.8), custom_call_target="tpu_custom_call" | custom-call | tf_op jit(solution)/shard_map/pallas_call | solution.py:574
  55.3 3.9 %all-to-all-start.3 = ((bf16[32,8,128]{2,1,0:T(8,128)(2,1)}), bf16[32,8,128]{2,1,0:T(8,128)(2,1)S(1)}, u32[]{:S(2)}, u32[]{:S(2)}) async-start(bf16[32,8,128]{2,1,0:T(8,128)(2,1)} %bitcast.4), calls=%async_computation.3 | async-start | bytes 131072 | tf_op jit(solution)/shard_map/all_to_all | solution.py:598
  59.2 2.0 %shard_map.74 = (bf16[528,256]{1,0:T(8,128)(2,1)S(1)}, bf16[528,256]{1,0:T(8,128)(2,1)S(1)}) custom-call(s32[4]{0:T(128)S(1)} %copy-done.1, bf16[512,256]{1,0:T(8,128)(2,1)S(1)} %get-tuple-element.47.queries, bf16[512,256]{1,0:T(8,128)(2,1)S(1)} %get-tuple-element.39.keys, bf16[512,256]{1,0:T(8,128)(2,1)S(1)} %get-tuple-element.40.values, ...), custom_call_target="tpu_custom_call" | custom-call | tf_op jit(solution)/shard_map/pallas_call | solution.py:574
  61.1 6.9 %all-to-all-done.3 = bf16[32,8,128]{2,1,0:T(8,128)(2,1)S(1)} async-done(((bf16[32,8,128]{2,1,0:T(8,128)(2,1)}), bf16[32,8,128]{2,1,0:T(8,128)(2,1)S(1)}, u32[]{:S(2)}, u32[]{:S(2)}) %all-to-all-start.3) | async-done | bytes 65568 | tf_op jit(solution)/shard_map/all_to_all | solution.py:598
  68.0 1.5 %shard_map.75 = bf16[16,4,32,256]{3,2,1,0:T(8,128)(2,1)S(1)} custom-call(s32[4]{0:T(128)S(1)} %copy-done.1, bf16[512,256]{1,0:T(8,128)(2,1)S(1)} %get-tuple-element.39.keys, bf16[512,256]{1,0:T(8,128)(2,1)S(1)} %get-tuple-element.40.values, bf16[3,16,256]{2,1,0:T(8,128)(2,1)S(1)} %get-tuple-element.54.top_qkv, f32[2,8,256]{2,1,0:T(8,128)S(1)} %get-tuple-element.55.top_slope, ...), custom_call_target="tpu_custom_call" | custom-call | tf_op jit(solution)/shard_map/pallas_call | solution.py:574
  69.6 43.8 %all_to_all.26.sent = bf16[16,4,32,256]{3,2,1,0:T(8,128)(2,1)S(1)} all-to-all(bf16[16,4,32,256]{3,2,1,0:T(8,128)(2,1)S(1)} %shard_map.75), channel_id=1, replica_groups=mesh['seq'=32,'head'=16] {'head'}, dimensions={0} | all-to-all | bytes 2097152 | tf_op jit(solution)/shard_map/all_to_all | solution.py:654
  113.4 1.1 shard_map.76
Async XLA Ops:
  3.3 19.9 %all-to-all-start = ((bf16[32,24,128]{2,1,0:T(8,128)(2,1)}), bf16[32,24,128]{2,1,0:T(8,128)(2,1)S(1)}, u32[]{:S(2)}, u32[]{:S(2)}) async-start(bf16[32,24,128]{2,1,0:T(8,128)(2,1)} %get-tuple-element.41), calls=%async_computation | async-start | bytes 393216 | tf_op jit(solution)/shard_map/all_to_all | solution.py:598
  13.8 0.7 copy-start.1
  23.2 15.6 %copy-start = (bf16[512,256]{1,0:T(8,128)(2,1)S(1)}, bf16[512,256]{1,0:T(8,128)(2,1)}, u32[]{:S(2)}) copy-start(bf16[512,256]{1,0:T(8,128)(2,1)} %cot.1) | copy-start | bytes 786436
  41.2 12.7 %all-to-all-start.2 = ((bf16[32,8,128]{2,1,0:T(8,128)(2,1)}), bf16[32,8,128]{2,1,0:T(8,128)(2,1)S(1)}, u32[]{:S(2)}, u32[]{:S(2)}) async-start(bf16[32,8,128]{2,1,0:T(8,128)(2,1)} %bitcast.2), calls=%async_computation.2 | async-start | bytes 131072 | tf_op jit(solution)/shard_map/all_to_all | solution.py:598
  55.3 12.7 %all-to-all-start.3 = ((bf16[32,8,128]{2,1,0:T(8,128)(2,1)}), bf16[32,8,128]{2,1,0:T(8,128)(2,1)S(1)}, u32[]{:S(2)}, u32[]{:S(2)}) async-start(bf16[32,8,128]{2,1,0:T(8,128)(2,1)} %bitcast.4), calls=%async_computation.3 | async-start | bytes 131072 | tf_op jit(solution)/shard_map/all_to_all | solution.py:598

commit v7 on v6

--- a/solution.py
+++ b/solution.py
@@ -147,17 +147,19 @@
 
 def conv_kernel(
     starts_far, raw_far, cot_far, taps_far, gain_far,
-    keys, values, message, raw_end, tops, taps, gain, raw, starts, sems,
+    keys, values, message, rims, taps, raw, gain, starts, sems,
 ):
     _, rows, width = raw.shape
     heads = range(width // HEAD_DIM)
     first = lax.axis_index("seq") * rows
-    taps_load = pltpu.make_async_copy(taps_far, taps, sems.at[0])
+    taps_load = pltpu.make_async_copy(taps_far, taps.at[pl.ds(0, 3)], sems.at[0])
     loads = [pltpu.make_async_copy(raw_far.at[m], raw.at[m - 1], sems.at[m]) for m in (1, 2)]
     others = [
-        pltpu.make_async_copy(raw_far.at[:, pl.ds(0, HALO)], tops.at[pl.ds(0, 3)], sems.at[3]),
-        pltpu.make_async_copy(cot_far.at[pl.ds(0, HALO)], tops.at[3], sems.at[4]),
-        pltpu.make_async_copy(raw_far.at[:, pl.ds(rows - HALO, HALO)], raw_end, sems.at[5]),
+        pltpu.make_async_copy(raw_far.at[:, pl.ds(0, HALO)], rims.at[pl.ds(0, 3)], sems.at[3]),
+        pltpu.make_async_copy(cot_far.at[pl.ds(0, HALO)], rims.at[3], sems.at[4]),
+        pltpu.make_async_copy(
+            raw_far.at[:, pl.ds(rows - HALO, HALO)], rims.at[pl.ds(4, 3)], sems.at[5]
+        ),
         pltpu.make_async_copy(gain_far, gain, sems.at[6]),
     ]
     starts_load = pltpu.make_async_copy(starts_far, starts, sems.at[7])
@@ -182,21 +184,23 @@
             out[:, at] = made[m, h]
     for load in others:
         load.wait()
+    taps[3] = jnp.broadcast_to(gain[...], (TAPS, width))
     share = HEAD_DIM // SHARE
     line = iota((SHARE, HEAD_DIM), 0)
     ends, routed = {}, []
     for h in heads:
         at = head_columns(h)
         for m in range(3):
-            low = raw_end[m, :, at].astype(f32)[HALO - SHARE :]
-            top = tops[m, :, at].astype(f32)[:SHARE]
+            low = rims[4 + m, :, at].astype(f32)[HALO - SHARE :]
+            top = rims[m, :, at].astype(f32)[:SHARE]
             ends[m, h] = pltpu.roll(jnp.where(line >= SHARE - EDGE, low, top), EDGE, 0)
     for base in (0, EDGE):
         for h in heads:
             routed += [ends[0, h][base + a : base + a + 1] for a in range(EDGE)]
     for h in heads:
-        top = tops[3, :, head_columns(h)].astype(f32)
+        top = rims[3, :, head_columns(h)].astype(f32)
         routed += [top[a : a + 1] for a in range(EDGE)]
+    parts = []
     for h in heads:
         summary = tn(jnp.where(keep, made[1, h], jnp.zeros((), bf16)), made[2, h])
         for n in range(share):
@@ -204,8 +208,10 @@
             k_ends = ends[1, h]
             if r < len(routed):
                 k_ends = jnp.where(line == ROUTE, spread(routed[r]), k_ends)
-            part = summary[n * SHARE : (n + 1) * SHARE]
-            message[r] = jnp.concatenate([part, k_ends, ends[2, h]], axis=0).astype(bf16)
+            parts += [summary[n * SHARE : (n + 1) * SHARE], k_ends, ends[2, h]]
+            if r % 2:
+                message[r // 2] = jnp.concatenate(parts, axis=0).astype(bf16)
+                parts = []
 
 
 def local_kernel(
@@ -225,7 +231,7 @@
             )
             conv = conv_docs(ext, taps.at[:, :, at], m, starts, first)
             sigma = logistic(conv)
-            slope[:, at] = silu_slope(conv, sigma)
+            slope[:, at] = silu_slope(conv, sigma).astype(bf16)
             if m == 0:
                 queries[:, at] = (conv * sigma).astype(bf16)
     for h in range(width // HEAD_DIM):
@@ -282,12 +288,13 @@
 
 
 def norm_kernel(
-    starts, queries, local, incoming, cot, gain, tops, taps, slope_q, slope_k, keys, values,
+    starts, queries, local, incoming, cot, rims, taps, slope_q, slope_k, keys, values,
     attn_out, grad_norm, back, top_qkv, top_slope,
 ):
     rows, width = local.shape
     heads = width // HEAD_DIM
     share = HEAD_DIM // SHARE
+    gain = taps.at[3, pl.ds(0, 1)]
     first = lax.axis_index("seq") * rows
     begin = row_starts(starts, first, iota((rows, HEAD_DIM), 0))
     joined = doc_start(starts, first, 0) < 0
@@ -298,7 +305,7 @@
         top = []
         for m, made in enumerate((queries, keys, values)):
             behind = jnp.where(joined, heard_ends(incoming, m, h, heads), 0.0)
-            own = pltpu.roll(tops[m, :, at].astype(f32)[:SHARE], EDGE, 0)
+            own = pltpu.roll(rims[m, :, at].astype(f32)[:SHARE], EDGE, 0)
             ext = jnp.where(line < EDGE, behind, own)
             conv = taps[m, 0:1, at] * ext
             for j in range(1, TAPS):
@@ -306,7 +313,7 @@
             conv = pltpu.roll(conv, SHARE - EDGE, 0)
             if m < 2:
                 sigma = logistic(conv)
-                old = (slope_q, slope_k)[m][:SHARE, at]
+                old = (slope_q, slope_k)[m][:HALO, at].astype(f32)[:SHARE]
                 top_slope[m, :, at] = jnp.where(line < EDGE, silu_slope(conv, sigma), old)
                 conv = conv * sigma
             fresh = to_halo(only_top(conv)).astype(bf16)
@@ -349,15 +356,13 @@
 
 
 def query_kernel(
-    starts, keys, values, top_qkv, top_slope, grad_norm, slope, incoming, raw_end, taps, gain,
-    attn_out, early, edge_qkv, edge_slope, edge_grad, sem,
+    starts, keys, values, top_qkv, top_slope, grad_norm, slope, incoming, rims, taps,
+    out_q, edge_qkv, edge_slope, edge_grad,
 ):
     rows, width = grad_norm.shape
     heads = width // HEAD_DIM
     share = HEAD_DIM // SHARE
     first = lax.axis_index("seq") * rows
-    copy = pltpu.make_async_copy(attn_out, early.at[:, 0], sem)
-    copy.start()
     carry = row_starts(starts, first, iota((rows, HEAD_DIM), 0)) < 0
     start = doc_start(starts, first, rows)
     edge_age = iota((2 * HALO, HEAD_DIM), 0, rows - HALO)
@@ -370,12 +375,12 @@
         k = patched(top_qkv[1, :, at], keys[:, at])
         v = patched(top_qkv[2, :, at], values[:, at])
         g = grad_norm[:, at]
-        slope_top = patched(top_slope[0, :, at], slope[:, at])
+        slope_top = patched(top_slope[0, :, at], slope[:, at].astype(f32))
         edges, slopes = [], []
         for m in range(3):
             after = pltpu.roll(heard_ends(incoming, m, h, heads), SHARE - EDGE, 0)
             after = to_halo(only_top(after))
-            ext = jnp.concatenate([raw_end[m, :, at].astype(f32), after], axis=0)
+            ext = jnp.concatenate([rims[4 + m, :, at].astype(f32), after], axis=0)
             conv = conv_rows(ext, taps.at[:, :, at], m, edge_age)[HALO:]
             if m < 2:
                 sigma = logistic(conv)
@@ -393,7 +398,7 @@
             return nn(scores, values) + nn(scores_e, values_e) + added
 
         attn_e = edge_sums(q_e, k, k_e, v, v_e, nn(q_e, state))
-        _, g_e = normed(attn_e, gain[:, at], to_halo(next_cot(incoming, h, heads)))
+        _, g_e = normed(attn_e, taps[3, 0:1, at], to_halo(next_cot(incoming, h, heads)))
         edge_grad[:, at] = g_e
         grad_q_e = edge_sums(g_e, v, v_e, k, k_e, nt(g_e, state)) * slopes[0]
 
@@ -406,8 +411,7 @@
         grad_q = (jnp.concatenate(parts, axis=0) + carried) * slope_top
         both = jnp.concatenate([grad_q, grad_q_e], axis=0)
         out = conv_back(both, taps.at[:, :, at], 0, starts, first, rows)
-        early[:, 1, :, at] = out.reshape((early.shape[0], early.shape[2], HEAD_DIM))
-    copy.wait()
+        out_q[:, :, at] = out.reshape(out_q.shape[:2] + (HEAD_DIM,))
 
 
 def key_kernel(
@@ -435,15 +439,32 @@
         local_v[rows:, at] = nn(scores, g_e).astype(bf16)
 
 
+def gradient_kernel(
+    starts, queries, keys, values, top_qkv, top_slope, grad_norm, slope, incoming, rims, taps,
+    out_q, edge_qkv, edge_slope, local_k, local_v, edge_grad,
+):
+    query_kernel(
+        starts, keys, values, top_qkv, top_slope, grad_norm, slope, incoming, rims, taps,
+        out_q, edge_qkv, edge_slope, edge_grad,
+    )
+    key_kernel(
+        starts, queries, keys, values, top_qkv, grad_norm, edge_qkv, edge_grad, local_k, local_v
+    )
+
+
 def last_kernel(
     starts, keys, values, top_qkv, top_slope, edge_qkv, slope, edge_slope, local_k, local_v,
-    future, taps, early, sent, sem,
+    future, taps, attn_out, out_q, sent, sems,
 ):
     total, width = local_k.shape
     rows = total - HALO
     first = lax.axis_index("seq") * rows
-    copy = pltpu.make_async_copy(early, sent.at[:, pl.ds(0, 2)], sem)
-    copy.start()
+    copies = [
+        pltpu.make_async_copy(part, sent.at[:, n], sems.at[n])
+        for n, part in enumerate((attn_out, out_q))
+    ]
+    for copy in copies:
+        copy.start()
     after = iota((total, HEAD_DIM), 0) >= doc_start(starts, first, rows)
     shape = (sent.shape[0], sent.shape[2], HEAD_DIM)
     for m in (2, 1):
@@ -457,12 +478,13 @@
             else:
                 v = patched(top_qkv[2, :, at], values[:, at])
                 v = jnp.concatenate([v, edge_qkv[2, :, at]], axis=0)
-                slopes = patched(top_slope[1, :, at], slope[:, at])
+                slopes = patched(top_slope[1, :, at], slope[:, at].astype(f32))
                 slopes = jnp.concatenate([slopes, edge_slope[:, at]], axis=0)
                 grad = (local_k[:, at].astype(f32) + jnp.where(after, nt(v, state), 0.0)) * slopes
             out = conv_back(grad, taps.at[:, :, at], m, starts, first, rows)
             sent[:, m + 1, :, at] = out.reshape(shape)
-    copy.wait()
+    for copy in copies:
+        copy.wait()
 
 
 def closed(starts, rows, i):
@@ -473,7 +495,7 @@
 
 
 def forward_kernel(rows, starts, sums, taps, out):
-    count = sums.shape[0]
+    count = 2 * sums.shape[0]
     share = HEAD_DIM // SHARE
     place = lax.axis_index("seq")
     part, head = lax.rem(place, share), lax.div(place, share)
@@ -487,7 +509,10 @@
             row = jnp.where(head == h, taps[m, j : j + 1, head_columns(h)], row)
         return row
 
-    heard = [sums[i].astype(f32) for i in range(count)]
+    heard = []
+    for i in range(count // 2):
+        pair = sums[i].astype(f32)
+        heard += [pair[: 3 * SHARE], pair[3 * SHARE :]]
     ends = {m: [block[m * SHARE : (m + 1) * SHARE] for block in heard] for m in (1, 2)}
     tops = {1: [], 2: []}
     for m in (1, 2):
@@ -582,15 +607,17 @@
 
     wide = pltpu.VMEM((rows, width), bf16)
     tall = pltpu.VMEM((rows, width), f32)
-    keys, values, message, raw_end, tops, taps, gain = flat_call(
+    keys, values, message, rims, taps = flat_call(
         conv_kernel,
         [hbm] * 4,
         [
-            wide, wide, pltpu.VMEM((devices, 3 * SHARE, hd), bf16),
-            pltpu.VMEM((3, HALO, width), bf16), pltpu.VMEM((4, HALO, width), bf16),
-            pltpu.VMEM(conv_weight.shape, f32), pltpu.VMEM((1, width), f32),
+            wide, wide, pltpu.VMEM((devices // 2, 6 * SHARE, hd), bf16),
+            pltpu.VMEM((7, HALO, width), bf16), pltpu.VMEM((4, TAPS, width), f32),
         ],
-        [pltpu.VMEM((2, rows, width), bf16), pltpu.SMEM(doc_starts.shape, jnp.int32), dma((8,))],
+        [
+            pltpu.VMEM((2, rows, width), bf16), pltpu.VMEM((1, width), f32),
+            pltpu.SMEM(doc_starts.shape, jnp.int32), dma((8,)),
+        ],
         raw, cotangent, conv_weight, norm_gain.reshape(1, width),
     )
 
@@ -605,51 +632,48 @@
         return found
 
     beside = flat_call(
-        local_kernel, [hbm] + [vmem] * 3, [wide, tall, tall, tall],
+        local_kernel, [hbm] + [vmem] * 3, [wide, wide, wide, tall],
         [pltpu.VMEM((2, rows, width), bf16), dma((2,))],
         raw, taps, keys, values,
     )
-    message, beside = lax.optimization_barrier((swap(message), beside))
+    swapped = swap(message.reshape(devices, 3 * SHARE, hd)).reshape(message.shape)
+    message, beside = lax.optimization_barrier((swapped, beside))
     queries, slope_q, slope_k, local = beside
     message = scan(forward_kernel, (devices, 2 * SHARE, hd), message, taps)
     incoming = swap(message)
     attn_out, grad_norm, back, top_qkv, top_slope = flat_call(
         norm_kernel,
-        [vmem] * 11,
+        [vmem] * 10,
         [
             pltpu.VMEM((columns, piece, width), bf16), wide,
             pltpu.VMEM((heads * hd, hd), bf16), pltpu.VMEM((3, HALO, width), bf16),
             pltpu.VMEM((2, SHARE, width), f32),
         ],
         [],
-        queries, local, incoming, cotangent, gain, tops, taps, slope_q, slope_k, keys, values,
-    )
-    early, edge_qkv, edge_slope, edge_grad = flat_call(
-        query_kernel,
-        [vmem] * 11,
+        queries, local, incoming, cotangent, rims, taps, slope_q, slope_k, keys, values,
+    )
+    out_q, edge_qkv, edge_slope, local_k, local_v = flat_call(
+        gradient_kernel,
+        [vmem] * 10,
         [
-            pltpu.VMEM((columns, 2, piece, width), bf16), pltpu.VMEM((3, HALO, width), bf16),
-            pltpu.VMEM((HALO, width), f32), pltpu.VMEM((HALO, width), bf16),
+            pltpu.VMEM((columns, piece, width), bf16), pltpu.VMEM((3, HALO, width), bf16),
+            pltpu.VMEM((HALO, width), f32), pltpu.VMEM((total, width), bf16),
+            pltpu.VMEM((total, width), bf16),
         ],
-        [dma(())],
-        keys, values, top_qkv, top_slope, grad_norm, slope_q, incoming, raw_end, taps, gain,
-        attn_out,
+        [pltpu.VMEM((HALO, width), bf16)],
+        queries, keys, values, top_qkv, top_slope, grad_norm, slope_q, incoming, rims, taps,
     )
     back = swap(back.reshape(devices, SHARE, hd))
-    back, early, edge_qkv, edge_slope, edge_grad = lax.optimization_barrier(
-        (back, early, edge_qkv, edge_slope, edge_grad)
+    back, out_q, edge_qkv, edge_slope, local_k, local_v = lax.optimization_barrier(
+        (back, out_q, edge_qkv, edge_slope, local_k, local_v)
     )
     pairs = (devices // 2, 2 * SHARE, hd)
     back = scan(backward_kernel, pairs, back.reshape(pairs))
-    local_k, local_v = flat_call(
-        key_kernel, [vmem] * 7, [pltpu.VMEM((total, width), bf16)] * 2, [],
-        queries, keys, values, top_qkv, grad_norm, edge_qkv, edge_grad,
-    )
-    future, local_k, local_v = lax.optimization_barrier((swap(back.reshape(devices, SHARE, hd)), local_k, local_v))
+    future = swap(back.reshape(devices, SHARE, hd))
     (sent,) = flat_call(
-        last_kernel, [vmem] * 12, [pltpu.VMEM((columns, 4, piece, width), bf16)], [dma(())],
+        last_kernel, [vmem] * 13, [pltpu.VMEM((columns, 4, piece, width), bf16)], [dma((2,))],
         keys, values, top_qkv, top_slope, edge_qkv, slope_k, edge_slope, local_k, local_v,
-        future.reshape(heads * hd, hd), taps, early,
+        future.reshape(heads * hd, hd), taps, attn_out, out_q,
     )
     sent = lax.all_to_all(sent, "head", 0, 0, tiled=True)
     out, grad = pl.pallas_call(

time: 115 us -> 114 us (level)
  blocking collectives: 58.2 us -> 70.9 us
  waiting for transfers between devices: 18.5 us -> 10 us
  starting transfers between devices: 18.2 us -> 14.4 us
    all_to_all x1 -> x2, blocking collectives: 14.4 us -> 27.7 us  [swap(): return lax.all_to_all(parts, 'seq', 0, 0, tiled=True)]
    all_to_all x3 -> x2, waiting for transfers between devices: 18.5 us -> 10 us  [swap(): return lax.all_to_all(parts, 'seq', 0, 0, tiled=True)]
    all_to_all x3 -> x2, starting transfers between devices: 18.2 us -> 14.4 us  [swap(): return lax.all_to_all(parts, 'seq', 0, 0, tiled=True)]
    pallas_call x8 -> x7, Pallas kernels: 17.1 us -> 16.1 us  [flat_call(): pl.pallas_call(body, in_specs=[spec] + ins, out_specs=[hbm if out.memory_...]
  transfers between devices with their start and end apart: 3 -> 2, of which waited for: 3 -> 2; matrix products, arithmetic and copies ran while one was open for 0% -> 0% of each run, Pallas kernels for 7% -> 7%
where the time goes in v7:
time: 114 us
  blocking collectives  70.9 us (62%)
  Pallas kernels  17.2 us (15%)
  starting transfers between devices  14.4 us (13%)
  waiting for transfers between devices  10 us (9%)
    all_to_all x1, blocking collectives, shards(): sent = lax.all_to_all(sent, 'head', 0, 0, tiled=True)  43.2 us
    all_to_all x2, blocking collectives, swap(): return lax.all_to_all(parts, 'seq', 0, 0, tiled=True)  27.7 us
    pallas_call x7, Pallas kernels, flat_call(): pl.pallas_call(body, in_specs=[spec] + ins, out_specs=[hbm if out.memory_...  16.1 us
    all_to_all x2, starting transfers between devices, swap(): return lax.all_to_all(parts, 'seq', 0, 0, tiled=True)  14.4 us
    all_to_all x2, waiting for transfers between devices, swap(): return lax.all_to_all(parts, 'seq', 0, 0, tiled=True)  10 us
  transfers between devices with their start and end apart: 2, of which 2 were waited for; matrix products, arithmetic and copies ran while one was open for 0% of the time, Pallas kernels for 7%

profile of v7, /device:TPU:1, one launch (start us, length us, event | category | flops | bytes accessed | tf_op | source)
XLA Modules:
  0.0 113.9 jit_solution(11502848793948591351)
XLA Ops:
  0.6 2.7 %shard_map.68 = (bf16[512,256]{1,0:T(8,128)(2,1)S(1)}, bf16[512,256]{1,0:T(8,128)(2,1)S(1)}, bf16[16,48,128]{2,1,0:T(8,128)(2,1)}, bf16[7,16,256]{2,1,0:T(8,128)(2,1)S(1)}, f32[4,4,256]{2,1,0:T(4,128)S(1)}) custom-call(s32[4]{0:T(128)} %starts.11, bf16[3,512,256]{2,1,0:T(8,128)(2,1)} %bitcast.13, bf16[512,256]{1,0:T(8,128)(2,1)} %cot.1, ...), custom_call_target="tpu_custom_call" | custom-call | tf_op jit(solution)/shard_map/pallas_call | solution.py:599
  3.3 10.5 %all-to-all-start = ((bf16[32,24,128]{2,1,0:T(8,128)(2,1)}), bf16[32,24,128]{2,1,0:T(8,128)(2,1)S(1)}, u32[]{:S(2)}, u32[]{:S(2)}) async-start(bf16[32,24,128]{2,1,0:T(8,128)(2,1)} %bitcast.2), calls=%async_computation | async-start | bytes 393216 | tf_op jit(solution)/shard_map/all_to_all | solution.py:625
  13.8 0.0 copy-start.1
  13.8 0.6 copy-done.1
  14.5 3.3 %shard_map.69 = (bf16[512,256]{1,0:T(8,128)(2,1)S(1)}, bf16[512,256]{1,0:T(8,128)(2,1)S(1)}, bf16[512,256]{1,0:T(8,128)(2,1)S(1)}, f32[512,256]{1,0:T(8,128)S(1)}) custom-call(s32[4]{0:T(128)S(1)} %copy-done.1, bf16[3,512,256]{2,1,0:T(8,128)(2,1)} %bitcast.14, f32[4,4,256]{2,1,0:T(4,128)S(1)} %get-tuple-element.37.taps, ...), custom_call_target="tpu_custom_call" | custom-call | tf_op jit(solution)/shard_map/pallas_call | solution.py:599
  17.8 5.5 %all-to-all-done = bf16[32,24,128]{2,1,0:T(8,128)(2,1)S(1)} async-done(((bf16[32,24,128]{2,1,0:T(8,128)(2,1)}), bf16[32,24,128]{2,1,0:T(8,128)(2,1)S(1)}, u32[]{:S(2)}, u32[]{:S(2)}) %all-to-all-start) | async-done | bytes 196640 | tf_op jit(solution)/shard_map/all_to_all | solution.py:625
  23.2 0.0 copy-start
  23.2 1.2 %shard_map.70 = bf16[32,16,128]{2,1,0:T(8,128)(2,1)S(1)} custom-call(s32[4]{0:T(128)S(1)} %copy-done.1, bf16[16,48,128]{2,1,0:T(8,128)(2,1)S(1)} %bitcast.9, f32[4,4,256]{2,1,0:T(4,128)S(1)} %get-tuple-element.37.taps), custom_call_target="tpu_custom_call" | custom-call | tf_op jit(solution)/shard_map/pallas_call | solution.py:599
  24.4 14.4 %all_to_all.25.incoming = bf16[32,16,128]{2,1,0:T(8,128)(2,1)S(1)} all-to-all(bf16[32,16,128]{2,1,0:T(8,128)(2,1)S(1)} %shard_map.70), channel_id=1, replica_groups=mesh['seq'=32,'head'=16] {'seq'}, dimensions={0} | all-to-all | bytes 262144 | tf_op jit(solution)/shard_map/all_to_all | solution.py:625
  38.8 0.0 copy-done
  38.8 2.5 %shard_map.71 = (bf16[16,32,256]{2,1,0:T(8,128)(2,1)S(1)}, bf16[512,256]{1,0:T(8,128)(2,1)S(1)}, bf16[256,128]{1,0:T(8,128)(2,1)}, bf16[3,16,256]{2,1,0:T(8,128)(2,1)S(1)}, f32[2,8,256]{2,1,0:T(8,128)S(1)}) custom-call(s32[4]{0:T(128)S(1)} %copy-done.1, bf16[512,256]{1,0:T(8,128)(2,1)S(1)} %get-tuple-element.42.queries, ...), custom_call_target="tpu_custom_call" | custom-call | tf_op jit(solution)/shard_map/pallas_call | solution.py:599
  41.3 3.9 %all-to-all-start.2 = ((bf16[32,8,128]{2,1,0:T(8,128)(2,1)}), bf16[32,8,128]{2,1,0:T(8,128)(2,1)S(1)}, u32[]{:S(2)}, u32[]{:S(2)}) async-start(bf16[32,8,128]{2,1,0:T(8,128)(2,1)} %bitcast.4), calls=%async_computation.2 | async-start | bytes 131072 | tf_op jit(solution)/shard_map/all_to_all | solution.py:625
  45.1 4.3 %shard_map.72 = (bf16[16,32,256]{2,1,0:T(8,128)(2,1)S(1)}, bf16[3,16,256]{2,1,0:T(8,128)(2,1)S(1)}, f32[16,256]{1,0:T(8,128)S(1)}, bf16[528,256]{1,0:T(8,128)(2,1)S(1)}, bf16[528,256]{1,0:T(8,128)(2,1)S(1)}) custom-call(s32[4]{0:T(128)S(1)} %copy-done.1, bf16[512,256]{1,0:T(8,128)(2,1)S(1)} %get-tuple-element.42.queries, ...), custom_call_target="tpu_custom_call" | custom-call | tf_op jit(solution)/shard_map/pallas_call | solution.py:599
  49.4 4.6 %all-to-all-done.2 = bf16[32,8,128]{2,1,0:T(8,128)(2,1)S(1)} async-done(((bf16[32,8,128]{2,1,0:T(8,128)(2,1)}), bf16[32,8,128]{2,1,0:T(8,128)(2,1)S(1)}, u32[]{:S(2)}, u32[]{:S(2)}) %all-to-all-start.2) | async-done | bytes 65568 | tf_op jit(solution)/shard_map/all_to_all | solution.py:625
  54.0 0.7 shard_map.73
  54.7 13.3 %all_to_all.26 = bf16[32,8,128]{2,1,0:T(8,128)(2,1)S(1)} all-to-all(bf16[32,8,128]{2,1,0:T(8,128)(2,1)S(1)} %bitcast.12), channel_id=1, replica_groups=mesh['seq'=32,'head'=16] {'seq'}, dimensions={0} | all-to-all | bytes 131072 | tf_op jit(solution)/shard_map/all_to_all | solution.py:625
  68.0 1.5 %shard_map.74 = bf16[16,4,32,256]{3,2,1,0:T(8,128)(2,1)S(1)} custom-call(s32[4]{0:T(128)S(1)} %copy-done.1, bf16[512,256]{1,0:T(8,128)(2,1)S(1)} %get-tuple-element.34.keys, bf16[512,256]{1,0:T(8,128)(2,1)S(1)} %get-tuple-element.35.values, bf16[3,16,256]{2,1,0:T(8,128)(2,1)S(1)} %get-tuple-element.48.top_qkv, f32[2,8,256]{2,1,0:T(8,128)S(1)} %get-tuple-element.49.top_slope, ...), custom_call_target="tpu_custom_call" | custom-call | tf_op jit(solution)/shard_map/pallas_call | solution.py:599
  69.6 43.2 %all_to_all.27.sent = bf16[16,4,32,256]{3,2,1,0:T(8,128)(2,1)S(1)} all-to-all(bf16[16,4,32,256]{3,2,1,0:T(8,128)(2,1)S(1)} %shard_map.74), channel_id=1, replica_groups=mesh['seq'=32,'head'=16] {'head'}, dimensions={0} | all-to-all | bytes 2097152 | tf_op jit(solution)/shard_map/all_to_all | solution.py:678
  112.8 1.1 shard_map.75
Async XLA Ops:
  3.3 19.9 %all-to-all-start = ((bf16[32,24,128]{2,1,0:T(8,128)(2,1)}), bf16[32,24,128]{2,1,0:T(8,128)(2,1)S(1)}, u32[]{:S(2)}, u32[]{:S(2)}) async-start(bf16[32,24,128]{2,1,0:T(8,128)(2,1)} %bitcast.2), calls=%async_computation | async-start | bytes 393216 | tf_op jit(solution)/shard_map/all_to_all | solution.py:625
  13.8 0.7 copy-start.1
  23.2 15.6 %copy-start = (bf16[512,256]{1,0:T(8,128)(2,1)S(1)}, bf16[512,256]{1,0:T(8,128)(2,1)}, u32[]{:S(2)}) copy-start(bf16[512,256]{1,0:T(8,128)(2,1)} %cot.1) | copy-start | bytes 786436
  41.3 12.7 %all-to-all-start.2 = ((bf16[32,8,128]{2,1,0:T(8,128)(2,1)}), bf16[32,8,128]{2,1,0:T(8,128)(2,1)S(1)}, u32[]{:S(2)}, u32[]{:S(2)}) async-start(bf16[32,8,128]{2,1,0:T(8,128)(2,1)} %bitcast.4), calls=%async_computation.2 | async-start | bytes 131072 | tf_op jit(solution)/shard_map/all_to_all | solution.py:625
